TPU v7x, 128 devices: a whole 4x4x4 slice. The times are simulated.
128 devices in a mesh: dp: 32 (over z, y, core), replica: 4 (over x).
Axes of the slice: x: 4, y: 4, z: 4, core: 2. Of those that a mesh axis runs over, the one named last changes fastest.
Arguments:
- gradients: bfloat16 [64, 1024, 1024], P(None, 'dp')
- stat_left: float32 [64, 1024, 1024], P('dp', 'replica'), may hold values from -6 to 6
- stat_right: float32 [64, 1024, 1024], P('dp', 'replica'), may hold values from -6 to 6
- inv_left: bfloat16 [32, 4, 2, 1024, 1024], P('dp', 'replica')
- inv_right: bfloat16 [32, 4, 2, 1024, 1024], P('dp', 'replica')
- owned_blocks: int32 [32, 4, 2], replicated, may hold values from 0 to 1, as said below
- owner_counts: int32 [32, 4], replicated, may hold values from 0 to 2, as said below
- block_matrix: int32 [64], replicated, may hold values from 0 to 4
Outputs:
- update: bfloat16 [64, 1024, 1024], P(None, 'dp')
- new_left: float32 [64, 1024, 1024], P('dp', 'replica')
- new_right: float32 [64, 1024, 1024], P('dp', 'replica')
Inputs may be any that keep to these rules, and one draw needn't show every extreme that they name: `owned_blocks`: at each dp index the first owner_counts entries of a replica's list name, in rising order, the local blocks that replica owns; each of the 2 local blocks has exactly one owner; entries past the count name other local blocks. `owner_counts`: the counts of a dp index sum to 2; at dp index 0 one replica owns all 2 blocks.
All inputs are finite; a program needn't handle non-finite values.
Results may differ from a plain program's by a relative error of at most 0.0058.
Values may be sent and summed in bfloat16 or wider, within the bound.
No kernel may reach another device: no remote copies, remote signals or barrier semaphores. Data moves between devices by JAX's collectives and lax.ppermute only.
A program may use at most 128 MiB of HBM per device.

v0:
```python
import jax
import jax.numpy as jnp
from jax import lax
from jax.sharding import PartitionSpec as P

NMAT = 5


STAT_DECAY = 0.95
EPSILON = 1e-06


def apply_roots(left_factor, block, right_factor):
    middle = jnp.dot(left_factor, block, preferred_element_type=jnp.float32).astype(jnp.bfloat16)
    return jnp.dot(middle, right_factor, preferred_element_type=jnp.float32).astype(jnp.bfloat16)


def skip_roots(left_factor, block, right_factor):
    return jnp.zeros(block.shape, jnp.bfloat16)


def per_device(
    gradients, stat_left, stat_right, inv_left, inv_right, owned_blocks, owner_counts, block_matrix
):
    dp_count = lax.axis_size("dp")
    owner_total = lax.axis_size("replica")
    dp_index = lax.axis_index("dp")
    owner_index = lax.axis_index("replica")
    block_total, shard_rows, order = gradients.shape
    local_total = block_total // dp_count
    slot_total = inv_left.shape[2]
    matrix_ids = jnp.arange(NMAT, dtype=jnp.int32)
    matrix_hot = (block_matrix[:, None] == matrix_ids[None, :]).astype(jnp.float32)
    squares = jnp.square(gradients.astype(jnp.float32))
    grad_sq = jnp.sum(squares, axis=(1, 2))
    grad_total = lax.psum(jnp.sum(matrix_hot * grad_sq[:, None], axis=0), "dp")
    whole_blocks = lax.all_to_all(gradients, "dp", split_axis=0, concat_axis=1, tiled=True)
    stat_rows = order // owner_total
    row_start = owner_index * stat_rows
    row_part = lax.dynamic_slice_in_dim(whole_blocks, row_start, stat_rows, 1)
    column_part = lax.dynamic_slice_in_dim(whole_blocks, row_start, stat_rows, 2)
    outer = jnp.einsum("brk,bck->brc", row_part, whole_blocks, preferred_element_type=jnp.float32)
    inner = jnp.einsum(
        "bkr,bkc->brc", column_part, whole_blocks, preferred_element_type=jnp.float32
    )
    new_left = STAT_DECAY * stat_left + (1.0 - STAT_DECAY) * outer
    new_right = STAT_DECAY * stat_right + (1.0 - STAT_DECAY) * inner
    row_owned = lax.dynamic_index_in_dim(owned_blocks, dp_index, 0, keepdims=False)
    row_counts = lax.dynamic_index_in_dim(owner_counts, dp_index, 0, keepdims=False)
    my_owned = lax.dynamic_index_in_dim(row_owned, owner_index, 0, keepdims=False)
    my_count = lax.dynamic_index_in_dim(row_counts, owner_index, 0, keepdims=False)
    left_slots = inv_left[0, 0]
    right_slots = inv_right[0, 0]
    results = []
    for slot in range(slot_total):
        block = lax.dynamic_index_in_dim(whole_blocks, my_owned[slot], 0, keepdims=False)
        results.append(
            lax.cond(
                slot < my_count, apply_roots, skip_roots, left_slots[slot], block, right_slots[slot]
            )
        )
    pre_slots = jnp.stack(results, axis=0)
    slot_ids = jnp.arange(slot_total, dtype=jnp.int32)
    slot_live = slot_ids < my_count
    global_ids = dp_index * local_total + my_owned
    slot_hot = (jnp.take(block_matrix, global_ids)[:, None] == matrix_ids[None, :]).astype(
        jnp.float32
    )
    pre_sq = jnp.sum(jnp.square(pre_slots.astype(jnp.float32)), axis=(1, 2))
    pre_part = jnp.sum(slot_hot * jnp.where(slot_live, pre_sq, 0.0)[:, None], axis=0)
    pre_total = lax.psum(pre_part, ("dp", "replica"))
    graft = jnp.sqrt(grad_total) / jnp.sqrt(pre_total + EPSILON)
    slot_scale = jnp.sum(slot_hot * graft[None, :], axis=1)
    pre_slots = (pre_slots.astype(jnp.float32) * slot_scale[:, None, None]).astype(jnp.bfloat16)
    local_ids = jnp.arange(local_total, dtype=jnp.int32)
    gathered = lax.all_gather(pre_slots, "replica", axis=0, tiled=True)
    live_table = slot_ids[None, :] < row_counts[:, None]
    match = (row_owned[:, :, None] == local_ids[None, None, :]) & live_table[:, :, None]
    codes = jnp.arange(owner_total, dtype=jnp.int32)[:, None] * slot_total + slot_ids[None, :]
    picks = jnp.sum(jnp.where(match, codes[:, :, None], 0), axis=(0, 1))
    mine = jnp.take(gathered, picks, axis=0)
    returned = lax.all_to_all(mine, "dp", split_axis=1, concat_axis=0, tiled=True)
    return (returned, new_left, new_right)


def solution(mesh):
    return jax.shard_map(
        per_device,
        mesh=mesh,
        in_specs=(
            P(None, "dp", None),
            P("dp", "replica", None),
            P("dp", "replica", None),
            P("dp", "replica", None, None, None),
            P("dp", "replica", None, None, None),
            P(),
            P(),
            P(),
        ),
        out_specs=(P(None, "dp", None), P("dp", "replica", None), P("dp", "replica", None)),
        check_vma=False,
    )
```

profile of v0, /device:TPU:0, one launch (start us, length us, event | category | flops | bytes accessed | tf_op | source)
XLA Modules:
  0.0 481.2 jit_solution(853816850467425245)
XLA Ops:
  7.2 8.7 %all-to-all-start = ((bf16[64,32,1024]{2,1,0:T(8,128)(2,1)}), bf16[64,32,1024]{2,1,0:T(8,128)(2,1)}, u32[]{:S(2)}, u32[]{:S(2)}) async-start(bf16[64,32,1024]{2,1,0:T(8,128)(2,1)} %param.12), calls=%async_computation | async-start | bytes 8388608 | tf_op jit(solution)/shard_map/all_to_all | solution.py:37
  16.1 0.6 dynamic_slice.39
  18.1 0.6 gather_fusion
  18.7 3.5 multiply_reduce_fusion
  22.3 47.0 %all-to-all-done = bf16[64,32,1024]{2,1,0:T(8,128)(2,1)} async-done(((bf16[64,32,1024]{2,1,0:T(8,128)(2,1)}), bf16[64,32,1024]{2,1,0:T(8,128)(2,1)}, u32[]{:S(2)}, u32[]{:S(2)}) %all-to-all-start) | async-done | bytes 4194336 | tf_op jit(solution)/shard_map/all_to_all | solution.py:37
  69.4 5.0 %copy.32 = bf16[32,2,32,1024]{3,2,0,1:T(8,128)(2,1)} copy(bf16[32,2,32,1024]{3,2,1,0:T(8,128)(2,1)} %bitcast.12) | data formatting | bytes 8388608 | tf_op jit(solution)/shard_map/all_to_all | solution.py:37
  74.7 1.6 conditional.3
  74.7 1.6 stack.16
  76.3 2.5 fusion.46
  78.8 0.6 compare_select_fusion.4
  79.5 73.2 %psum.14 = f32[5]{0:T(128)S(1)} all-reduce(f32[5]{0:T(128)S(1)} %select_reduce_fusion), channel_id=1, replica_groups=mesh['dp'=32,'replica'=4] {'dp'}, use_global_device_ids=true, to_apply=%region_7.8 | all-reduce | flops 5 | bytes 40 | tf_op jit(solution)/shard_map/psum | solution.py:36
  152.8 69.3 %psum.15 = f32[5]{0:T(128)S(1)} all-reduce(f32[5]{0:T(128)S(1)} %select_reduce_fusion.2), channel_id=1, replica_groups=mesh['dp'=32,'replica'=4] {'dp','replica'}, use_global_device_ids=true, to_apply=%region_10.11 | all-reduce | flops 5 | bytes 40 | tf_op jit(solution)/shard_map/psum | solution.py:71
  222.3 4.3 fusion.47
  227.1 150.6 %all-gather.2.cloned.1.call-done = bf16[8,1024,1024]{2,1,0:T(8,128)(2,1)} async-done(((bf16[2,1024,1024]{2,1,0:T(8,128)(2,1)}), bf16[8,1024,1024]{2,1,0:T(8,128)(2,1)}) %all-gather.2.cloned.1.call-update) | async-done | bytes 16777232 | tf_op jit(solution)/shard_map/all_gather | solution.py:76
  377.7 11.6 %fusion.55 = (bf16[8,512,1024]{2,1,0:T(8,128)(2,1)}, bf16[8,512,1024]{2,1,0:T(8,128)(2,1)}) fusion(bf16[8,1024,1024]{2,1,0:T(8,128)(2,1)} %all-gather.2.cloned.1.call-done), kind=kLoop, calls=%fused_computation.63 | loop fusion | bytes 33554432 | tf_op jit(solution)/shard_map/jit(_take)/gather | solution.py:81
  389.3 4.1 gather_fusion.1
  393.4 5.4 %gather_fusion.2 = bf16[2,512,1024]{2,1,0:T(8,128)(2,1)} fusion(bf16[8,512,1024]{2,1,0:T(8,128)(2,1)} %get-tuple-element.102, s32[1024]{0:T(1024)S(1)} %pad_clamp_fusion), kind=kCustom, calls=%fused_computation.2 | custom fusion | bytes 4194312 | tf_op jit(solution)/shard_map/jit(_take)/gather | solution.py:81
  398.8 2.6 maximum_select_fusion
  401.4 6.3 %copy.33 = bf16[2,1024,1024]{2,0,1:T(2,128)(2,1)} copy(bf16[2,1024,1024]{2,1,0:T(8,128)(2,1)S(1)} %maximum_select_fusion) | data formatting | bytes 8388608 | tf_op jit(solution)/shard_map/jit(_take)/select_n | solution.py:81
  407.7 7.7 %all-to-all-start.1 = ((bf16[2,1024,1024]{2,0,1:T(2,128)(2,1)}), bf16[2,1024,1024]{2,0,1:T(2,128)(2,1)}, u32[]{:S(2)}, u32[]{:S(2)}) async-start(bf16[2,1024,1024]{2,0,1:T(2,128)(2,1)} %copy.33), calls=%async_computation.1 | async-start | bytes 8388608 | tf_op jit(solution)/shard_map/all_to_all | solution.py:82
  415.5 5.5 %multiply_add_fusion = f32[2,256,1024]{2,1,0:T(8,128)} fusion(f32[2,256,1024]{2,1,0:T(8,128)S(1)} %copy-done.4, bf16[2,1024,1024]{2,1,0:T(8,128)(2,1)} %bitcast.69, s32[]{:T(128)S(6)} %select_n.101), kind=kOutput, calls=%fused_computation.32 | convolution fusion | flops 1075314688 | bytes 9437188 | tf_op jit(solution)/shard_map/bkr,bkc->brc/dot_general | solution.py:43
  420.9 2.7 multiply_add_fusion.1
  423.7 45.0 %all-to-all-done.1 = bf16[2,1024,1024]{2,0,1:T(2,128)(2,1)} async-done(((bf16[2,1024,1024]{2,0,1:T(2,128)(2,1)}), bf16[2,1024,1024]{2,0,1:T(2,128)(2,1)}, u32[]{:S(2)}, u32[]{:S(2)}) %all-to-all-start.1) | async-done | bytes 4194336 | tf_op jit(solution)/shard_map/all_to_all | solution.py:82
  468.7 5.6 %copy.34 = bf16[32,2,32,1024]{3,2,1,0:T(8,128)(2,1)} copy(bf16[32,2,32,1024]{3,1,2,0:T(2,128)(2,1)} %bitcast.21) | data formatting | bytes 8388608 | tf_op jit(solution)/shard_map/all_to_all | solution.py:82
  (37 shorter events, 1.7 us)
Async XLA Ops:
  7.2 8.8 %copy-start = (s32[32,4,2]{0,2,1:T(2,128)S(1)}, s32[32,4,2]{0,2,1:T(2,128)}, u32[]{:S(2)}) copy-start(s32[32,4,2]{0,2,1:T(2,128)} %param.17) | copy-start | bytes 3076
  7.2 9.0 %copy-start.6 = (s32[32,4]{0,1:T(4,128)S(1)}, s32[32,4]{0,1:T(4,128)}, u32[]{:S(2)}) copy-start(s32[32,4]{0,1:T(4,128)} %param.18) | copy-start | bytes 1540
  7.2 10.9 %copy-start.2 = (s32[64]{0:T(128)S(1)}, s32[64]{0:T(128)}, u32[]{:S(2)}) copy-start(s32[64]{0:T(128)} %param.19) | copy-start | bytes 772
  7.2 62.2 %all-to-all-start = ((bf16[64,32,1024]{2,1,0:T(8,128)(2,1)}), bf16[64,32,1024]{2,1,0:T(8,128)(2,1)}, u32[]{:S(2)}, u32[]{:S(2)}) async-start(bf16[64,32,1024]{2,1,0:T(8,128)(2,1)} %param.12), calls=%async_computation | async-start | bytes 8388608 | tf_op jit(solution)/shard_map/all_to_all | solution.py:37
  15.9 361.8 %all-gather.2.cloned.1.call-start = ((), (), s32[]{:S(2)}) async-start(), calls=%async_computation.2 | async-start | bytes 20971520 | tf_op jit(solution)/shard_map/all_gather | solution.py:76
  407.7 7.8 %copy-start.4 = (f32[2,256,1024]{2,1,0:T(8,128)S(1)}, f32[2,256,1024]{2,1,0:T(8,128)}, u32[]{:S(2)}) copy-start(f32[2,256,1024]{2,1,0:T(8,128)} %param.14) | copy-start | bytes 6291460
  407.7 61.0 %all-to-all-start.1 = ((bf16[2,1024,1024]{2,0,1:T(2,128)(2,1)}), bf16[2,1024,1024]{2,0,1:T(2,128)(2,1)}, u32[]{:S(2)}, u32[]{:S(2)}) async-start(bf16[2,1024,1024]{2,0,1:T(2,128)(2,1)} %copy.33), calls=%async_computation.1 | async-start | bytes 8388608 | tf_op jit(solution)/shard_map/all_to_all | solution.py:82
  415.4 5.5 %copy-start.3 = (bf16[32,2,32,1024]{3,2,0,1:T(8,128)(2,1)S(1)}, bf16[32,2,32,1024]{3,2,0,1:T(8,128)(2,1)}, u32[]{:S(2)}) copy-start(bf16[32,2,32,1024]{3,2,0,1:T(8,128)(2,1)} %copy.32) | copy-start | bytes 12582916
  415.4 5.5 %copy-start.5 = (f32[2,256,1024]{2,1,0:T(8,128)S(1)}, f32[2,256,1024]{2,1,0:T(8,128)}, u32[]{:S(2)}) copy-start(f32[2,256,1024]{2,1,0:T(8,128)} %param.13) | copy-start | bytes 6291460
  468.7 5.6 %copy-start.1 = (s32[32,4,2]{0,2,1:T(2,128)S(1)}, s32[32,4,2]{0,2,1:T(2,128)}, u32[]{:S(2)}) copy-start(s32[32,4,2]{0,2,1:T(2,128)} %param.17) | copy-start | bytes 3076
Sparse Core Ops, SparseCore 0:
  226.7 150.9 all-gather.1
where the time goes:
time: 482 us; the launch traced here: 481 us
  waiting for transfers between devices  243 us (50%)
  blocking collectives  143 us (30%)
  local copies, waits for them, and re-layouts  41.6 us (9%)
  starting transfers between devices  16.5 us (3%)
  between operations  15.5 us (3%)
  other arithmetic  14.1 us (3%)
  matrix products  8.22 us (2%)
    all_gather x1, waiting for transfers between devices, per_device(): gathered = lax.all_gather(pre_slots, 'replica', axis=0, tiled=True)  151 us
    psum x1, blocking collectives, per_device(): grad_total = lax.psum(jnp.sum(matrix_hot * grad_sq[:, None], axis=0), 'dp')  73.2 us
    psum x1, blocking collectives, per_device(): pre_total = lax.psum(pre_part, ('dp', 'replica'))  69.3 us
    all_to_all x1, waiting for transfers between devices, per_device(): lax.all_to_all(gradients, 'dp', split_axis=0, concat_axis=1, tiled=True)  47 us
    all_to_all x1, waiting for transfers between devices, per_device(): lax.all_to_all(mine, 'dp', split_axis=1, concat_axis=0, tiled=True)  45 us
    gather x3, local copies, waits for them, and re-layouts, per_device(): mine = jnp.take(gathered, picks, axis=0)  21.1 us
  transfers between devices with their start and end apart: 3, of which 3 were waited for; matrix products, arithmetic and copies ran while one was open for 3% of the time, Pallas kernels for 0%

commit v1 on v0

v1 whole, which is shorter than its diff:
```python
import jax
import jax.numpy as jnp
from jax import lax
from jax.experimental import pallas as pl
from jax.experimental.pallas import tpu as pltpu
from jax.sharding import PartitionSpec as P

NMAT = 5
STAT_DECAY = 0.95
EPSILON = 1e-06
BF16 = jnp.bfloat16
F32 = jnp.float32
VMEM_LIMIT = 48 * 1024 * 1024
OFFSETS = (2, 1, 3, 0)


def shift(x, step):
    count = lax.axis_size("replica")
    return lax.ppermute(x, "replica", [(i, (i + step) % count) for i in range(count)])


def exchange(x, axis, bit):
    count = lax.axis_size(axis)
    return lax.ppermute(x, axis, [(i, i ^ bit) for i in range(count)])


def sum_everywhere(x):
    for axis in ("replica", "dp"):
        bit = 1
        while bit < lax.axis_size(axis):
            x = x + exchange(x, axis, bit)
            bit *= 2
    return x


def roots_kernel(info, left, block, right, *refs):
    outs, total, middle = refs[:7], refs[7], refs[8]
    step = pl.program_id(0)
    tiles = pl.num_programs(0) // 2
    rows = left.shape[1]
    owned = info[1] == 1

    @pl.when(step == 0)
    def _():
        total[...] = jnp.zeros_like(total)

    @pl.when(owned & (step < tiles))
    def _():
        product = jnp.dot(left[0], block[...], preferred_element_type=F32)
        middle[pl.ds(pl.multiple_of(step * rows, rows), rows), :] = product.astype(BF16)

    def quarter(place):
        half = middle.shape[0] // 2
        pieces = []
        for top in (0, half):
            product = jnp.dot(middle[top : top + half, :], right[0], preferred_element_type=F32)
            pieces.append(product.astype(BF16))
            wide = pieces[-1].astype(F32)
            squares = jnp.sum(jnp.square(wide).reshape(half // 8, 8, wide.shape[1]), axis=0)
            total[...] += squares[:, :128] + squares[:, 128:]
        if place < 3:
            outs[2 * place][...] = pieces[0]
            outs[2 * place + 1][...] = pieces[1]
        else:
            outs[6][:half, :] = pieces[0]
            outs[6][half:, :] = pieces[1]

    for place in range(4):
        pl.when(owned & (step == tiles + place))(lambda place=place: quarter(place))


def apply_roots(info, left, block, right):
    order = block.shape[0]
    tile = order // 4
    half = order // 2

    def left_map(step, info):
        return (info[0], jnp.where(info[1] == 1, jnp.minimum(step, 3), 0), 0)

    def right_map(step, info):
        place = jnp.maximum(step - 4, 0)
        offset = jnp.where(place == 0, 2, jnp.where(place == 1, 1, jnp.where(place == 2, 3, 0)))
        return (info[0], 0, jnp.where(info[1] == 1, lax.rem(info[2] + offset, 4), 0))

    whole = lambda step, info: (0, 0)
    piece = jax.ShapeDtypeStruct((half, tile), BF16)
    return pl.pallas_call(
        roots_kernel,
        out_shape=[piece] * 6
        + [jax.ShapeDtypeStruct((order, tile), BF16), jax.ShapeDtypeStruct((8, 128), F32)],
        grid_spec=pltpu.PrefetchScalarGridSpec(
            num_scalar_prefetch=1,
            grid=(8,),
            in_specs=[
                pl.BlockSpec((1, tile, order), left_map),
                pl.BlockSpec((order, order), whole),
                pl.BlockSpec((1, order, tile), right_map),
            ],
            out_specs=[pl.BlockSpec((half, tile), whole)] * 6
            + [pl.BlockSpec((order, tile), whole), pl.BlockSpec((8, 128), whole)],
            scratch_shapes=[pltpu.VMEM((order, order), BF16)],
        ),
        compiler_params=pltpu.CompilerParams(
            dimension_semantics=("arbitrary",), vmem_limit_bytes=VMEM_LIMIT
        ),
        cost_estimate=pl.CostEstimate(
            flops=4 * order**3, bytes_accessed=8 * order * order * 2, transcendentals=0
        ),
        name="roots",
    )(info, left, block, right)


def scale_kernel(which, slots, scales, place, *refs):
    ins, out = refs[:8], refs[-1]
    part, sub = pl.program_id(0), pl.program_id(1)
    count = out.shape[0]
    width = ins[0].shape[-1]
    base = (part * pl.num_programs(1) + sub) * count

    def write(sources):
        for i in range(count):
            factor = scales[(base + i) * slots + which]
            for source, offset in sources:
                column = pl.multiple_of(lax.rem(place[0] + offset, 4) * width, width)
                values = source[i].astype(F32) * factor
                out[i, 0, :, pl.ds(column, width)] = values.astype(BF16)

    @pl.when(part == 0)
    def _():
        write([(ins[0], 0), (ins[1], 3), (ins[2], 1), (ins[3], 2)])

    @pl.when(part == 1)
    def _():
        write([(ins[4], 0), (ins[5], 3), (ins[6], 1), (ins[7], 2)])


def scale_rows(which, slots, scales, place, low, high, earlier):
    half, rows, width = low[0].shape
    per_step = 8
    subs = half // per_step
    low_map = lambda part, sub: (jnp.where(part == 0, sub, subs - 1), 0, 0)
    high_map = lambda part, sub: (jnp.where(part == 1, sub, 0), 0, 0)
    smem = pl.BlockSpec(memory_space=pltpu.SMEM)
    block = (per_step, rows, width)
    operands = [scales, place, *low, *high]
    in_specs = (
        [smem, smem] + [pl.BlockSpec(block, low_map)] * 4 + [pl.BlockSpec(block, high_map)] * 4
    )
    aliases = {}
    if earlier is not None:
        aliases = {len(operands): 0}
        operands.append(earlier)
        in_specs.append(pl.BlockSpec(memory_space=pl.ANY))
    return pl.pallas_call(
        lambda *refs: scale_kernel(which, slots, *refs),
        out_shape=jax.ShapeDtypeStruct((2 * half, slots, rows, 4 * width), BF16),
        grid=(2, subs),
        in_specs=in_specs,
        out_specs=pl.BlockSpec(
            (per_step, 1, rows, 4 * width), lambda part, sub: (part * subs + sub, which, 0, 0)
        ),
        input_output_aliases=aliases,
        compiler_params=pltpu.CompilerParams(
            dimension_semantics=("arbitrary", "arbitrary"), vmem_limit_bytes=VMEM_LIMIT
        ),
        cost_estimate=pl.CostEstimate(
            flops=2 * half * rows * 4 * width,
            bytes_accessed=2 * 2 * half * rows * 4 * width * 2,
            transcendentals=0,
        ),
        name="scale",
    )(*operands)


def scatter_quarters(pieces, own, owner, me):
    far_low, far_high, right_low, right_high, left_low, left_high = pieces
    half = far_low.shape[0]
    mine = owner == me
    via_right = shift(far_low, 1)
    via_left = shift(far_high, -1)
    got_left_high = shift(right_high, 1)
    got_right_low = shift(left_low, -1)
    got_left_low = shift(jnp.where(mine, right_low, via_right), 1)
    got_right_high = shift(jnp.where(mine, left_high, via_left), -1)
    from_right = owner == lax.rem(me + 1, 4)
    from_left = owner == lax.rem(me + 3, 4)
    low = jnp.where(mine, own[:half], jnp.where(from_right, got_right_low, got_left_low))
    high = jnp.where(mine, own[half:], jnp.where(from_left, got_left_high, got_right_high))
    return jnp.concatenate([low, high], axis=0)


def gather_quarters(quarter):
    half = quarter.shape[0] // 2
    low, high = quarter[:half], quarter[half:]
    left_low = shift(low, 1)
    right_high = shift(high, -1)
    left_high = shift(high, 1)
    right_low = shift(low, -1)
    far_low = shift(left_low, 1)
    far_high = shift(right_high, -1)
    return (low, left_low, right_low, far_low), (high, left_high, right_high, far_high)


def per_device(
    gradients, stat_left, stat_right, inv_left, inv_right, owned_blocks, owner_counts, block_matrix
):
    dp_count = lax.axis_size("dp")
    owner_total = lax.axis_size("replica")
    dp_index = lax.axis_index("dp")
    me = lax.axis_index("replica")
    block_total, shard_rows, order = gradients.shape
    local_total = block_total // dp_count
    slot_total = inv_left.shape[2]
    width = order // owner_total
    matrix_ids = jnp.arange(NMAT, dtype=jnp.int32)
    matrix_hot = (block_matrix[:, None] == matrix_ids[None, :]).astype(F32)

    by_owner = gradients.reshape(dp_count, local_total, shard_rows, order)
    blocks = []
    for b in range(local_total):
        arrived = lax.all_to_all(by_owner[:, b], "dp", split_axis=0, concat_axis=0, tiled=True)
        blocks.append(arrived.reshape(order, order))

    grad_sq = jnp.sum(jnp.square(gradients.astype(F32)), axis=(1, 2))
    grad_part = jnp.sum(matrix_hot * grad_sq[:, None], axis=0)

    row_owned = lax.dynamic_index_in_dim(owned_blocks, dp_index, 0, keepdims=False)
    row_counts = lax.dynamic_index_in_dim(owner_counts, dp_index, 0, keepdims=False)
    slot_ids = jnp.arange(slot_total, dtype=jnp.int32)
    live = slot_ids[None, :] < row_counts[:, None]
    replica_ids = jnp.arange(owner_total, dtype=jnp.int32)

    quarters, pre_part = [], jnp.zeros((NMAT,), F32)
    for b in range(local_total):
        match = (row_owned == b) & live
        owner = jnp.sum(jnp.where(match, replica_ids[:, None], 0))
        slot = jnp.sum(jnp.where(match, slot_ids[None, :], 0))
        mine = owner == me
        info = jnp.stack([slot, mine.astype(jnp.int32), me]).astype(jnp.int32)
        *pieces, own, squares = apply_roots(info, inv_left[0, 0], blocks[b], inv_right[0, 0])
        number = lax.dynamic_index_in_dim(matrix_hot, dp_index * local_total + b, 0, keepdims=False)
        pre_part = pre_part + number * jnp.sum(squares)
        mixed = scatter_quarters(pieces, own, owner, me)
        quarters.append(
            lax.all_to_all(
                mixed.reshape(dp_count, shard_rows, width), "dp", split_axis=0, concat_axis=0, tiled=True
            )
        )

    parts = jnp.stack([pre_part, jnp.where(me == 0, grad_part, 0.0)])
    pre_total, grad_total = sum_everywhere(parts)
    graft = jnp.sqrt(grad_total) / jnp.sqrt(pre_total + EPSILON)
    scales = jnp.sum(matrix_hot * graft[None, :], axis=1)

    place = me.reshape(1).astype(jnp.int32)
    update = None
    for b in range(local_total):
        low, high = gather_quarters(quarters[b])
        update = scale_rows(b, local_total, scales, place, low, high, update)
    update = update.reshape(block_total, shard_rows, order)

    start = me * width
    left_parts, right_parts = [], []
    for b in range(local_total):
        rows = lax.dynamic_slice_in_dim(blocks[b], start, width, 0)
        columns = lax.dynamic_slice_in_dim(blocks[b], start, width, 1)
        left_parts.append(jnp.einsum("rk,ck->rc", rows, blocks[b], preferred_element_type=F32))
        right_parts.append(jnp.einsum("kr,kc->rc", columns, blocks[b], preferred_element_type=F32))
    new_left = STAT_DECAY * stat_left + (1.0 - STAT_DECAY) * jnp.stack(left_parts)
    new_right = STAT_DECAY * stat_right + (1.0 - STAT_DECAY) * jnp.stack(right_parts)
    return (update, new_left, new_right)


def solution(mesh):
    return jax.shard_map(
        per_device,
        mesh=mesh,
        in_specs=(
            P(None, "dp", None),
            P("dp", "replica", None),
            P("dp", "replica", None),
            P("dp", "replica", None, None, None),
            P("dp", "replica", None, None, None),
            P(),
            P(),
            P(),
        ),
        out_specs=(P(None, "dp", None), P("dp", "replica", None), P("dp", "replica", None)),
        check_vma=False,
    )
```

time: 482 us -> 209 us (0.43)
  waiting for transfers between devices: 243 us -> 79 us
  blocking collectives: 143 us -> 0 us
  starting transfers between devices: 16.5 us -> 74.6 us
  local copies, waits for them, and re-layouts: 41.6 us -> 9.5 us
  between operations: 15.5 us -> 4.97 us
  Pallas kernels: 0 us -> 10.4 us
  other arithmetic: 14.1 us -> 23.1 us
    all_gather x1 -> x0, waiting for transfers between devices: 151 us -> none  [per_device(): gathered = lax.all_gather(pre_slots, 'replica', axis=0, tiled=True)]
    psum x2 -> x0, blocking collectives: 143 us -> none  [the longest x1 73.2 us: per_device(): grad_total = lax.psum(jnp.sum(matrix_hot * grad_sq[:, None], axis=0), 'dp')]
    ppermute x0 -> x31, starting transfers between devices: none -> 54.2 us  [the longest x24 51.5 us: shift(): lax.ppermute(x, 'replica', [(i, (i + step) % count) for i in range(count)])]
    all_to_all x2 -> x4, waiting for transfers between devices: 92 us -> 45.6 us  [the longest x2 30.1 us: per_device(): lax.all_to_all(by_owner[:, b], 'dp', split_axis=0, concat_axis=0, tiled=T...]
    ppermute x0 -> x31, waiting for transfers between devices: none -> 33.4 us  [the longest x7 17.2 us: exchange(): return lax.ppermute(x, axis, [(i, i ^ bit) for i in range(count)])]
    gather x4 -> x0, local copies, waits for them, and re-layouts: 21.7 us -> none  [the longest x3 21.1 us: per_device(): mine = jnp.take(gathered, picks, axis=0)]
    all_to_all x2 -> x0, local copies, waits for them, and re-layouts: 10.7 us -> none  [the longest x1 5.64 us: per_device(): lax.all_to_all(mine, 'dp', split_axis=1, concat_axis=0, tiled=True)]
    pallas_call x0 -> x4, Pallas kernels: none -> 10.4 us  [the longest x2 5.29 us: apply_roots(): pl.pallas_call(roots_kernel, out_shape=[piece] * 6 + [jax.ShapeDtypeStruc...]
  transfers between devices with their start and end apart: 3 -> 35, of which waited for: 3 -> 13; matrix products, arithmetic and copies ran while one was open for 3% -> 15% of each run, Pallas kernels for 0% -> 4%
where the time goes in v1:
time: 209 us; the launch traced here: 208 us
  waiting for transfers between devices  79 us (38%)
  starting transfers between devices  74.6 us (36%)
  other arithmetic  23.1 us (11%)
  Pallas kernels  10.4 us (5%)
  local copies, waits for them, and re-layouts  9.5 us (5%)
  matrix products  6.92 us (3%)
  between operations  4.97 us (2%)
    ppermute x24, starting transfers between devices, shift(): lax.ppermute(x, 'replica', [(i, (i + step) % count) for i in range(count)])  51.5 us
    all_to_all x2, waiting for transfers between devices, per_device(): lax.all_to_all(by_owner[:, b], 'dp', split_axis=0, concat_axis=0, tiled=T...  30.1 us
    ppermute x7, waiting for transfers between devices, exchange(): return lax.ppermute(x, axis, [(i, i ^ bit) for i in range(count)])  17.2 us
    ppermute x24, waiting for transfers between devices, shift(): lax.ppermute(x, 'replica', [(i, (i + step) % count) for i in range(count)])  16.2 us
    all_to_all x2, waiting for transfers between devices, per_device(): lax.all_to_all(mixed.reshape(dp_count, shard_rows, width), 'dp', split_ax...  15.5 us
    all_to_all x2, starting transfers between devices, per_device(): lax.all_to_all(by_owner[:, b], 'dp', split_axis=0, concat_axis=0, tiled=T...  12.6 us
    all_to_all x2, starting transfers between devices, per_device(): lax.all_to_all(mixed.reshape(dp_count, shard_rows, width), 'dp', split_ax...  7.78 us
    add x1, other arithmetic, per_device(): STAT_DECAY * stat_left + (1.0 - STAT_DECAY) * jnp.stack(left_parts)  6.57 us
  transfers between devices with their start and end apart: 35, of which 13 were waited for; matrix products, arithmetic and copies ran while one was open for 15% of the time, Pallas kernels for 4%

profile of v1, /device:TPU:0, one launch (start us, length us, event | category | flops | bytes accessed | tf_op | source)
XLA Modules:
  0.0 208.4 jit_solution(17400427764473876837)
XLA Ops:
  0.6 5.1 %slice_bitcast_fusion.1 = (bf16[32,32,1024]{2,1,0:T(8,128)(2,1)}, bf16[32,32,1024]{2,1,0:T(8,128)(2,1)}) fusion(bf16[32,2,32,1024]{3,2,1,0:T(8,128)(2,1)} %bitcast.43), kind=kLoop, calls=%fused_computation.2 | loop fusion | bytes 8388608 | tf_op jit(solution)/shard_map/squeeze | solution.py:221
  5.7 8.5 %all-to-all-start.1 = ((bf16[32,32,1024]{2,1,0:T(8,128)(2,1)}), bf16[32,32,1024]{2,1,0:T(8,128)(2,1)S(1)}, u32[]{:S(2)}, u32[]{:S(2)}) async-start(bf16[32,32,1024]{2,1,0:T(8,128)(2,1)} %get-tuple-element.42), calls=%async_computation.1 | async-start | bytes 4194304 | tf_op jit(solution)/shard_map/all_to_all | solution.py:221
  19.7 24.6 %all-to-all-done.1 = bf16[32,32,1024]{2,1,0:T(8,128)(2,1)S(1)} async-done(((bf16[32,32,1024]{2,1,0:T(8,128)(2,1)}), bf16[32,32,1024]{2,1,0:T(8,128)(2,1)S(1)}, u32[]{:S(2)}, u32[]{:S(2)}) %all-to-all-start.1) | async-done | bytes 2097184 | tf_op jit(solution)/shard_map/all_to_all | solution.py:221
  45.6 4.0 %all-to-all-start = ((bf16[32,32,1024]{2,1,0:T(8,128)(2,1)}), bf16[32,32,1024]{2,1,0:T(8,128)(2,1)S(1)}, u32[]{:S(2)}, u32[]{:S(2)}) async-start(bf16[32,32,1024]{2,1,0:T(8,128)(2,1)} %get-tuple-element.41), calls=%async_computation | async-start | bytes 4194304 | tf_op jit(solution)/shard_map/all_to_all | solution.py:221
  51.0 3.7 %multiply_reduce_fusion = f32[64]{0:T(128)S(1)} fusion(bf16[64,32,1024]{2,1,0:T(8,128)(2,1)} %param.8), kind=kLoop, calls=%fused_computation | loop fusion | flops 6291392 | bytes 4194560 | tf_op jit(solution)/shard_map/reduce_sum | solution.py:224
  57.5 9.8 %collective-permute-start.7 = (bf16[512,256]{1,0:T(8,128)(2,1)}, bf16[512,256]{1,0:T(8,128)(2,1)}, u32[]{:S(2)}, u32[]{:S(2)}) collective-permute-start(bf16[512,256]{1,0:T(8,128)(2,1)} %get-tuple-element.22), channel_id=1, source_target_pairs={{0,3},{1,0},{2,1},{3,2},{4,7},{5,4},{6,5},{7,6},{8,11},{9,8},{10,9... | collective-permute-start | bytes 786440 | tf_op jit(solution)/shard_map/ppermute | solution.py:19
  67.3 3.3 %collective-permute-start.11 = (bf16[512,256]{1,0:T(8,128)(2,1)}, bf16[512,256]{1,0:T(8,128)(2,1)}, u32[]{:S(2)}, u32[]{:S(2)}) collective-permute-start(bf16[512,256]{1,0:T(8,128)(2,1)} %get-tuple-element.27), channel_id=1, source_target_pairs={{0,3},{1,0},{2,1},{3,2},{4,7},{5,4},{6,5},{7,6},{8,11},{9,8},{10,9... | collective-permute-start | bytes 786440 | tf_op jit(solution)/shard_map/ppermute | solution.py:19
  74.0 5.5 %all-to-all-done = bf16[32,32,1024]{2,1,0:T(8,128)(2,1)S(1)} async-done(((bf16[32,32,1024]{2,1,0:T(8,128)(2,1)}), bf16[32,32,1024]{2,1,0:T(8,128)(2,1)S(1)}, u32[]{:S(2)}, u32[]{:S(2)}) %all-to-all-start) | async-done | bytes 2097184 | tf_op jit(solution)/shard_map/all_to_all | solution.py:221
  89.5 8.5 %collective-permute-start.23 = (bf16[512,256]{1,0:T(8,128)(2,1)}, bf16[512,256]{1,0:T(8,128)(2,1)S(1)}, u32[]{:S(2)}, u32[]{:S(2)}) collective-permute-start(bf16[512,256]{1,0:T(8,128)(2,1)} %copy-done.7), channel_id=1, source_target_pairs={{0,3},{1,0},{2,1},{3,2},{4,7},{5,4},{6,5},{7,6},{8,11},{9,8},{10,9... | collective-permute-start | bytes 786440 | tf_op jit(solution)/shard_map/ppermute | solution.py:19
  100.1 4.1 %collective-permute-done.20 = bf16[512,256]{1,0:T(8,128)(2,1)S(1)} collective-permute-done((bf16[512,256]{1,0:T(8,128)(2,1)}, bf16[512,256]{1,0:T(8,128)(2,1)S(1)}, u32[]{:S(2)}, u32[]{:S(2)}) %collective-permute-start.20) | collective-permute-done | bytes 262176 | tf_op jit(solution)/shard_map/ppermute | solution.py:19
  109.8 3.2 %collective-permute-start.24 = (bf16[512,256]{1,0:T(8,128)(2,1)}, bf16[512,256]{1,0:T(8,128)(2,1)}, u32[]{:S(2)}, u32[]{:S(2)}) collective-permute-start(bf16[512,256]{1,0:T(8,128)(2,1)} %broadcast_select_fusion), channel_id=1, source_target_pairs={{0,3},{1,0},{2,1},{3,2},{4,7},{5,4},{6,5},{7,6},{8,11},{9,8},{10,9... | collective-permute-start | bytes 786440 | tf_op jit(solution)/shard_map/ppermute | solution.py:19
  114.9 3.9 %all-to-all-start.2 = ((bf16[32,32,256]{2,1,0:T(8,128)(2,1)}), bf16[32,32,256]{2,1,0:T(8,128)(2,1)S(1)}, u32[]{:S(2)}, u32[]{:S(2)}) async-start(bf16[32,32,256]{2,1,0:T(8,128)(2,1)} %bitcast.45), calls=%async_computation.2 | async-start | bytes 1048576 | tf_op jit(solution)/shard_map/all_to_all | solution.py:245
  122.1 8.4 %all-to-all-done.2 = bf16[32,32,256]{2,1,0:T(8,128)(2,1)S(1)} async-done(((bf16[32,32,256]{2,1,0:T(8,128)(2,1)}), bf16[32,32,256]{2,1,0:T(8,128)(2,1)S(1)}, u32[]{:S(2)}, u32[]{:S(2)}) %all-to-all-start.2) | async-done | bytes 524320 | tf_op jit(solution)/shard_map/all_to_all | solution.py:245
  130.6 3.9 %all-to-all-start.3 = ((bf16[32,32,256]{2,1,0:T(8,128)(2,1)}), bf16[32,32,256]{2,1,0:T(8,128)(2,1)S(1)}, u32[]{:S(2)}, u32[]{:S(2)}) async-start(bf16[32,32,256]{2,1,0:T(8,128)(2,1)} %bitcast.15), calls=%async_computation.3 | async-start | bytes 1048576 | tf_op jit(solution)/shard_map/all_to_all | solution.py:245
  136.3 2.8 %collective-permute-start.17 = (bf16[16,32,256]{2,1,0:T(8,128)(2,1)S(1)}, bf16[16,32,256]{2,1,0:T(8,128)(2,1)S(1)}, u32[]{:S(2)}, u32[]{:S(2)}) collective-permute-start(bf16[16,32,256]{2,1,0:T(8,128)(2,1)S(1)} %get-tuple-element.47.refs_6_), channel_id=1, source_target_pairs={{0,3},{1,0},{2,1},{3,2},{4,7},{5,4},{6,5},{7,6},{8,11},{9,8},{10,9... | collective-permute-start | bytes 786440 | tf_op jit(solution)/shard_map/ppermute | solution.py:19
  139.2 7.1 %all-to-all-done.3 = bf16[32,32,256]{2,1,0:T(8,128)(2,1)S(1)} async-done(((bf16[32,32,256]{2,1,0:T(8,128)(2,1)}), bf16[32,32,256]{2,1,0:T(8,128)(2,1)S(1)}, u32[]{:S(2)}, u32[]{:S(2)}) %all-to-all-start.3) | async-done | bytes 524320 | tf_op jit(solution)/shard_map/all_to_all | solution.py:245
  146.3 2.8 %collective-permute-start.29 = (bf16[16,32,256]{2,1,0:T(8,128)(2,1)S(1)}, bf16[16,32,256]{2,1,0:T(8,128)(2,1)S(1)}, u32[]{:S(2)}, u32[]{:S(2)}) collective-permute-start(bf16[16,32,256]{2,1,0:T(8,128)(2,1)S(1)} %get-tuple-element.43.refs_6_), channel_id=1, source_target_pairs={{0,3},{1,0},{2,1},{3,2},{4,7},{5,4},{6,5},{7,6},{8,11},{9,8},{10,9... | collective-permute-start | bytes 786440 | tf_op jit(solution)/shard_map/ppermute | solution.py:19
  149.2 5.1 %collective-permute-done.1 = f32[2,5]{1,0:T(2,128)S(1)} collective-permute-done((f32[2,5]{1,0:T(2,128)S(1)}, f32[2,5]{1,0:T(2,128)S(1)}, u32[]{:S(2)}, u32[]{:S(2)}) %collective-permute-start.1) | collective-permute-done | bytes 72 | tf_op jit(solution)/shard_map/ppermute | solution.py:24
  156.0 3.0 %collective-permute-done.3 = f32[2,5]{1,0:T(2,128)S(1)} collective-permute-done((f32[2,5]{1,0:T(2,128)S(1)}, f32[2,5]{1,0:T(2,128)S(1)}, u32[]{:S(2)}, u32[]{:S(2)}) %collective-permute-start.3) | collective-permute-done | bytes 72 | tf_op jit(solution)/shard_map/ppermute | solution.py:24
  160.3 3.9 %collective-permute-done.4 = f32[2,5]{1,0:T(2,128)S(1)} collective-permute-done((f32[2,5]{1,0:T(2,128)S(1)}, f32[2,5]{1,0:T(2,128)S(1)}, u32[]{:S(2)}, u32[]{:S(2)}) %collective-permute-start.4) | collective-permute-done | bytes 72 | tf_op jit(solution)/shard_map/ppermute | solution.py:24
  164.1 3.6 %collective-permute-done.5 = f32[2,5]{1,0:T(2,128)S(1)} collective-permute-done((f32[2,5]{1,0:T(2,128)S(1)}, f32[2,5]{1,0:T(2,128)S(1)}, u32[]{:S(2)}, u32[]{:S(2)}) %collective-permute-start.5) | collective-permute-done | bytes 72 | tf_op jit(solution)/shard_map/ppermute | solution.py:24
  175.1 3.2 %collective-permute-start.30 = (bf16[16,32,256]{2,1,0:T(8,128)(2,1)S(1)}, bf16[16,32,256]{2,1,0:T(8,128)(2,1)S(1)}, u32[]{:S(2)}, u32[]{:S(2)}) collective-permute-start(bf16[16,32,256]{2,1,0:T(8,128)(2,1)S(1)} %collective-permute-done.29.refs_8_), channel_id=1, source_target_pairs={{0,3},{1,0},{2,1},{3,2},{4,7},{5,4},{6,5},{7,6},{8,11},{9,8},{10,9... | collective-permute-start | bytes 786440 | tf_op jit(solution)/shard_map/ppermute | solution.py:19
  178.3 6.6 %fusion = (f32[2,256,1024]{2,1,0:T(8,128)}, f32[2,256,1024]{2,1,0:T(8,128)}) fusion(f32[1,256,1024]{2,1,0:T(8,128)} %convolution_bitcast_fusion.2, f32[1,256,1024]{2,1,0:T(8,128)} %convolution_bitcast_fusion.3, f32[2,256,1024]{2,1,0:T(8,128)} %param.9, f32[1,256,1024]{2,1,0:T(8,128)} %convolution_bitcast_fusion, f32[1,256,1024]{2,1,0:T(8,128)S(1)} %copy-done.9, ...), kind=kLoop, calls=%fused_computation.4 | loop fusion | flops 4194304 | bytes 12582912 | tf_op jit(solution)/shard_map/add | solution.py:269
  193.1 10.2 %collective-permute-done.27.refs_5_ = bf16[16,32,256]{2,1,0:T(8,128)(2,1)S(1)} collective-permute-done((bf16[16,32,256]{2,1,0:T(8,128)(2,1)S(1)}, bf16[16,32,256]{2,1,0:T(8,128)(2,1)S(1)}, u32[]{:S(2)}, u32[]{:S(2)}) %collective-permute-start.27) | collective-permute-done | bytes 262176 | tf_op jit(solution)/shard_map/ppermute | solution.py:19
  (113 shorter events, 58.8 us)
Async XLA Ops:
  5.7 38.5 %all-to-all-start.1 = ((bf16[32,32,1024]{2,1,0:T(8,128)(2,1)}), bf16[32,32,1024]{2,1,0:T(8,128)(2,1)S(1)}, u32[]{:S(2)}, u32[]{:S(2)}) async-start(bf16[32,32,1024]{2,1,0:T(8,128)(2,1)} %get-tuple-element.42), calls=%async_computation.1 | async-start | bytes 4194304 | tf_op jit(solution)/shard_map/all_to_all | solution.py:221
  45.6 34.0 %all-to-all-start = ((bf16[32,32,1024]{2,1,0:T(8,128)(2,1)}), bf16[32,32,1024]{2,1,0:T(8,128)(2,1)S(1)}, u32[]{:S(2)}, u32[]{:S(2)}) async-start(bf16[32,32,1024]{2,1,0:T(8,128)(2,1)} %get-tuple-element.41), calls=%async_computation | async-start | bytes 4194304 | tf_op jit(solution)/shard_map/all_to_all | solution.py:221
  57.5 51.1 %collective-permute-start.7 = (bf16[512,256]{1,0:T(8,128)(2,1)}, bf16[512,256]{1,0:T(8,128)(2,1)}, u32[]{:S(2)}, u32[]{:S(2)}) collective-permute-start(bf16[512,256]{1,0:T(8,128)(2,1)} %get-tuple-element.22), channel_id=1, source_target_pairs={{0,3},{1,0},{2,1},{3,2},{4,7},{5,4},{6,5},{7,6},{8,11},{9,8},{10,9... | collective-permute-start | bytes 786440 | tf_op jit(solution)/shard_map/ppermute | solution.py:19
  67.3 22.2 %collective-permute-start.8 = (bf16[512,256]{1,0:T(8,128)(2,1)}, bf16[512,256]{1,0:T(8,128)(2,1)}, u32[]{:S(2)}, u32[]{:S(2)}) collective-permute-start(bf16[512,256]{1,0:T(8,128)(2,1)} %get-tuple-element.24), channel_id=1, source_target_pairs={{0,1},{1,2},{2,3},{3,0},{4,5},{5,6},{6,7},{7,4},{8,9},{9,10},{10,1... | collective-permute-start | bytes 786440 | tf_op jit(solution)/shard_map/ppermute | solution.py:19
  67.3 42.4 %collective-permute-start.10 = (bf16[512,256]{1,0:T(8,128)(2,1)}, bf16[512,256]{1,0:T(8,128)(2,1)}, u32[]{:S(2)}, u32[]{:S(2)}) collective-permute-start(bf16[512,256]{1,0:T(8,128)(2,1)} %get-tuple-element.25), channel_id=1, source_target_pairs={{0,1},{1,2},{2,3},{3,0},{4,5},{5,6},{6,7},{7,4},{8,9},{9,10},{10,1... | collective-permute-start | bytes 786440 | tf_op jit(solution)/shard_map/ppermute | solution.py:19
  67.3 31.7 %collective-permute-start.11 = (bf16[512,256]{1,0:T(8,128)(2,1)}, bf16[512,256]{1,0:T(8,128)(2,1)}, u32[]{:S(2)}, u32[]{:S(2)}) collective-permute-start(bf16[512,256]{1,0:T(8,128)(2,1)} %get-tuple-element.27), channel_id=1, source_target_pairs={{0,3},{1,0},{2,1},{3,2},{4,7},{5,4},{6,5},{7,6},{8,11},{9,8},{10,9... | collective-permute-start | bytes 786440 | tf_op jit(solution)/shard_map/ppermute | solution.py:19
  88.0 16.2 %collective-permute-start.20 = (bf16[512,256]{1,0:T(8,128)(2,1)}, bf16[512,256]{1,0:T(8,128)(2,1)S(1)}, u32[]{:S(2)}, u32[]{:S(2)}) collective-permute-start(bf16[512,256]{1,0:T(8,128)(2,1)} %copy-done.8), channel_id=1, source_target_pairs={{0,1},{1,2},{2,3},{3,0},{4,5},{5,6},{6,7},{7,4},{8,9},{9,10},{10,1... | collective-permute-start | bytes 786440 | tf_op jit(solution)/shard_map/ppermute | solution.py:19
  89.5 17.5 %collective-permute-start.23 = (bf16[512,256]{1,0:T(8,128)(2,1)}, bf16[512,256]{1,0:T(8,128)(2,1)S(1)}, u32[]{:S(2)}, u32[]{:S(2)}) collective-permute-start(bf16[512,256]{1,0:T(8,128)(2,1)} %copy-done.7), channel_id=1, source_target_pairs={{0,3},{1,0},{2,1},{3,2},{4,7},{5,4},{6,5},{7,6},{8,11},{9,8},{10,9... | collective-permute-start | bytes 786440 | tf_op jit(solution)/shard_map/ppermute | solution.py:19
  107.0 13.1 %collective-permute-start.19 = (bf16[512,256]{1,0:T(8,128)(2,1)}, bf16[512,256]{1,0:T(8,128)(2,1)S(1)}, u32[]{:S(2)}, u32[]{:S(2)}) collective-permute-start(bf16[512,256]{1,0:T(8,128)(2,1)} %get-tuple-element.29), channel_id=1, source_target_pairs={{0,3},{1,0},{2,1},{3,2},{4,7},{5,4},{6,5},{7,6},{8,11},{9,8},{10,9... | collective-permute-start | bytes 786440 | tf_op jit(solution)/shard_map/ppermute | solution.py:19
  108.7 11.4 %collective-permute-start.22 = (bf16[512,256]{1,0:T(8,128)(2,1)}, bf16[512,256]{1,0:T(8,128)(2,1)}, u32[]{:S(2)}, u32[]{:S(2)}) collective-permute-start(bf16[512,256]{1,0:T(8,128)(2,1)} %get-tuple-element.32), channel_id=1, source_target_pairs={{0,1},{1,2},{2,3},{3,0},{4,5},{5,6},{6,7},{7,4},{8,9},{9,10},{10,1... | collective-permute-start | bytes 786440 | tf_op jit(solution)/shard_map/ppermute | solution.py:19
  114.9 15.7 %all-to-all-start.2 = ((bf16[32,32,256]{2,1,0:T(8,128)(2,1)}), bf16[32,32,256]{2,1,0:T(8,128)(2,1)S(1)}, u32[]{:S(2)}, u32[]{:S(2)}) async-start(bf16[32,32,256]{2,1,0:T(8,128)(2,1)} %bitcast.45), calls=%async_computation.2 | async-start | bytes 1048576 | tf_op jit(solution)/shard_map/all_to_all | solution.py:245
  130.6 15.7 %all-to-all-start.3 = ((bf16[32,32,256]{2,1,0:T(8,128)(2,1)}), bf16[32,32,256]{2,1,0:T(8,128)(2,1)S(1)}, u32[]{:S(2)}, u32[]{:S(2)}) async-start(bf16[32,32,256]{2,1,0:T(8,128)(2,1)} %bitcast.15), calls=%async_computation.3 | async-start | bytes 1048576 | tf_op jit(solution)/shard_map/all_to_all | solution.py:245
  134.5 14.6 %collective-permute-start = (f32[2,5]{1,0:T(2,128)S(1)}, f32[2,5]{1,0:T(2,128)S(1)}, u32[]{:S(2)}, u32[]{:S(2)}) collective-permute-start(f32[2,5]{1,0:T(2,128)S(1)} %pad_maximum_fusion.2), channel_id=1, source_target_pairs={{0,1},{1,0},{2,3},{3,2},{4,5},{5,4},{6,7},{7,6},{8,9},{9,8},{10,11... | collective-permute-start | bytes 128 | tf_op jit(solution)/shard_map/ppermute | solution.py:24
  136.3 38.7 %collective-permute-start.17 = (bf16[16,32,256]{2,1,0:T(8,128)(2,1)S(1)}, bf16[16,32,256]{2,1,0:T(8,128)(2,1)S(1)}, u32[]{:S(2)}, u32[]{:S(2)}) collective-permute-start(bf16[16,32,256]{2,1,0:T(8,128)(2,1)S(1)} %get-tuple-element.47.refs_6_), channel_id=1, source_target_pairs={{0,3},{1,0},{2,1},{3,2},{4,7},{5,4},{6,5},{7,6},{8,11},{9,8},{10,9... | collective-permute-start | bytes 786440 | tf_op jit(solution)/shard_map/ppermute | solution.py:19
  146.3 28.8 %collective-permute-start.29 = (bf16[16,32,256]{2,1,0:T(8,128)(2,1)S(1)}, bf16[16,32,256]{2,1,0:T(8,128)(2,1)S(1)}, u32[]{:S(2)}, u32[]{:S(2)}) collective-permute-start(bf16[16,32,256]{2,1,0:T(8,128)(2,1)S(1)} %get-tuple-element.43.refs_6_), channel_id=1, source_target_pairs={{0,3},{1,0},{2,1},{3,2},{4,7},{5,4},{6,5},{7,6},{8,11},{9,8},{10,9... | collective-permute-start | bytes 786440 | tf_op jit(solution)/shard_map/ppermute | solution.py:19
  168.4 20.4 %collective-permute-start.28 = (bf16[16,32,256]{2,1,0:T(8,128)(2,1)S(1)}, bf16[16,32,256]{2,1,0:T(8,128)(2,1)S(1)}, u32[]{:S(2)}, u32[]{:S(2)}) collective-permute-start(bf16[16,32,256]{2,1,0:T(8,128)(2,1)S(1)} %get-tuple-element.43.refs_6_), channel_id=1, source_target_pairs={{0,1},{1,2},{2,3},{3,0},{4,5},{5,6},{6,7},{7,4},{8,9},{9,10},{10,1... | collective-permute-start | bytes 786440 | tf_op jit(solution)/shard_map/ppermute | solution.py:19
  171.1 18.8 %collective-permute-start.26 = (bf16[16,32,256]{2,1,0:T(8,128)(2,1)S(1)}, bf16[16,32,256]{2,1,0:T(8,128)(2,1)S(1)}, u32[]{:S(2)}, u32[]{:S(2)}) collective-permute-start(bf16[16,32,256]{2,1,0:T(8,128)(2,1)S(1)} %get-tuple-element.44.refs_2_), channel_id=1, source_target_pairs={{0,3},{1,0},{2,1},{3,2},{4,7},{5,4},{6,5},{7,6},{8,11},{9,8},{10,9... | collective-permute-start | bytes 786440 | tf_op jit(solution)/shard_map/ppermute | solution.py:19
  172.8 19.2 %collective-permute-start.25 = (bf16[16,32,256]{2,1,0:T(8,128)(2,1)S(1)}, bf16[16,32,256]{2,1,0:T(8,128)(2,1)S(1)}, u32[]{:S(2)}, u32[]{:S(2)}) collective-permute-start(bf16[16,32,256]{2,1,0:T(8,128)(2,1)S(1)} %get-tuple-element.44.refs_2_), channel_id=1, source_target_pairs={{0,1},{1,2},{2,3},{3,0},{4,5},{5,6},{6,7},{7,4},{8,9},{9,10},{10,1... | collective-permute-start | bytes 786440 | tf_op jit(solution)/shard_map/ppermute | solution.py:19
  175.0 11.7 %collective-permute-start.13 = (bf16[16,32,256]{2,1,0:T(8,128)(2,1)S(1)}, bf16[16,32,256]{2,1,0:T(8,128)(2,1)S(1)}, u32[]{:S(2)}, u32[]{:S(2)}) collective-permute-start(bf16[16,32,256]{2,1,0:T(8,128)(2,1)S(1)} %get-tuple-element.48.refs_2_), channel_id=1, source_target_pairs={{0,1},{1,2},{2,3},{3,0},{4,5},{5,6},{6,7},{7,4},{8,9},{9,10},{10,1... | collective-permute-start | bytes 786440 | tf_op jit(solution)/shard_map/ppermute | solution.py:19
  175.1 16.9 %collective-permute-start.30 = (bf16[16,32,256]{2,1,0:T(8,128)(2,1)S(1)}, bf16[16,32,256]{2,1,0:T(8,128)(2,1)S(1)}, u32[]{:S(2)}, u32[]{:S(2)}) collective-permute-start(bf16[16,32,256]{2,1,0:T(8,128)(2,1)S(1)} %collective-permute-done.29.refs_8_), channel_id=1, source_target_pairs={{0,3},{1,0},{2,1},{3,2},{4,7},{5,4},{6,5},{7,6},{8,11},{9,8},{10,9... | collective-permute-start | bytes 786440 | tf_op jit(solution)/shard_map/ppermute | solution.py:19
  186.7 19.1 %collective-permute-start.16 = (bf16[16,32,256]{2,1,0:T(8,128)(2,1)S(1)}, bf16[16,32,256]{2,1,0:T(8,128)(2,1)S(1)}, u32[]{:S(2)}, u32[]{:S(2)}) collective-permute-start(bf16[16,32,256]{2,1,0:T(8,128)(2,1)S(1)} %get-tuple-element.47.refs_6_), channel_id=1, source_target_pairs={{0,1},{1,2},{2,3},{3,0},{4,5},{5,6},{6,7},{7,4},{8,9},{9,10},{10,1... | collective-permute-start | bytes 786440 | tf_op jit(solution)/shard_map/ppermute | solution.py:19
  188.8 16.9 %collective-permute-start.14 = (bf16[16,32,256]{2,1,0:T(8,128)(2,1)S(1)}, bf16[16,32,256]{2,1,0:T(8,128)(2,1)S(1)}, u32[]{:S(2)}, u32[]{:S(2)}) collective-permute-start(bf16[16,32,256]{2,1,0:T(8,128)(2,1)S(1)} %get-tuple-element.48.refs_2_), channel_id=1, source_target_pairs={{0,3},{1,0},{2,1},{3,2},{4,7},{5,4},{6,5},{7,6},{8,11},{9,8},{10,9... | collective-permute-start | bytes 786440 | tf_op jit(solution)/shard_map/ppermute | solution.py:19
  189.9 15.8 %collective-permute-start.18 = (bf16[16,32,256]{2,1,0:T(8,128)(2,1)S(1)}, bf16[16,32,256]{2,1,0:T(8,128)(2,1)S(1)}, u32[]{:S(2)}, u32[]{:S(2)}) collective-permute-start(bf16[16,32,256]{2,1,0:T(8,128)(2,1)S(1)} %collective-permute-done.17.refs_8_), channel_id=1, source_target_pairs={{0,3},{1,0},{2,1},{3,2},{4,7},{5,4},{6,5},{7,6},{8,11},{9,8},{10,9... | collective-permute-start | bytes 786440 | tf_op jit(solution)/shard_map/ppermute | solution.py:19
  192.0 13.8 %collective-permute-start.15 = (bf16[16,32,256]{2,1,0:T(8,128)(2,1)S(1)}, bf16[16,32,256]{2,1,0:T(8,128)(2,1)S(1)}, u32[]{:S(2)}, u32[]{:S(2)}) collective-permute-start(bf16[16,32,256]{2,1,0:T(8,128)(2,1)S(1)} %collective-permute-done.13.refs_3_), channel_id=1, source_target_pairs={{0,1},{1,2},{2,3},{3,0},{4,5},{5,6},{6,7},{7,4},{8,9},{9,10},{10,1... | collective-permute-start | bytes 786440 | tf_op jit(solution)/shard_map/ppermute | solution.py:19
  (23 other events, 185.9 us)

commit v2 on v0

v2 whole, which is shorter than its diff:
```python
import jax
import jax.numpy as jnp
from jax import lax
from jax.experimental import pallas as pl
from jax.experimental.pallas import tpu as pltpu
from jax.sharding import PartitionSpec as P

NMAT = 5
ORDER = ""
FRONT = "QD"
COSTS = (16, 24, 48, 8)
MERGED = False
STAT_DECAY = 0.95
EPSILON = 1e-06
BF16 = jnp.bfloat16
F32 = jnp.float32
VMEM_LIMIT = 60 * 1024 * 1024
EXTRA = 16
SUM_SCALE = 1.0 / 16.0


def params(steps=1):
    semantics = ("arbitrary",) * steps if steps else None
    return pltpu.CompilerParams(dimension_semantics=semantics, vmem_limit_bytes=VMEM_LIMIT)


def cost(flops, size):
    return pl.CostEstimate(flops=flops, bytes_accessed=size, transcendentals=0)


def shift(x, step):
    count = lax.axis_size("replica")
    return lax.ppermute(x, "replica", [(i, (i + step) % count) for i in range(count)])


def over_dp(x):
    return lax.all_to_all(x, "dp", split_axis=0, concat_axis=0, tiled=True)


def anywhere(count):
    return [pl.BlockSpec(memory_space=pl.ANY)] * count


SMEM = pl.BlockSpec(memory_space=pltpu.SMEM)


def pick_kernel(b, source, out, held, come, go):
    parts = come.shape[0]
    size = held.shape[0] // parts
    spans = [pl.ds(i * size, size) for i in range(parts)]
    reads = [
        pltpu.make_async_copy(source.at[span, b], held.at[span], come.at[i])
        for i, span in enumerate(spans)
    ]
    writes = [
        pltpu.make_async_copy(held.at[span], out.at[span], go.at[i]) for i, span in enumerate(spans)
    ]
    for read in reads:
        read.start()
    for read, write in zip(reads, writes):
        read.wait()
        write.start()
    for write in writes:
        write.wait()


def pick_block(by_owner, b, parts=8):
    count, _, rows, order = by_owner.shape
    return pl.pallas_call(
        lambda *refs: pick_kernel(b, *refs),
        out_shape=jax.ShapeDtypeStruct((count, rows, order), BF16),
        in_specs=anywhere(1),
        out_specs=anywhere(1)[0],
        scratch_shapes=[
            pltpu.VMEM((count, rows, order), BF16),
            pltpu.SemaphoreType.DMA((parts,)),
            pltpu.SemaphoreType.DMA((parts,)),
        ],
        compiler_params=params(0),
        cost_estimate=cost(0, COSTS[3] * count * rows * order),
        name="pick",
    )(by_owner)


def piece_places(me, pieces):
    count, _, width = pieces[0].shape
    for i, piece in enumerate(pieces):
        column = lax.rem(me + (0, 3, 1, 2, 2)[i], 4) * width
        first = count // 2 if i == 4 else 0
        yield piece, pl.ds(first, piece.shape[0]), pl.ds(pl.multiple_of(column, width), width)


def block_copies(me, which, pieces, block, sems):
    if len(pieces) == 1:
        source = pieces[0] if len(pieces[0].shape) == 3 else pieces[0].at[:, which]
        return [pltpu.make_async_copy(source, block, sems.at[0])]
    return [
        pltpu.make_async_copy(piece, block.at[chunks, :, columns], sems.at[i])
        for i, (piece, chunks, columns) in enumerate(piece_places(me, pieces))
    ]


def sum_squares(x):
    wide = x.astype(F32)
    return jnp.sum(jnp.square(wide).reshape(-1, 8, wide.shape[-1]), axis=0)


def split_sum(total, first, rows, shape):
    value = jnp.full(shape, jnp.sum(total) * SUM_SCALE, F32)
    out = jnp.zeros(shape, F32)
    for part in range(3):
        rounded = value.astype(BF16).astype(F32)
        out = jnp.where(rows == first + part, rounded, out)
        value = jnp.where(value == rounded, 0.0, value - rounded)
    return out


def roots_kernel(parts, last, info, left, right, *refs):
    pieces, refs = refs[:parts], refs[parts:]
    if last:
        before, refs = refs[0], refs[1:]
    outs, (block, left_held, right_held, middle, pre_sum, grad_sum, sems) = refs[:-7], refs[-7:]
    to_right, to_left, keep_right, keep_left, own = outs[:5]
    slot, owned, me = info[0], info[1] == 1, info[2]
    order = middle.shape[0]
    wide = order // 2
    width = order // 4
    pre_sum[...] = jnp.zeros_like(pre_sum)
    grad_sum[...] = jnp.zeros_like(grad_sum)

    @pl.when(owned)
    def _():
        first = block_copies(me, 1 if last else 0, pieces, block, sems)
        first.append(pltpu.make_async_copy(left.at[slot], left_held, sems.at[8]))
        second = []
        for place, offset in enumerate((2, 1, 3, 0)):
            column = pl.multiple_of(lax.rem(me + offset, 4) * width, width)
            source = right.at[slot, :, pl.ds(column, width)]
            target = right_held.at[:, pl.ds(place * width, width)]
            second.append(pltpu.make_async_copy(source, target, sems.at[9 + place]))
        for copy in first + second:
            copy.start()
        for copy in first:
            copy.wait()

        @pl.loop(0, 2)
        def _(i):
            columns = pl.ds(pl.multiple_of(i * wide, wide), wide)
            values = block[:, :, columns].reshape(order, wide)
            product = jnp.dot(left_held[...], values, preferred_element_type=F32)
            middle[:, columns] = product.astype(BF16)
            grad_sum[...] += sum_squares(values)

        for copy in second:
            copy.wait()
        for i in range(2):
            columns = slice(i * wide, (i + 1) * wide)
            product = jnp.dot(middle[...], right_held[:, columns], preferred_element_type=F32)
            product = product.astype(BF16)
            pre_sum[...] += sum_squares(product)
            chunks = product.reshape(block.shape[0], block.shape[1], wide)
            near, far = chunks[:, :, :width], chunks[:, :, width:]
            half = block.shape[0] // 2
            if i == 0:
                to_right[half : 2 * half] = near[:half]
                to_left[half : 2 * half] = near[half:]
                keep_right[:half] = far[:half]
                to_right[:half] = far[half:]
            else:
                to_left[:half] = near[:half]
                keep_left[:half] = near[half:]
                own[: 2 * half] = far

    shape = (block.shape[1], width)
    at = lax.broadcasted_iota(jnp.int32, shape, 0)
    extra = split_sum(pre_sum[...], 0, at, shape) + split_sum(grad_sum[...], 3, at, shape)
    if last:
        lane = lax.broadcasted_iota(jnp.int32, shape, 1)
        extra = jnp.where(lane < width // 2, before[...].astype(F32), extra).astype(BF16)
        for out in outs:
            out[out.shape[0] - 1] = extra
    else:
        outs[5][...] = extra.astype(BF16)


def apply_roots(info, left, pieces, right, before=None):
    order = left.shape[-1]
    width = order // 4
    rows = pieces[0].shape[-2]
    count = order // rows
    more = 0 if before is None else 1
    sizes = (count, count, count // 2, count // 2, count)
    shapes = [(size + more, rows, width) for size in sizes] + [(rows, width)] * (1 - more)
    operands = [info, left, right, *pieces]
    in_specs = [SMEM] + anywhere(len(operands) - 1)
    if before is not None:
        operands.append(before)
        in_specs.append(pl.BlockSpec(before.shape, lambda: (0, 0)))
    square = pltpu.VMEM((order, order), BF16)
    zeros = {2: lambda: (0, 0), 3: lambda: (0, 0, 0)}
    return pl.pallas_call(
        lambda *refs: roots_kernel(len(pieces), before is not None, *refs),
        out_shape=[jax.ShapeDtypeStruct(shape, BF16) for shape in shapes],
        in_specs=in_specs,
        out_specs=[pl.BlockSpec(shape, zeros[len(shape)]) for shape in shapes],
        scratch_shapes=[
            pltpu.VMEM((count, rows, order), BF16),
            square,
            square,
            square,
            pltpu.VMEM((8, order // 2), F32),
            pltpu.VMEM((8, order // 2), F32),
            pltpu.SemaphoreType.DMA((13,)),
        ],
        compiler_params=params(0),
        cost_estimate=cost(COSTS[0] * order**3, 10 * order * order),
        name="roots",
    )(*operands)


def stats_kernel(which, parts, info, *refs):
    pieces, (stat_left, stat_right), refs = refs[:parts], refs[parts : parts + 2], refs[parts + 2 :]
    new_left, new_right, block, turned, sems = refs[-5:]
    step = pl.program_id(0)
    width, order = turned.shape
    wide = new_left.shape[-1]
    rows = block.shape[1]
    start = pl.multiple_of(info[2] * width, width)
    span = width // rows

    @pl.when(step == 0)
    def _():
        copies = block_copies(info[2], which, pieces, block, sems)
        for copy in copies:
            copy.start()
        for copy in copies:
            copy.wait()
        turned[...] = block[:, :, pl.ds(start, width)].reshape(order, width).T

    mine = block[pl.ds(info[2] * span, span)].reshape(width, order)
    chunks = pl.ds(step * (wide // rows), wide // rows)
    others = block[chunks].reshape(wide, order)
    outer = lax.dot_general(mine, others, (((1,), (1,)), ((), ())), preferred_element_type=F32)
    new_left[0] = STAT_DECAY * stat_left[0] + (1.0 - STAT_DECAY) * outer
    columns = block[:, :, pl.ds(pl.multiple_of(step * wide, wide), wide)].reshape(order, wide)
    inner = jnp.dot(turned[...], columns, preferred_element_type=F32)
    new_right[0] = STAT_DECAY * stat_right[0] + (1.0 - STAT_DECAY) * inner


def update_stats(b, info, pieces, stat_left, stat_right, earlier, steps=2):
    _, rows, order = stat_left.shape
    spec = pl.BlockSpec((1, rows, order // steps), lambda step: (b, 0, step))
    operands = [info, *pieces, stat_left, stat_right]
    in_specs = [SMEM] + anywhere(len(pieces)) + [spec, spec]
    aliases = {}
    if earlier is not None:
        aliases = {len(operands): 0, len(operands) + 1: 1}
        operands += earlier
        in_specs += anywhere(2)
    chunk_rows = pieces[0].shape[-2]
    return pl.pallas_call(
        lambda *refs: stats_kernel(b, len(pieces), *refs),
        out_shape=[jax.ShapeDtypeStruct(stat_left.shape, F32)] * 2,
        grid=(steps,),
        in_specs=in_specs,
        out_specs=[spec, spec],
        scratch_shapes=[
            pltpu.VMEM((order // chunk_rows, chunk_rows, order), BF16),
            pltpu.VMEM((rows, order), BF16),
            pltpu.SemaphoreType.DMA((8,)),
        ],
        input_output_aliases=aliases,
        compiler_params=params(),
        cost_estimate=cost(COSTS[1] * rows * order**2, 2 * order * order + 16 * rows * order),
        name="stats",
    )(*operands)


def scale_kernel(which, slots, scales, place, *refs):
    pieces = refs[:5]
    out, held, ready, come, go = refs[-5:]
    half = pieces[4].shape[0]
    reads = []
    for part in range(2):
        for at in range(4):
            i = 4 * part + at
            source = pieces[3 + part] if at == 3 else pieces[at].at[pl.ds(part * half, half)]
            reads.append(pltpu.make_async_copy(source, held.at[i], come.at[i]))
    for read in reads:
        read.start()
    writes = []
    for part in range(2):
        for read in reads[4 * part : 4 * part + 4]:
            read.wait()
        for i in range(half):
            factor = scales[(part * half + i) * slots + which]
            for at, (_, _, columns) in enumerate(piece_places(place[0], pieces[:4])):
                values = held[4 * part + at, i].astype(F32) * factor
                ready[part * half + i, :, columns] = values.astype(BF16)
        span = pl.ds(part * half, half)
        writes.append(pltpu.make_async_copy(ready.at[span], out.at[span, which], go.at[part]))
        writes[-1].start()
    for write in writes:
        write.wait()


def scale_rows(which, slots, scales, place, pieces, earlier):
    count, rows, width = pieces[0].shape
    operands = [scales, place, *pieces] + ([] if earlier is None else [earlier])
    return pl.pallas_call(
        lambda *refs: scale_kernel(which, slots, *refs),
        out_shape=jax.ShapeDtypeStruct((count, slots, rows, 4 * width), BF16),
        in_specs=[SMEM, SMEM] + anywhere(len(operands) - 2),
        out_specs=anywhere(1)[0],
        scratch_shapes=[
            pltpu.VMEM((8, count // 2, rows, width), BF16),
            pltpu.VMEM((count, rows, 4 * width), BF16),
            pltpu.SemaphoreType.DMA((8,)),
            pltpu.SemaphoreType.DMA((2,)),
        ],
        input_output_aliases={} if earlier is None else {len(operands) - 1: 0},
        compiler_params=params(0),
        cost_estimate=cost(0, COSTS[2] * count * rows * width),
        name="scale",
    )(*operands)


def scale_both_kernel(scales, place, *refs):
    pieces = refs[:5]
    out, held, ready, come, go = refs[-5:]
    parts, _, size, _, width = held.shape
    slots = out.shape[1]
    rows = out.shape[2]
    reads = []
    for part in range(parts):
        for at in range(4):
            if at < 3:
                source = pieces[at].at[pl.ds(part * size, size)]
            else:
                source = pieces[3 + part // (parts // 2)].at[pl.ds(part % (parts // 2) * size, size)]
            reads.append(pltpu.make_async_copy(source, held.at[part, at], come.at[4 * part + at]))
    for read in reads:
        read.start()
    writes = []
    for part in range(parts):
        for read in reads[4 * part : 4 * part + 4]:
            read.wait()
        for i in range(size):
            for b in range(slots):
                factor = scales[(part * size + i) * slots + b]
                for at, (_, _, columns) in enumerate(piece_places(place[0], pieces[:4])):
                    values = held[part, at, i, b * rows : (b + 1) * rows].astype(F32) * factor
                    ready[part * size + i, b, :, columns] = values.astype(BF16)
        span = pl.ds(part * size, size)
        writes.append(pltpu.make_async_copy(ready.at[span], out.at[span], go.at[part]))
        writes[-1].start()
    for write in writes:
        write.wait()


def scale_both(scales, place, pieces, parts=4, slots=2):
    count, rows, width = pieces[0].shape
    shape = (count, slots, rows // slots, 4 * width)
    return pl.pallas_call(
        scale_both_kernel,
        out_shape=jax.ShapeDtypeStruct(shape, BF16),
        in_specs=[SMEM, SMEM] + anywhere(5),
        out_specs=anywhere(1)[0],
        scratch_shapes=[
            pltpu.VMEM((parts, 4, count // parts, rows, width), BF16),
            pltpu.VMEM(shape, BF16),
            pltpu.SemaphoreType.DMA((4 * parts,)),
            pltpu.SemaphoreType.DMA((parts,)),
        ],
        compiler_params=params(0),
        cost_estimate=cost(0, COSTS[2] * count * rows * width),
        name="scale",
    )(scales, place, *pieces)


def in_order(flag, first, *later):
    if flag not in ORDER:
        return (first, *later)
    return lax.optimization_barrier((first, *later))


def scatter_first(messages):
    return shift(messages[0], 1), shift(messages[1], -1)


def scatter_second(messages, first, mine):
    _, _, keep_right, keep_left, own = messages
    half = own.shape[0] // 2
    from_left, from_right = first
    return (
        shift(jnp.where(mine, keep_right, from_left[half:]), 1),
        shift(jnp.where(mine, keep_left, from_right[half:]), -1),
    )


def merge(messages, first, second, away):
    own, half = messages[4], messages[4].shape[0] // 2
    low = jnp.where(away == 1, first[1][:half], second[0][:half])
    low = jnp.where(away == 0, own[:half], low)
    high = jnp.where(away == 3, first[0][:half], second[1][:half])
    high = jnp.where(away == 0, own[half : 2 * half], high)
    return jnp.concatenate([low, high], axis=0)


def gather_first(quarter):
    return quarter, shift(quarter, 1), shift(quarter, -1)


def gather_second(pieces):
    _, left, right = pieces
    half = left.shape[0] // 2
    return [*pieces, shift(left[:half], 1), shift(right[half:], -1)]


def per_device(
    gradients, stat_left, stat_right, inv_left, inv_right, owned_blocks, owner_counts, block_matrix
):
    dp_count = lax.axis_size("dp")
    owner_total = lax.axis_size("replica")
    dp_index = lax.axis_index("dp")
    me = lax.axis_index("replica")
    block_total, shard_rows, order = gradients.shape
    local_total = block_total // dp_count
    slot_total = inv_left.shape[2]
    width = order // owner_total
    half = dp_count // 2

    by_owner = gradients.reshape(dp_count, local_total, shard_rows, order)
    if FRONT == "QD":
        my_columns = lax.dynamic_slice(
            by_owner, (0, 0, 0, me * width), (dp_count, 1, shard_rows, width)
        ).reshape(dp_count, shard_rows, width)
        arrived, late = in_order("p", over_dp(my_columns), by_owner)
        first_pieces = gather_first(arrived)
        second_block = over_dp(pick_block(late, 1))
        blocks = [gather_second(first_pieces), [second_block]]
    elif FRONT == "DD":
        picked = [pick_block(by_owner, b) for b in range(local_total)]
        arrived = over_dp(picked[0])
        arrived, picked[1] = in_order("p", arrived, picked[1])
        blocks = [[arrived], [over_dp(picked[1])]]
    else:
        arrived = over_dp(gradients).reshape(dp_count, local_total, shard_rows, order)
        blocks = [[arrived], [arrived]]

    slot_ids = jnp.arange(slot_total, dtype=jnp.int32)
    live = slot_ids[None, None, :] < owner_counts[:, :, None]
    replica_ids = jnp.arange(owner_total, dtype=jnp.int32)
    infos, owners = [], []
    for b in range(local_total):
        match = (owned_blocks == b) & live
        owners.append(jnp.sum(jnp.where(match, replica_ids[None, :, None], 0), axis=(1, 2)))
        slots = jnp.sum(jnp.where(match, slot_ids[None, None, :], 0), axis=(1, 2))
        owner = lax.dynamic_index_in_dim(owners[b], dp_index, 0, keepdims=False)
        slot = lax.dynamic_index_in_dim(slots, dp_index, 0, keepdims=False)
        away = lax.rem(owner - me + owner_total, owner_total)
        info = jnp.stack([slot, (away == 0).astype(jnp.int32), me, away])
        infos.append(info.astype(jnp.int32))

    away = [info[3] for info in infos]

    *sent, sums = apply_roots(infos[0], inv_left[0, 0], blocks[0], inv_right[0, 0])
    got = scatter_first(sent)
    sent_next = apply_roots(infos[1], inv_left[0, 0], blocks[1], inv_right[0, 0], sums)
    sent_next, got = in_order("r", sent_next, got)
    got_more = scatter_second(sent, got, away[0] == 0)
    got_more, sent_next = in_order("s", got_more, sent_next)
    got_next = scatter_first(sent_next)
    got_more, sent_next = in_order("m", got_more, sent_next)
    quarter = merge(sent, got, got_more, away[0])
    quarter, stat_left, stat_right = in_order("a", quarter, stat_left, stat_right)
    if not MERGED:
        first = over_dp(quarter)
        first, stat_left, stat_right = in_order("t", first, stat_left, stat_right)
        first, got_next = in_order("x", first, got_next)
    stats = update_stats(0, infos[0], blocks[0], stat_left, stat_right, None)
    stats, got_next = in_order("b", stats, got_next)

    chunk = lax.broadcasted_iota(jnp.int32, sent_next[2].shape, 0)
    lane = lax.broadcasted_iota(jnp.int32, sent_next[2].shape, 2)
    of_before = (chunk == half) & (lane < width // 2)
    got_next_more = scatter_second(sent_next, got_next, jnp.where(of_before, away[0], away[1]) == 0)
    far_off = jnp.where(of_before[half], away[0], away[1])
    sums = jnp.where(far_off == 1, got_next[1][2 * half], got_next_more[0][half])
    sums = jnp.where(far_off == 3, got_next[0][2 * half], sums)
    sums = jnp.where(far_off == 0, sent_next[4][2 * half], sums)
    sums = jnp.broadcast_to(sums[None, :EXTRA], (dp_count, EXTRA, width))
    stats, got_next_more = in_order("c", stats, got_next_more)
    stats = update_stats(1, infos[1], blocks[1], stat_left, stat_right, stats)
    quarter_next = merge(sent_next, got_next, got_next_more, away[1])
    stats, quarter_next = in_order("u", stats, quarter_next)
    if MERGED:
        second = over_dp(jnp.concatenate([quarter, quarter_next, sums], axis=1))
        stats, second = in_order("d", stats, second)
        both = gather_first(second[:, : 2 * shard_rows])
        far = gather_second(both)
        sums = second[:, 2 * shard_rows : 2 * shard_rows + 6, :].astype(F32)
    else:
        pieces = gather_first(first)
        pieces, quarter_next = in_order("y", pieces, quarter_next)
        second = over_dp(jnp.concatenate([quarter_next, sums], axis=1))
        pieces, second = in_order("v", pieces, second)
        gathered = gather_second(pieces)
        pieces_next = gather_first(second[:, :shard_rows])
        gathered, pieces_next = in_order("w", gathered, pieces_next)
        sums = second[:, shard_rows : shard_rows + 6, :].astype(F32)

    sums = sums.reshape(dp_count, 2, 3, local_total, width // local_total)[..., 0]
    sums = jnp.sum(sums, axis=2) / SUM_SCALE
    sums = jnp.swapaxes(sums, 1, 2).reshape(block_total, 2)

    matrix_ids = jnp.arange(NMAT, dtype=jnp.int32)
    matrix_hot = (block_matrix[:, None] == matrix_ids[None, :]).astype(F32)
    totals = jnp.sum(matrix_hot[:, :, None] * sums[:, None, :], axis=0)
    graft = jnp.sqrt(totals[:, 1]) / jnp.sqrt(totals[:, 0] + EPSILON)
    scales = jnp.sum(matrix_hot * graft[None, :], axis=1)

    place = me.reshape(1).astype(jnp.int32)
    if MERGED:
        update = scale_both(scales, place, far)
    else:
        update = scale_rows(0, local_total, scales, place, gathered, None)
        update, pieces_next = in_order("z", update, pieces_next)
        update = scale_rows(1, local_total, scales, place, gather_second(pieces_next), update)
    return (update.reshape(block_total, shard_rows, order), *stats)


def solution(mesh):
    return jax.shard_map(
        per_device,
        mesh=mesh,
        in_specs=(
            P(None, "dp", None),
            P("dp", "replica", None),
            P("dp", "replica", None),
            P("dp", "replica", None, None, None),
            P("dp", "replica", None, None, None),
            P(),
            P(),
            P(),
        ),
        out_specs=(P(None, "dp", None), P("dp", "replica", None), P("dp", "replica", None)),
        check_vma=False,
    )
```

time: 482 us -> 167 us (0.35)
  waiting for transfers between devices: 243 us -> 48.7 us
  blocking collectives: 143 us -> 20 us
  starting transfers between devices: 16.5 us -> 49.2 us
  local copies, waits for them, and re-layouts: 41.6 us -> 11.4 us
  Pallas kernels: 0 us -> 24.7 us
  between operations: 15.5 us -> 2.58 us
  matrix products: 8.22 us -> 0 us
    all_gather x1 -> x0, waiting for transfers between devices: 151 us -> none  [per_device(): gathered = lax.all_gather(pre_slots, 'replica', axis=0, tiled=True)]
    psum x2 -> x0, blocking collectives: 143 us -> none  [the longest x1 73.2 us: per_device(): grad_total = lax.psum(jnp.sum(matrix_hot * grad_sq[:, None], axis=0), 'dp')]
    all_to_all x2 -> x3, waiting for transfers between devices: 92 us -> 15.7 us  [over_dp(): return lax.all_to_all(x, 'dp', split_axis=0, concat_axis=0, tiled=True)]
    ppermute x0 -> x20, starting transfers between devices: none -> 37.2 us  [shift(): lax.ppermute(x, 'replica', [(i, (i + step) % count) for i in range(count)])]
    ppermute x0 -> x20, waiting for transfers between devices: none -> 33 us  [shift(): lax.ppermute(x, 'replica', [(i, (i + step) % count) for i in range(count)])]
    pallas_call x0 -> x7, Pallas kernels: none -> 24.7 us  [the longest x2 11 us: update_stats(): pl.pallas_call(lambda *refs: stats_kernel(b, len(pieces), *refs), out_sha...]
    gather x4 -> x0, local copies, waits for them, and re-layouts: 21.7 us -> none  [the longest x3 21.1 us: per_device(): mine = jnp.take(gathered, picks, axis=0)]
    all_to_all x0 -> x1, blocking collectives: none -> 20 us  [over_dp(): return lax.all_to_all(x, 'dp', split_axis=0, concat_axis=0, tiled=True)]
  transfers between devices with their start and end apart: 3 -> 23, of which waited for: 3 -> 15; matrix products, arithmetic and copies ran while one was open for 3% -> 10% of each run, Pallas kernels for 0% -> 13%
where the time goes in v2:
time: 167 us
  starting transfers between devices  49.2 us (29%)
  waiting for transfers between devices  48.7 us (29%)
  Pallas kernels  24.7 us (15%)
  blocking collectives  20 us (12%)
  local copies, waits for them, and re-layouts  11.4 us (7%)
  other arithmetic  9.89 us (6%)
  between operations  2.58 us (2%)
    ppermute x20, starting transfers between devices, shift(): lax.ppermute(x, 'replica', [(i, (i + step) % count) for i in range(count)])  37.2 us
    ppermute x20, waiting for transfers between devices, shift(): lax.ppermute(x, 'replica', [(i, (i + step) % count) for i in range(count)])  33 us
    all_to_all x1, blocking collectives, over_dp(): return lax.all_to_all(x, 'dp', split_axis=0, concat_axis=0, tiled=True)  20 us
    all_to_all x3, waiting for transfers between devices, over_dp(): return lax.all_to_all(x, 'dp', split_axis=0, concat_axis=0, tiled=True)  15.7 us
    all_to_all x3, starting transfers between devices, over_dp(): return lax.all_to_all(x, 'dp', split_axis=0, concat_axis=0, tiled=True)  12 us
    pallas_call x2, Pallas kernels, update_stats(): pl.pallas_call(lambda *refs: stats_kernel(b, len(pieces), *refs), out_sha...  11 us
    pallas_call x2, Pallas kernels, scale_rows(): pl.pallas_call(lambda *refs: scale_kernel(which, slots, *refs), out_shape...  6.85 us
    pallas_call x2, Pallas kernels, apply_roots(): pl.pallas_call(lambda *refs: roots_kernel(len(pieces), before is not None...  4.53 us
  transfers between devices with their start and end apart: 23, of which 15 were waited for; matrix products, arithmetic and copies ran while one was open for 10% of the time, Pallas kernels for 13%

profile of v2, /device:TPU:0, one launch (start us, length us, event | category | flops | bytes accessed | tf_op | source)
XLA Modules:
  0.0 166.6 jit_solution(2987375098950255811)
XLA Ops:
  1.7 20.0 %all_to_all.20.refs_3_.refs_1_ = bf16[32,32,256]{2,1,0:T(8,128)(2,1)S(1)} all-to-all(bf16[32,32,256]{2,1,0:T(8,128)(2,1)S(1)} %dynamic-slice_bitcast_fusion), channel_id=1, replica_groups=mesh['dp'=32,'replica'=4] {'dp'}, dimensions={0} | all-to-all | bytes 1048576 | tf_op jit(solution)/shard_map/all_to_all | solution.py:37
  21.7 2.8 %collective-permute-start.1 = (bf16[32,32,256]{2,1,0:T(8,128)(2,1)S(1)}, bf16[32,32,256]{2,1,0:T(8,128)(2,1)S(1)}, u32[]{:S(2)}, u32[]{:S(2)}) collective-permute-start(bf16[32,32,256]{2,1,0:T(8,128)(2,1)S(1)} %all_to_all.20.refs_3_.refs_1_), channel_id=1, source_target_pairs={{0,3},{1,0},{2,1},{3,2},{4,7},{5,4},{6,5},{7,6},{8,11},{9,8},{10,9... | collective-permute-start | bytes 1572872 | tf_op jit(solution)/shard_map/ppermute | solution.py:33
  24.5 2.4 %pick.1 = bf16[32,32,1024]{2,1,0:T(8,128)(2,1)} custom-call(bf16[32,2,32,1024]{3,2,1,0:T(8,128)(2,1)} %bitcast.21), custom_call_target="tpu_custom_call" | custom-call | bytes 8388608 | tf_op jit(solution)/shard_map/pick/pallas_call | solution.py:69
  26.9 4.0 %all-to-all-start = ((bf16[32,32,1024]{2,1,0:T(8,128)(2,1)}), bf16[32,32,1024]{2,1,0:T(8,128)(2,1)S(1)}, u32[]{:S(2)}, u32[]{:S(2)}) async-start(bf16[32,32,1024]{2,1,0:T(8,128)(2,1)} %pick.1), calls=%async_computation | async-start | bytes 4194304 | tf_op jit(solution)/shard_map/all_to_all | solution.py:37
  31.0 4.9 %collective-permute-done.1.refs_5_.refs_3_ = bf16[32,32,256]{2,1,0:T(8,128)(2,1)S(1)} collective-permute-done((bf16[32,32,256]{2,1,0:T(8,128)(2,1)S(1)}, bf16[32,32,256]{2,1,0:T(8,128)(2,1)S(1)}, u32[]{:S(2)}, u32[]{:S(2)}) %collective-permute-start.1) | collective-permute-done | bytes 524320 | tf_op jit(solution)/shard_map/ppermute | solution.py:33
  35.9 3.8 %collective-permute-start.3 = (bf16[16,32,256]{2,1,0:T(8,128)(2,1)S(1)}, bf16[16,32,256]{2,1,0:T(8,128)(2,1)}, u32[]{:S(2)}, u32[]{:S(2)}) collective-permute-start(bf16[16,32,256]{2,1,0:T(8,128)(2,1)S(1)} %slice.130), channel_id=1, source_target_pairs={{0,3},{1,0},{2,1},{3,2},{4,7},{5,4},{6,5},{7,6},{8,11},{9,8},{10,9... | collective-permute-start | bytes 786440 | tf_op jit(solution)/shard_map/ppermute | solution.py:33
  46.8 2.2 %collective-permute-done.2.refs_6_.refs_4_ = bf16[16,32,256]{2,1,0:T(8,128)(2,1)S(1)} collective-permute-done((bf16[16,32,256]{2,1,0:T(8,128)(2,1)S(1)}, bf16[16,32,256]{2,1,0:T(8,128)(2,1)S(1)}, u32[]{:S(2)}, u32[]{:S(2)}) %collective-permute-start.2) | collective-permute-done | bytes 262176 | tf_op jit(solution)/shard_map/ppermute | solution.py:33
  49.8 2.1 %roots.2 = (bf16[32,32,256]{2,1,0:T(8,128)(2,1)}, bf16[32,32,256]{2,1,0:T(8,128)(2,1)}, bf16[16,32,256]{2,1,0:T(8,128)(2,1)}, bf16[16,32,256]{2,1,0:T(8,128)(2,1...) custom-call(s32[4]{0:T(128)} %pad_add_fusion.1.refs_0_, bf16[2,1024,1024]{2,1,0:T(8,128)(2,1)} %bitcast.22, ...), custom_call_target="tpu_custom_call" | custom-call | flops 17179869184 | bytes 10485760 | tf_op jit(solution)/shard_map/roots/pallas_call | solution.py:201
  51.9 8.2 %collective-permute-start.12 = (bf16[32,32,256]{2,1,0:T(8,128)(2,1)}, bf16[32,32,256]{2,1,0:T(8,128)(2,1)S(1)}, u32[]{:S(2)}, u32[]{:S(2)}) collective-permute-start(bf16[32,32,256]{2,1,0:T(8,128)(2,1)} %get-tuple-element.25), channel_id=1, source_target_pairs={{0,3},{1,0},{2,1},{3,2},{4,7},{5,4},{6,5},{7,6},{8,11},{9,8},{10,9... | collective-permute-start | bytes 1572872 | tf_op jit(solution)/shard_map/ppermute | solution.py:33
  62.3 2.4 %roots.3 = (bf16[33,32,256]{2,1,0:T(8,128)(2,1)}, bf16[33,32,256]{2,1,0:T(8,128)(2,1)}, bf16[17,32,256]{2,1,0:T(8,128)(2,1)}, bf16[17,32,256]{2,1,0:T(8,128)(2,1)}, bf16[33,32,256]{2,1,0:T(8,128)(2,1)}) custom-call(s32[4]{0:T(128)} %pad_add_fusion.refs_0_, bf16[2,1024,1024]{2,1,0:T(8,128)(2,1)} %bitcast.23, bf16[2,1024,1024]{2,1,0:T(8,128)(2,1)} %bitcast.25, ...), custom_call_target="tpu_custom_call" | custom-call | flops 17179869184 | bytes 10485760 | tf_op jit(solution)/shard_map/roots/pallas_call | solution.py:201
  64.7 10.4 %collective-permute-start.4 = (bf16[33,32,256]{2,1,0:T(8,128)(2,1)}, bf16[33,32,256]{2,1,0:T(8,128)(2,1)S(1)}, u32[]{:S(2)}, u32[]{:S(2)}) collective-permute-start(bf16[33,32,256]{2,1,0:T(8,128)(2,1)} %get-tuple-element.20), channel_id=1, source_target_pairs={{0,3},{1,0},{2,1},{3,2},{4,7},{5,4},{6,5},{7,6},{8,11},{9,8},{10,9... | collective-permute-start | bytes 1622024 | tf_op jit(solution)/shard_map/ppermute | solution.py:33
  75.3 3.3 %collective-permute-start.15 = (bf16[16,32,256]{2,1,0:T(8,128)(2,1)S(1)}, bf16[16,32,256]{2,1,0:T(8,128)(2,1)S(1)}, u32[]{:S(2)}, u32[]{:S(2)}) collective-permute-start(bf16[16,32,256]{2,1,0:T(8,128)(2,1)S(1)} %slice_select_fusion), channel_id=1, source_target_pairs={{0,3},{1,0},{2,1},{3,2},{4,7},{5,4},{6,5},{7,6},{8,11},{9,8},{10,9... | collective-permute-start | bytes 786440 | tf_op jit(solution)/shard_map/ppermute | solution.py:33
  80.4 7.7 %collective-permute-done.4 = bf16[33,32,256]{2,1,0:T(8,128)(2,1)S(1)} collective-permute-done((bf16[33,32,256]{2,1,0:T(8,128)(2,1)}, bf16[33,32,256]{2,1,0:T(8,128)(2,1)S(1)}, u32[]{:S(2)}, u32[]{:S(2)}) %collective-permute-start.4) | collective-permute-done | bytes 540704 | tf_op jit(solution)/shard_map/ppermute | solution.py:33
  88.1 3.7 %collective-permute-done.5 = bf16[33,32,256]{2,1,0:T(8,128)(2,1)S(1)} collective-permute-done((bf16[33,32,256]{2,1,0:T(8,128)(2,1)}, bf16[33,32,256]{2,1,0:T(8,128)(2,1)S(1)}, u32[]{:S(2)}, u32[]{:S(2)}) %collective-permute-start.5) | collective-permute-done | bytes 540704 | tf_op jit(solution)/shard_map/ppermute | solution.py:33
  93.1 4.1 %collective-permute-done.14 = bf16[16,32,256]{2,1,0:T(8,128)(2,1)S(1)} collective-permute-done((bf16[16,32,256]{2,1,0:T(8,128)(2,1)S(1)}, bf16[16,32,256]{2,1,0:T(8,128)(2,1)S(1)}, u32[]{:S(2)}, u32[]{:S(2)}) %collective-permute-start.14) | collective-permute-done | bytes 262176 | tf_op jit(solution)/shard_map/ppermute | solution.py:33
  99.2 3.9 %all-to-all-start.3 = ((bf16[32,32,256]{2,1,0:T(8,128)(2,1)}), bf16[32,32,256]{2,1,0:T(8,128)(2,1)S(1)}, u32[]{:S(2)}, u32[]{:S(2)}) async-start(bf16[32,32,256]{2,1,0:T(8,128)(2,1)} %pad_maximum_fusion.1), calls=%async_computation.3 | async-start | bytes 1048576 | tf_op jit(solution)/shard_map/all_to_all | solution.py:37
  106.9 8.0 %all-to-all-done.3.refs_2_ = bf16[32,32,256]{2,1,0:T(8,128)(2,1)S(1)} async-done(((bf16[32,32,256]{2,1,0:T(8,128)(2,1)}), bf16[32,32,256]{2,1,0:T(8,128)(2,1)S(1)}, u32[]{:S(2)}, u32[]{:S(2)}) %all-to-all-start.3) | async-done | bytes 524320 | tf_op jit(solution)/shard_map/all_to_all | solution.py:37
  114.9 4.1 %all-to-all-start.2 = ((bf16[32,48,256]{2,1,0:T(8,128)(2,1)}), bf16[32,48,256]{2,1,0:T(8,128)(2,1)S(1)}, u32[]{:S(2)}, u32[]{:S(2)}) async-start(bf16[32,48,256]{2,1,0:T(8,128)(2,1)} %pad_maximum_fusion), calls=%async_computation.2 | async-start | bytes 1572864 | tf_op jit(solution)/shard_map/all_to_all | solution.py:37
  119.0 5.5 %stats.2 = (f32[2,256,1024]{2,1,0:T(8,128)}, f32[2,256,1024]{2,1,0:T(8,128)}) custom-call(s32[4]{0:T(128)} %pad_add_fusion.1.refs_0_, bf16[32,32,256]{2,1,0:T(8,128)(2,1)} %copy-done.7, bf16[32,32,256]{2,1,0:T(8,128)(2,1)} %collective-permute-done.refs_4_.refs_2_, bf16[32,32,256]{2,1,0:T(8,128)(2,1)} %copy-done.14, bf16[16,32,256]{2,1,0:T(8,128)(2,1)} %copy-done.18, ...), custom_call_target="tpu_custom_call" | custom-call | flops 6442450944 | bytes 6291456 | tf_op jit(solution)/shard_map/stats/pallas_call | solution.py:261
  126.6 6.9 %all-to-all-done.2 = bf16[32,48,256]{2,1,0:T(8,128)(2,1)S(1)} async-done(((bf16[32,48,256]{2,1,0:T(8,128)(2,1)}), bf16[32,48,256]{2,1,0:T(8,128)(2,1)S(1)}, u32[]{:S(2)}, u32[]{:S(2)}) %all-to-all-start.2) | async-done | bytes 786464 | tf_op jit(solution)/shard_map/all_to_all | solution.py:37
  135.8 5.5 %stats.3 = (f32[2,256,1024]{2,1,0:T(8,128)}, f32[2,256,1024]{2,1,0:T(8,128)}) custom-call(s32[4]{0:T(128)} %pad_add_fusion.refs_0_, bf16[32,32,1024]{2,1,0:T(8,128)(2,1)} %copy-done, f32[2,256,1024]{2,1,0:T(8,128)} %refs_2_.1, f32[2,256,1024]{2,1,0:T(8,128)} %refs_3_.1, ...), custom_call_target="tpu_custom_call", output_to_operand_aliasing={{0}: (4, {}), {1}: (5, {})} | custom-call | flops 6442450944 | bytes 6291456 | tf_op jit(solution)/shard_map/stats/pallas_call | solution.py:261
  145.2 5.2 %collective-permute-done.9.refs_4_ = bf16[32,32,256]{2,1,0:T(8,128)(2,1)S(1)} collective-permute-done((bf16[32,32,256]{2,1,0:T(8,128)(2,1)S(1)}, bf16[32,32,256]{2,1,0:T(8,128)(2,1)S(1)}, u32[]{:S(2)}, u32[]{:S(2)}) %collective-permute-start.9) | collective-permute-done | bytes 524320 | tf_op jit(solution)/shard_map/ppermute | solution.py:33
  157.6 3.4 %scale.2.refs_7_ = bf16[32,2,32,1024]{3,2,1,0:T(8,128)(2,1)} custom-call(f32[64]{0:T(128)} %select_reduce_fusion.refs_0_, s32[1]{0:T(128)} %bitcast.2.refs_1_, bf16[32,32,256]{2,1,0:T(8,128)(2,1)} %copy-done.1, bf16[32,32,256]{2,1,0:T(8,128)(2,1)} %copy-done.4, bf16[32,32,256]{2,1,0:T(8,128)(2,1)} %copy-done.3, ...), custom_call_target="tpu_custom_call" | custom-call | bytes 12582912 | tf_op jit(solution)/shard_map/scale/pallas_call | solution.py:310
  163.0 3.4 %scale.3 = bf16[32,2,32,1024]{3,2,1,0:T(8,128)(2,1)} custom-call(f32[64]{0:T(128)} %select_reduce_fusion.refs_0_, s32[1]{0:T(128)} %bitcast.2.refs_1_, bf16[32,32,256]{2,1,0:T(8,128)(2,1)} %copy-done.2, bf16[32,32,256]{2,1,0:T(8,128)(2,1)} %collective-permute-done.8.refs_3_, bf16[32,32,256]{2,1,0:T(8,128)(2,1)} %copy-done.5, ...), custom_call_target="tpu_custom_call", output_to_operand_aliasing={{}: (7, {})} | custom-call | bytes 12582912 | tf_op jit(solution)/shard_map/scale/pallas_call | solution.py:310
  (111 shorter events, 36.3 us)
Async XLA Ops:
  21.7 14.2 %collective-permute-start.1 = (bf16[32,32,256]{2,1,0:T(8,128)(2,1)S(1)}, bf16[32,32,256]{2,1,0:T(8,128)(2,1)S(1)}, u32[]{:S(2)}, u32[]{:S(2)}) collective-permute-start(bf16[32,32,256]{2,1,0:T(8,128)(2,1)S(1)} %all_to_all.20.refs_3_.refs_1_), channel_id=1, source_target_pairs={{0,3},{1,0},{2,1},{3,2},{4,7},{5,4},{6,5},{7,6},{8,11},{9,8},{10,9... | collective-permute-start | bytes 1572872 | tf_op jit(solution)/shard_map/ppermute | solution.py:33
  24.5 15.2 %collective-permute-start = (bf16[32,32,256]{2,1,0:T(8,128)(2,1)S(1)}, bf16[32,32,256]{2,1,0:T(8,128)(2,1)}, u32[]{:S(2)}, u32[]{:S(2)}) collective-permute-start(bf16[32,32,256]{2,1,0:T(8,128)(2,1)S(1)} %all_to_all.20.refs_3_.refs_1_), channel_id=1, source_target_pairs={{0,1},{1,2},{2,3},{3,0},{4,5},{5,6},{6,7},{7,4},{8,9},{9,10},{10,1... | collective-permute-start | bytes 1572872 | tf_op jit(solution)/shard_map/ppermute | solution.py:33
  26.9 34.0 %all-to-all-start = ((bf16[32,32,1024]{2,1,0:T(8,128)(2,1)}), bf16[32,32,1024]{2,1,0:T(8,128)(2,1)S(1)}, u32[]{:S(2)}, u32[]{:S(2)}) async-start(bf16[32,32,1024]{2,1,0:T(8,128)(2,1)} %pick.1), calls=%async_computation | async-start | bytes 4194304 | tf_op jit(solution)/shard_map/all_to_all | solution.py:37
  35.9 10.9 %collective-permute-start.3 = (bf16[16,32,256]{2,1,0:T(8,128)(2,1)S(1)}, bf16[16,32,256]{2,1,0:T(8,128)(2,1)}, u32[]{:S(2)}, u32[]{:S(2)}) collective-permute-start(bf16[16,32,256]{2,1,0:T(8,128)(2,1)S(1)} %slice.130), channel_id=1, source_target_pairs={{0,3},{1,0},{2,1},{3,2},{4,7},{5,4},{6,5},{7,6},{8,11},{9,8},{10,9... | collective-permute-start | bytes 786440 | tf_op jit(solution)/shard_map/ppermute | solution.py:33
  40.6 8.4 %collective-permute-start.2 = (bf16[16,32,256]{2,1,0:T(8,128)(2,1)S(1)}, bf16[16,32,256]{2,1,0:T(8,128)(2,1)S(1)}, u32[]{:S(2)}, u32[]{:S(2)}) collective-permute-start(bf16[16,32,256]{2,1,0:T(8,128)(2,1)S(1)} %slice.129), channel_id=1, source_target_pairs={{0,1},{1,2},{2,3},{3,0},{4,5},{5,6},{6,7},{7,4},{8,9},{9,10},{10,1... | collective-permute-start | bytes 786440 | tf_op jit(solution)/shard_map/ppermute | solution.py:33
  51.9 23.3 %collective-permute-start.12 = (bf16[32,32,256]{2,1,0:T(8,128)(2,1)}, bf16[32,32,256]{2,1,0:T(8,128)(2,1)S(1)}, u32[]{:S(2)}, u32[]{:S(2)}) collective-permute-start(bf16[32,32,256]{2,1,0:T(8,128)(2,1)} %get-tuple-element.25), channel_id=1, source_target_pairs={{0,3},{1,0},{2,1},{3,2},{4,7},{5,4},{6,5},{7,6},{8,11},{9,8},{10,9... | collective-permute-start | bytes 1572872 | tf_op jit(solution)/shard_map/ppermute | solution.py:33
  60.1 18.5 %collective-permute-start.13 = (bf16[32,32,256]{2,1,0:T(8,128)(2,1)}, bf16[32,32,256]{2,1,0:T(8,128)(2,1)}, u32[]{:S(2)}, u32[]{:S(2)}) collective-permute-start(bf16[32,32,256]{2,1,0:T(8,128)(2,1)} %get-tuple-element.27), channel_id=1, source_target_pairs={{0,1},{1,2},{2,3},{3,0},{4,5},{5,6},{6,7},{7,4},{8,9},{9,10},{10,1... | collective-permute-start | bytes 1572872 | tf_op jit(solution)/shard_map/ppermute | solution.py:33
  64.7 32.5 %copy-start.8 = (bf16[32,32,256]{2,1,0:T(8,128)(2,1)S(1)}, bf16[32,32,256]{2,1,0:T(8,128)(2,1)}, u32[]{:S(2)}) copy-start(bf16[32,32,256]{2,1,0:T(8,128)(2,1)} %get-tuple-element.24) | copy-start | bytes 1572868
  64.7 23.4 %collective-permute-start.4 = (bf16[33,32,256]{2,1,0:T(8,128)(2,1)}, bf16[33,32,256]{2,1,0:T(8,128)(2,1)S(1)}, u32[]{:S(2)}, u32[]{:S(2)}) collective-permute-start(bf16[33,32,256]{2,1,0:T(8,128)(2,1)} %get-tuple-element.20), channel_id=1, source_target_pairs={{0,3},{1,0},{2,1},{3,2},{4,7},{5,4},{6,5},{7,6},{8,11},{9,8},{10,9... | collective-permute-start | bytes 1622024 | tf_op jit(solution)/shard_map/ppermute | solution.py:33
  75.1 16.6 %collective-permute-start.5 = (bf16[33,32,256]{2,1,0:T(8,128)(2,1)}, bf16[33,32,256]{2,1,0:T(8,128)(2,1)S(1)}, u32[]{:S(2)}, u32[]{:S(2)}) collective-permute-start(bf16[33,32,256]{2,1,0:T(8,128)(2,1)} %get-tuple-element.22), channel_id=1, source_target_pairs={{0,1},{1,2},{2,3},{3,0},{4,5},{5,6},{6,7},{7,4},{8,9},{9,10},{10,1... | collective-permute-start | bytes 1622024 | tf_op jit(solution)/shard_map/ppermute | solution.py:33
  75.3 17.8 %collective-permute-start.15 = (bf16[16,32,256]{2,1,0:T(8,128)(2,1)S(1)}, bf16[16,32,256]{2,1,0:T(8,128)(2,1)S(1)}, u32[]{:S(2)}, u32[]{:S(2)}) collective-permute-start(bf16[16,32,256]{2,1,0:T(8,128)(2,1)S(1)} %slice_select_fusion), channel_id=1, source_target_pairs={{0,3},{1,0},{2,1},{3,2},{4,7},{5,4},{6,5},{7,6},{8,11},{9,8},{10,9... | collective-permute-start | bytes 786440 | tf_op jit(solution)/shard_map/ppermute | solution.py:33
  79.6 17.6 %collective-permute-start.14 = (bf16[16,32,256]{2,1,0:T(8,128)(2,1)S(1)}, bf16[16,32,256]{2,1,0:T(8,128)(2,1)S(1)}, u32[]{:S(2)}, u32[]{:S(2)}) collective-permute-start(bf16[16,32,256]{2,1,0:T(8,128)(2,1)S(1)} %slice_select_fusion.2), channel_id=1, source_target_pairs={{0,1},{1,2},{2,3},{3,0},{4,5},{5,6},{6,7},{7,4},{8,9},{9,10},{10,1... | collective-permute-start | bytes 786440 | tf_op jit(solution)/shard_map/ppermute | solution.py:33
  93.0 10.1 %collective-permute-start.6 = (bf16[17,32,256]{2,1,0:T(8,128)(2,1)S(1)}, bf16[17,32,256]{2,1,0:T(8,128)(2,1)}, u32[]{:S(2)}, u32[]{:S(2)}) collective-permute-start(bf16[17,32,256]{2,1,0:T(8,128)(2,1)S(1)} %get-tuple-element.44), channel_id=1, source_target_pairs={{0,1},{1,2},{2,3},{3,0},{4,5},{5,6},{6,7},{7,4},{8,9},{9,10},{10,1... | collective-permute-start | bytes 835592 | tf_op jit(solution)/shard_map/ppermute | solution.py:33
  98.3 6.6 %collective-permute-start.7 = (bf16[17,32,256]{2,1,0:T(8,128)(2,1)S(1)}, bf16[17,32,256]{2,1,0:T(8,128)(2,1)S(1)}, u32[]{:S(2)}, u32[]{:S(2)}) collective-permute-start(bf16[17,32,256]{2,1,0:T(8,128)(2,1)S(1)} %get-tuple-element.43), channel_id=1, source_target_pairs={{0,3},{1,0},{2,1},{3,2},{4,7},{5,4},{6,5},{7,6},{8,11},{9,8},{10,9... | collective-permute-start | bytes 835592 | tf_op jit(solution)/shard_map/ppermute | solution.py:33
  99.2 15.7 %all-to-all-start.3 = ((bf16[32,32,256]{2,1,0:T(8,128)(2,1)}), bf16[32,32,256]{2,1,0:T(8,128)(2,1)S(1)}, u32[]{:S(2)}, u32[]{:S(2)}) async-start(bf16[32,32,256]{2,1,0:T(8,128)(2,1)} %pad_maximum_fusion.1), calls=%async_computation.3 | async-start | bytes 1048576 | tf_op jit(solution)/shard_map/all_to_all | solution.py:37
  114.9 18.7 %all-to-all-start.2 = ((bf16[32,48,256]{2,1,0:T(8,128)(2,1)}), bf16[32,48,256]{2,1,0:T(8,128)(2,1)S(1)}, u32[]{:S(2)}, u32[]{:S(2)}) async-start(bf16[32,48,256]{2,1,0:T(8,128)(2,1)} %pad_maximum_fusion), calls=%async_computation.2 | async-start | bytes 1572864 | tf_op jit(solution)/shard_map/all_to_all | solution.py:37
  124.5 16.8 %collective-permute-start.17 = (bf16[32,32,256]{2,1,0:T(8,128)(2,1)S(1)}, bf16[32,32,256]{2,1,0:T(8,128)(2,1)S(1)}, u32[]{:S(2)}, u32[]{:S(2)}) collective-permute-start(bf16[32,32,256]{2,1,0:T(8,128)(2,1)S(1)} %all-to-all-done.3.refs_2_), channel_id=1, source_target_pairs={{0,3},{1,0},{2,1},{3,2},{4,7},{5,4},{6,5},{7,6},{8,11},{9,8},{10,9... | collective-permute-start | bytes 1572872 | tf_op jit(solution)/shard_map/ppermute | solution.py:33
  124.5 18.8 %collective-permute-start.16 = (bf16[32,32,256]{2,1,0:T(8,128)(2,1)S(1)}, bf16[32,32,256]{2,1,0:T(8,128)(2,1)S(1)}, u32[]{:S(2)}, u32[]{:S(2)}) collective-permute-start(bf16[32,32,256]{2,1,0:T(8,128)(2,1)S(1)} %all-to-all-done.3.refs_2_), channel_id=1, source_target_pairs={{0,1},{1,2},{2,3},{3,0},{4,5},{5,6},{6,7},{7,4},{8,9},{9,10},{10,1... | collective-permute-start | bytes 1572872 | tf_op jit(solution)/shard_map/ppermute | solution.py:33
  133.6 16.9 %collective-permute-start.9 = (bf16[32,32,256]{2,1,0:T(8,128)(2,1)S(1)}, bf16[32,32,256]{2,1,0:T(8,128)(2,1)S(1)}, u32[]{:S(2)}, u32[]{:S(2)}) collective-permute-start(bf16[32,32,256]{2,1,0:T(8,128)(2,1)S(1)} %slice.148.refs_2_), channel_id=1, source_target_pairs={{0,3},{1,0},{2,1},{3,2},{4,7},{5,4},{6,5},{7,6},{8,11},{9,8},{10,9... | collective-permute-start | bytes 1572872 | tf_op jit(solution)/shard_map/ppermute | solution.py:33
  133.7 18.3 %collective-permute-start.8 = (bf16[32,32,256]{2,1,0:T(8,128)(2,1)S(1)}, bf16[32,32,256]{2,1,0:T(8,128)(2,1)}, u32[]{:S(2)}, u32[]{:S(2)}) collective-permute-start(bf16[32,32,256]{2,1,0:T(8,128)(2,1)S(1)} %slice.148.refs_2_), channel_id=1, source_target_pairs={{0,1},{1,2},{2,3},{3,0},{4,5},{5,6},{6,7},{7,4},{8,9},{9,10},{10,1... | collective-permute-start | bytes 1572872 | tf_op jit(solution)/shard_map/ppermute | solution.py:33
  142.1 14.1 %collective-permute-start.19 = (bf16[16,32,256]{2,1,0:T(8,128)(2,1)}, bf16[16,32,256]{2,1,0:T(8,128)(2,1)}, u32[]{:S(2)}, u32[]{:S(2)}) collective-permute-start(bf16[16,32,256]{2,1,0:T(8,128)(2,1)} %slice.156), channel_id=1, source_target_pairs={{0,3},{1,0},{2,1},{3,2},{4,7},{5,4},{6,5},{7,6},{8,11},{9,8},{10,9... | collective-permute-start | bytes 786440 | tf_op jit(solution)/shard_map/ppermute | solution.py:33
  144.1 13.5 %collective-permute-start.18 = (bf16[16,32,256]{2,1,0:T(8,128)(2,1)}, bf16[16,32,256]{2,1,0:T(8,128)(2,1)}, u32[]{:S(2)}, u32[]{:S(2)}) collective-permute-start(bf16[16,32,256]{2,1,0:T(8,128)(2,1)} %slice.155), channel_id=1, source_target_pairs={{0,1},{1,2},{2,3},{3,0},{4,5},{5,6},{6,7},{7,4},{8,9},{9,10},{10,1... | collective-permute-start | bytes 786440 | tf_op jit(solution)/shard_map/ppermute | solution.py:33
  150.5 10.7 %collective-permute-start.11 = (bf16[16,32,256]{2,1,0:T(8,128)(2,1)S(1)}, bf16[16,32,256]{2,1,0:T(8,128)(2,1)S(1)}, u32[]{:S(2)}, u32[]{:S(2)}) collective-permute-start(bf16[16,32,256]{2,1,0:T(8,128)(2,1)S(1)} %slice.150), channel_id=1, source_target_pairs={{0,3},{1,0},{2,1},{3,2},{4,7},{5,4},{6,5},{7,6},{8,11},{9,8},{10,9... | collective-permute-start | bytes 786440 | tf_op jit(solution)/shard_map/ppermute | solution.py:33
  152.9 9.4 %collective-permute-start.10 = (bf16[16,32,256]{2,1,0:T(8,128)(2,1)S(1)}, bf16[16,32,256]{2,1,0:T(8,128)(2,1)S(1)}, u32[]{:S(2)}, u32[]{:S(2)}) collective-permute-start(bf16[16,32,256]{2,1,0:T(8,128)(2,1)S(1)} %slice.149), channel_id=1, source_target_pairs={{0,1},{1,2},{2,3},{3,0},{4,5},{5,6},{6,7},{7,4},{8,9},{9,10},{10,1... | collective-permute-start | bytes 786440 | tf_op jit(solution)/shard_map/ppermute | solution.py:33
  (19 other events, 167.4 us)

commit v3 on v2

--- a/solution.py
+++ b/solution.py
@@ -6,22 +6,17 @@
 from jax.sharding import PartitionSpec as P
 
 NMAT = 5
-ORDER = ""
-FRONT = "QD"
-COSTS = (16, 24, 48, 8)
-MERGED = False
 STAT_DECAY = 0.95
 EPSILON = 1e-06
 BF16 = jnp.bfloat16
 F32 = jnp.float32
-VMEM_LIMIT = 60 * 1024 * 1024
 EXTRA = 16
 SUM_SCALE = 1.0 / 16.0
 
 
-def params(steps=1):
+def params(steps=1, mib=60):
     semantics = ("arbitrary",) * steps if steps else None
-    return pltpu.CompilerParams(dimension_semantics=semantics, vmem_limit_bytes=VMEM_LIMIT)
+    return pltpu.CompilerParams(dimension_semantics=semantics, vmem_limit_bytes=mib * 1024 * 1024)
 
 
 def cost(flops, size):
@@ -77,7 +72,7 @@
             pltpu.SemaphoreType.DMA((parts,)),
         ],
         compiler_params=params(0),
-        cost_estimate=cost(0, COSTS[3] * count * rows * order),
+        cost_estimate=cost(0, 8 * count * rows * order),
         name="pick",
     )(by_owner)
 
@@ -90,10 +85,9 @@
         yield piece, pl.ds(first, piece.shape[0]), pl.ds(pl.multiple_of(column, width), width)
 
 
-def block_copies(me, which, pieces, block, sems):
+def block_copies(me, pieces, block, sems):
     if len(pieces) == 1:
-        source = pieces[0] if len(pieces[0].shape) == 3 else pieces[0].at[:, which]
-        return [pltpu.make_async_copy(source, block, sems.at[0])]
+        return [pltpu.make_async_copy(pieces[0], block, sems.at[0])]
     return [
         pltpu.make_async_copy(piece, block.at[chunks, :, columns], sems.at[i])
         for i, (piece, chunks, columns) in enumerate(piece_places(me, pieces))
@@ -130,7 +124,7 @@
 
     @pl.when(owned)
     def _():
-        first = block_copies(me, 1 if last else 0, pieces, block, sems)
+        first = block_copies(me, pieces, block, sems)
         first.append(pltpu.make_async_copy(left.at[slot], left_held, sems.at[8]))
         second = []
         for place, offset in enumerate((2, 1, 3, 0)):
@@ -212,13 +206,13 @@
             pltpu.VMEM((8, order // 2), F32),
             pltpu.SemaphoreType.DMA((13,)),
         ],
-        compiler_params=params(0),
-        cost_estimate=cost(COSTS[0] * order**3, 10 * order * order),
+        compiler_params=params(0, 50),
+        cost_estimate=cost(16 * order**3, 10 * order * order),
         name="roots",
     )(*operands)
 
 
-def stats_kernel(which, parts, info, *refs):
+def stats_kernel(parts, info, *refs):
     pieces, (stat_left, stat_right), refs = refs[:parts], refs[parts : parts + 2], refs[parts + 2 :]
     new_left, new_right, block, turned, sems = refs[-5:]
     step = pl.program_id(0)
@@ -230,7 +224,7 @@
 
     @pl.when(step == 0)
     def _():
-        copies = block_copies(info[2], which, pieces, block, sems)
+        copies = block_copies(info[2], pieces, block, sems)
         for copy in copies:
             copy.start()
         for copy in copies:
@@ -259,7 +253,7 @@
         in_specs += anywhere(2)
     chunk_rows = pieces[0].shape[-2]
     return pl.pallas_call(
-        lambda *refs: stats_kernel(b, len(pieces), *refs),
+        lambda *refs: stats_kernel(len(pieces), *refs),
         out_shape=[jax.ShapeDtypeStruct(stat_left.shape, F32)] * 2,
         grid=(steps,),
         in_specs=in_specs,
@@ -271,7 +265,7 @@
         ],
         input_output_aliases=aliases,
         compiler_params=params(),
-        cost_estimate=cost(COSTS[1] * rows * order**2, 2 * order * order + 16 * rows * order),
+        cost_estimate=cost(24 * rows * order**2, 2 * order * order + 16 * rows * order),
         name="stats",
     )(*operands)
 
@@ -319,83 +313,25 @@
             pltpu.SemaphoreType.DMA((2,)),
         ],
         input_output_aliases={} if earlier is None else {len(operands) - 1: 0},
-        compiler_params=params(0),
-        cost_estimate=cost(0, COSTS[2] * count * rows * width),
+        compiler_params=params(0, 50),
+        cost_estimate=cost(0, 48 * count * rows * width),
         name="scale",
     )(*operands)
 
 
-def scale_both_kernel(scales, place, *refs):
-    pieces = refs[:5]
-    out, held, ready, come, go = refs[-5:]
-    parts, _, size, _, width = held.shape
-    slots = out.shape[1]
-    rows = out.shape[2]
-    reads = []
-    for part in range(parts):
-        for at in range(4):
-            if at < 3:
-                source = pieces[at].at[pl.ds(part * size, size)]
-            else:
-                source = pieces[3 + part // (parts // 2)].at[pl.ds(part % (parts // 2) * size, size)]
-            reads.append(pltpu.make_async_copy(source, held.at[part, at], come.at[4 * part + at]))
-    for read in reads:
-        read.start()
-    writes = []
-    for part in range(parts):
-        for read in reads[4 * part : 4 * part + 4]:
-            read.wait()
-        for i in range(size):
-            for b in range(slots):
-                factor = scales[(part * size + i) * slots + b]
-                for at, (_, _, columns) in enumerate(piece_places(place[0], pieces[:4])):
-                    values = held[part, at, i, b * rows : (b + 1) * rows].astype(F32) * factor
-                    ready[part * size + i, b, :, columns] = values.astype(BF16)
-        span = pl.ds(part * size, size)
-        writes.append(pltpu.make_async_copy(ready.at[span], out.at[span], go.at[part]))
-        writes[-1].start()
-    for write in writes:
-        write.wait()
-
-
-def scale_both(scales, place, pieces, parts=4, slots=2):
-    count, rows, width = pieces[0].shape
-    shape = (count, slots, rows // slots, 4 * width)
-    return pl.pallas_call(
-        scale_both_kernel,
-        out_shape=jax.ShapeDtypeStruct(shape, BF16),
-        in_specs=[SMEM, SMEM] + anywhere(5),
-        out_specs=anywhere(1)[0],
-        scratch_shapes=[
-            pltpu.VMEM((parts, 4, count // parts, rows, width), BF16),
-            pltpu.VMEM(shape, BF16),
-            pltpu.SemaphoreType.DMA((4 * parts,)),
-            pltpu.SemaphoreType.DMA((parts,)),
-        ],
-        compiler_params=params(0),
-        cost_estimate=cost(0, COSTS[2] * count * rows * width),
-        name="scale",
-    )(scales, place, *pieces)
-
-
-def in_order(flag, first, *later):
-    if flag not in ORDER:
-        return (first, *later)
-    return lax.optimization_barrier((first, *later))
-
-
 def scatter_first(messages):
     return shift(messages[0], 1), shift(messages[1], -1)
 
 
-def scatter_second(messages, first, mine):
+def choose_second(messages, first, mine):
     _, _, keep_right, keep_left, own = messages
     half = own.shape[0] // 2
     from_left, from_right = first
-    return (
-        shift(jnp.where(mine, keep_right, from_left[half:]), 1),
-        shift(jnp.where(mine, keep_left, from_right[half:]), -1),
-    )
+    return jnp.where(mine, keep_right, from_left[half:]), jnp.where(mine, keep_left, from_right[half:])
+
+
+def scatter_second(chosen):
+    return shift(chosen[0], 1), shift(chosen[1], -1)
 
 
 def merge(messages, first, second, away):
@@ -431,22 +367,12 @@
     half = dp_count // 2
 
     by_owner = gradients.reshape(dp_count, local_total, shard_rows, order)
-    if FRONT == "QD":
-        my_columns = lax.dynamic_slice(
-            by_owner, (0, 0, 0, me * width), (dp_count, 1, shard_rows, width)
-        ).reshape(dp_count, shard_rows, width)
-        arrived, late = in_order("p", over_dp(my_columns), by_owner)
-        first_pieces = gather_first(arrived)
-        second_block = over_dp(pick_block(late, 1))
-        blocks = [gather_second(first_pieces), [second_block]]
-    elif FRONT == "DD":
-        picked = [pick_block(by_owner, b) for b in range(local_total)]
-        arrived = over_dp(picked[0])
-        arrived, picked[1] = in_order("p", arrived, picked[1])
-        blocks = [[arrived], [over_dp(picked[1])]]
-    else:
-        arrived = over_dp(gradients).reshape(dp_count, local_total, shard_rows, order)
-        blocks = [[arrived], [arrived]]
+    my_columns = lax.dynamic_slice(
+        by_owner, (0, 0, 0, me * width), (dp_count, 1, shard_rows, width)
+    ).reshape(dp_count, shard_rows, width)
+    first_pieces = gather_first(over_dp(my_columns))
+    second_block = over_dp(pick_block(by_owner, 1))
+    blocks = [gather_second(first_pieces), [second_block]]
 
     slot_ids = jnp.arange(slot_total, dtype=jnp.int32)
     live = slot_ids[None, None, :] < owner_counts[:, :, None]
@@ -467,49 +393,28 @@
     *sent, sums = apply_roots(infos[0], inv_left[0, 0], blocks[0], inv_right[0, 0])
     got = scatter_first(sent)
     sent_next = apply_roots(infos[1], inv_left[0, 0], blocks[1], inv_right[0, 0], sums)
-    sent_next, got = in_order("r", sent_next, got)
-    got_more = scatter_second(sent, got, away[0] == 0)
-    got_more, sent_next = in_order("s", got_more, sent_next)
+    got_more = scatter_second(choose_second(sent, got, away[0] == 0))
     got_next = scatter_first(sent_next)
-    got_more, sent_next = in_order("m", got_more, sent_next)
-    quarter = merge(sent, got, got_more, away[0])
-    quarter, stat_left, stat_right = in_order("a", quarter, stat_left, stat_right)
-    if not MERGED:
-        first = over_dp(quarter)
-        first, stat_left, stat_right = in_order("t", first, stat_left, stat_right)
-        first, got_next = in_order("x", first, got_next)
+    first = over_dp(merge(sent, got, got_more, away[0]))
     stats = update_stats(0, infos[0], blocks[0], stat_left, stat_right, None)
-    stats, got_next = in_order("b", stats, got_next)
 
     chunk = lax.broadcasted_iota(jnp.int32, sent_next[2].shape, 0)
     lane = lax.broadcasted_iota(jnp.int32, sent_next[2].shape, 2)
     of_before = (chunk == half) & (lane < width // 2)
-    got_next_more = scatter_second(sent_next, got_next, jnp.where(of_before, away[0], away[1]) == 0)
+    mine = jnp.where(of_before, away[0], away[1]) == 0
+    got_next_more = scatter_second(choose_second(sent_next, got_next, mine))
     far_off = jnp.where(of_before[half], away[0], away[1])
     sums = jnp.where(far_off == 1, got_next[1][2 * half], got_next_more[0][half])
     sums = jnp.where(far_off == 3, got_next[0][2 * half], sums)
     sums = jnp.where(far_off == 0, sent_next[4][2 * half], sums)
     sums = jnp.broadcast_to(sums[None, :EXTRA], (dp_count, EXTRA, width))
-    stats, got_next_more = in_order("c", stats, got_next_more)
     stats = update_stats(1, infos[1], blocks[1], stat_left, stat_right, stats)
-    quarter_next = merge(sent_next, got_next, got_next_more, away[1])
-    stats, quarter_next = in_order("u", stats, quarter_next)
-    if MERGED:
-        second = over_dp(jnp.concatenate([quarter, quarter_next, sums], axis=1))
-        stats, second = in_order("d", stats, second)
-        both = gather_first(second[:, : 2 * shard_rows])
-        far = gather_second(both)
-        sums = second[:, 2 * shard_rows : 2 * shard_rows + 6, :].astype(F32)
-    else:
-        pieces = gather_first(first)
-        pieces, quarter_next = in_order("y", pieces, quarter_next)
-        second = over_dp(jnp.concatenate([quarter_next, sums], axis=1))
-        pieces, second = in_order("v", pieces, second)
-        gathered = gather_second(pieces)
-        pieces_next = gather_first(second[:, :shard_rows])
-        gathered, pieces_next = in_order("w", gathered, pieces_next)
-        sums = second[:, shard_rows : shard_rows + 6, :].astype(F32)
-
+    quarter = merge(sent_next, got_next, got_next_more, away[1])
+    second = over_dp(jnp.concatenate([quarter, sums], axis=1))
+
+    gathered = gather_second(gather_first(first))
+    pieces_next = gather_first(second[:, :shard_rows])
+    sums = second[:, shard_rows : shard_rows + 6, :].astype(F32)
     sums = sums.reshape(dp_count, 2, 3, local_total, width // local_total)[..., 0]
     sums = jnp.sum(sums, axis=2) / SUM_SCALE
     sums = jnp.swapaxes(sums, 1, 2).reshape(block_total, 2)
@@ -521,12 +426,8 @@
     scales = jnp.sum(matrix_hot * graft[None, :], axis=1)
 
     place = me.reshape(1).astype(jnp.int32)
-    if MERGED:
-        update = scale_both(scales, place, far)
-    else:
-        update = scale_rows(0, local_total, scales, place, gathered, None)
-        update, pieces_next = in_order("z", update, pieces_next)
-        update = scale_rows(1, local_total, scales, place, gather_second(pieces_next), update)
+    update = scale_rows(0, local_total, scales, place, gathered, None)
+    update = scale_rows(1, local_total, scales, place, gather_second(pieces_next), update)
     return (update.reshape(block_total, shard_rows, order), *stats)
 
 

time: 167 us -> 163 us (0.976)
  Pallas kernels: 24.7 us -> 22.1 us
  local copies, waits for them, and re-layouts: 11.4 us -> 9 us
    ppermute x20, waiting for transfers between devices: 33 us -> 28.1 us  [shift(): lax.ppermute(x, 'replica', [(i, (i + step) % count) for i in range(count)])]
    all_to_all x3, waiting for transfers between devices: 15.7 us -> 19.1 us  [over_dp(): return lax.all_to_all(x, 'dp', split_axis=0, concat_axis=0, tiled=True)]
    slice x6, local copies, waits for them, and re-layouts: 3.5 us -> 1.5 us  [gather_second(): return [*pieces, shift(left[:half], 1), shift(right[half:], -1)]]
  transfers between devices with their start and end apart: 23 -> 23, of which waited for: 15 -> 13; matrix products, arithmetic and copies ran while one was open for 10% -> 10% of each run, Pallas kernels for 13% -> 12%
where the time goes in v3:
time: 163 us; the launch traced here: 161 us
  starting transfers between devices  50.5 us (31%)
  waiting for transfers between devices  47.1 us (29%)
  Pallas kernels  22.1 us (14%)
  blocking collectives  20 us (12%)
  other arithmetic  10.3 us (6%)
  local copies, waits for them, and re-layouts  9 us (6%)
  between operations  2.51 us (2%)
    ppermute x20, starting transfers between devices, shift(): lax.ppermute(x, 'replica', [(i, (i + step) % count) for i in range(count)])  37.7 us
    ppermute x20, waiting for transfers between devices, shift(): lax.ppermute(x, 'replica', [(i, (i + step) % count) for i in range(count)])  28.1 us
    all_to_all x1, blocking collectives, over_dp(): return lax.all_to_all(x, 'dp', split_axis=0, concat_axis=0, tiled=True)  20 us
    all_to_all x3, waiting for transfers between devices, over_dp(): return lax.all_to_all(x, 'dp', split_axis=0, concat_axis=0, tiled=True)  19.1 us
    all_to_all x3, starting transfers between devices, over_dp(): return lax.all_to_all(x, 'dp', split_axis=0, concat_axis=0, tiled=True)  12.8 us
    pallas_call x2, Pallas kernels, update_stats(): pl.pallas_call(lambda *refs: stats_kernel(len(pieces), *refs), out_shape=...  11 us
    pallas_call x2, Pallas kernels, scale_rows(): pl.pallas_call(lambda *refs: scale_kernel(which, slots, *refs), out_shape...  5.39 us
    pallas_call x2, Pallas kernels, apply_roots(): pl.pallas_call(lambda *refs: roots_kernel(len(pieces), before is not None...  3.27 us
  transfers between devices with their start and end apart: 23, of which 13 were waited for; matrix products, arithmetic and copies ran while one was open for 10% of the time, Pallas kernels for 12%

profile of v3, /device:TPU:0, one launch (start us, length us, event | category | flops | bytes accessed | tf_op | source)
XLA Modules:
  0.0 161.5 jit_solution(11123144625493872999)
XLA Ops:
  1.7 20.0 %all_to_all.20.refs_3_.refs_1_ = bf16[32,32,256]{2,1,0:T(8,128)(2,1)S(1)} all-to-all(bf16[32,32,256]{2,1,0:T(8,128)(2,1)S(1)} %dynamic-slice_bitcast_fusion), channel_id=1, replica_groups=mesh['dp'=32,'replica'=4] {'dp'}, dimensions={0} | all-to-all | bytes 1048576 | tf_op jit(solution)/shard_map/all_to_all | solution.py:32
  21.7 2.8 %collective-permute-start.1 = (bf16[32,32,256]{2,1,0:T(8,128)(2,1)S(1)}, bf16[32,32,256]{2,1,0:T(8,128)(2,1)S(1)}, u32[]{:S(2)}, u32[]{:S(2)}) collective-permute-start(bf16[32,32,256]{2,1,0:T(8,128)(2,1)S(1)} %all_to_all.20.refs_3_.refs_1_), channel_id=1, source_target_pairs={{0,3},{1,0},{2,1},{3,2},{4,7},{5,4},{6,5},{7,6},{8,11},{9,8},{10,9... | collective-permute-start | bytes 1572872 | tf_op jit(solution)/shard_map/ppermute | solution.py:28
  24.5 2.4 %pick.1 = bf16[32,32,1024]{2,1,0:T(8,128)(2,1)} custom-call(bf16[32,2,32,1024]{3,2,1,0:T(8,128)(2,1)} %bitcast.21), custom_call_target="tpu_custom_call" | custom-call | bytes 8388608 | tf_op jit(solution)/shard_map/pick/pallas_call | solution.py:64
  26.9 4.8 %all-to-all-start = ((bf16[32,32,1024]{2,1,0:T(8,128)(2,1)}), bf16[32,32,1024]{2,1,0:T(8,128)(2,1)}, u32[]{:S(2)}, u32[]{:S(2)}) async-start(bf16[32,32,1024]{2,1,0:T(8,128)(2,1)} %pick.1), calls=%async_computation | async-start | bytes 4194304 | tf_op jit(solution)/shard_map/all_to_all | solution.py:32
  31.8 4.1 %collective-permute-done.1.refs_5_.refs_3_ = bf16[32,32,256]{2,1,0:T(8,128)(2,1)S(1)} collective-permute-done((bf16[32,32,256]{2,1,0:T(8,128)(2,1)S(1)}, bf16[32,32,256]{2,1,0:T(8,128)(2,1)S(1)}, u32[]{:S(2)}, u32[]{:S(2)}) %collective-permute-start.1) | collective-permute-done | bytes 524320 | tf_op jit(solution)/shard_map/ppermute | solution.py:28
  36.7 3.8 %collective-permute-start.3 = (bf16[16,32,256]{2,1,0:T(8,128)(2,1)S(1)}, bf16[16,32,256]{2,1,0:T(8,128)(2,1)S(1)}, u32[]{:S(2)}, u32[]{:S(2)}) collective-permute-start(bf16[16,32,256]{2,1,0:T(8,128)(2,1)S(1)} %slice.130), channel_id=1, source_target_pairs={{0,3},{1,0},{2,1},{3,2},{4,7},{5,4},{6,5},{7,6},{8,11},{9,8},{10,9... | collective-permute-start | bytes 786440 | tf_op jit(solution)/shard_map/ppermute | solution.py:28
  45.7 3.2 %collective-permute-done.2.refs_6_.refs_4_ = bf16[16,32,256]{2,1,0:T(8,128)(2,1)S(1)} collective-permute-done((bf16[16,32,256]{2,1,0:T(8,128)(2,1)S(1)}, bf16[16,32,256]{2,1,0:T(8,128)(2,1)S(1)}, u32[]{:S(2)}, u32[]{:S(2)}) %collective-permute-start.2) | collective-permute-done | bytes 262176 | tf_op jit(solution)/shard_map/ppermute | solution.py:28
  50.6 7.1 %collective-permute-start.12 = (bf16[32,32,256]{2,1,0:T(8,128)(2,1)}, bf16[32,32,256]{2,1,0:T(8,128)(2,1)}, u32[]{:S(2)}, u32[]{:S(2)}) collective-permute-start(bf16[32,32,256]{2,1,0:T(8,128)(2,1)} %get-tuple-element.25), channel_id=1, source_target_pairs={{0,3},{1,0},{2,1},{3,2},{4,7},{5,4},{6,5},{7,6},{8,11},{9,8},{10,9... | collective-permute-start | bytes 1572872 | tf_op jit(solution)/shard_map/ppermute | solution.py:28
  57.7 3.9 %all-to-all-done.refs_3_.refs_1_ = bf16[32,32,1024]{2,1,0:T(8,128)(2,1)} async-done(((bf16[32,32,1024]{2,1,0:T(8,128)(2,1)}), bf16[32,32,1024]{2,1,0:T(8,128)(2,1)}, u32[]{:S(2)}, u32[]{:S(2)}) %all-to-all-start) | async-done | bytes 2097184 | tf_op jit(solution)/shard_map/all_to_all | solution.py:32
  63.3 10.4 %collective-permute-start.4 = (bf16[33,32,256]{2,1,0:T(8,128)(2,1)}, bf16[33,32,256]{2,1,0:T(8,128)(2,1)}, u32[]{:S(2)}, u32[]{:S(2)}) collective-permute-start(bf16[33,32,256]{2,1,0:T(8,128)(2,1)} %get-tuple-element.20), channel_id=1, source_target_pairs={{0,3},{1,0},{2,1},{3,2},{4,7},{5,4},{6,5},{7,6},{8,11},{9,8},{10,9... | collective-permute-start | bytes 1622024 | tf_op jit(solution)/shard_map/ppermute | solution.py:28
  74.9 3.3 %collective-permute-start.15 = (bf16[16,32,256]{2,1,0:T(8,128)(2,1)S(1)}, bf16[16,32,256]{2,1,0:T(8,128)(2,1)S(1)}, u32[]{:S(2)}, u32[]{:S(2)}) collective-permute-start(bf16[16,32,256]{2,1,0:T(8,128)(2,1)S(1)} %slice_select_fusion), channel_id=1, source_target_pairs={{0,3},{1,0},{2,1},{3,2},{4,7},{5,4},{6,5},{7,6},{8,11},{9,8},{10,9... | collective-permute-start | bytes 786440 | tf_op jit(solution)/shard_map/ppermute | solution.py:28
  81.2 7.6 %collective-permute-done.5 = bf16[33,32,256]{2,1,0:T(8,128)(2,1)} collective-permute-done((bf16[33,32,256]{2,1,0:T(8,128)(2,1)S(1)}, bf16[33,32,256]{2,1,0:T(8,128)(2,1)}, u32[]{:S(2)}, u32[]{:S(2)}) %collective-permute-start.5) | collective-permute-done | bytes 540704 | tf_op jit(solution)/shard_map/ppermute | solution.py:28
  90.1 2.1 %collective-permute-done.14 = bf16[16,32,256]{2,1,0:T(8,128)(2,1)S(1)} collective-permute-done((bf16[16,32,256]{2,1,0:T(8,128)(2,1)S(1)}, bf16[16,32,256]{2,1,0:T(8,128)(2,1)S(1)}, u32[]{:S(2)}, u32[]{:S(2)}) %collective-permute-start.14) | collective-permute-done | bytes 262176 | tf_op jit(solution)/shard_map/ppermute | solution.py:28
  95.9 3.9 %all-to-all-start.3 = ((bf16[32,32,256]{2,1,0:T(8,128)(2,1)}), bf16[32,32,256]{2,1,0:T(8,128)(2,1)S(1)}, u32[]{:S(2)}, u32[]{:S(2)}) async-start(bf16[32,32,256]{2,1,0:T(8,128)(2,1)} %pad_maximum_fusion.1), calls=%async_computation.3 | async-start | bytes 1048576 | tf_op jit(solution)/shard_map/all_to_all | solution.py:32
  103.4 8.2 %all-to-all-done.3.refs_2_ = bf16[32,32,256]{2,1,0:T(8,128)(2,1)S(1)} async-done(((bf16[32,32,256]{2,1,0:T(8,128)(2,1)}), bf16[32,32,256]{2,1,0:T(8,128)(2,1)S(1)}, u32[]{:S(2)}, u32[]{:S(2)}) %all-to-all-start.3) | async-done | bytes 524320 | tf_op jit(solution)/shard_map/all_to_all | solution.py:32
  111.6 4.1 %all-to-all-start.2 = ((bf16[32,48,256]{2,1,0:T(8,128)(2,1)}), bf16[32,48,256]{2,1,0:T(8,128)(2,1)S(1)}, u32[]{:S(2)}, u32[]{:S(2)}) async-start(bf16[32,48,256]{2,1,0:T(8,128)(2,1)} %pad_maximum_fusion), calls=%async_computation.2 | async-start | bytes 1572864 | tf_op jit(solution)/shard_map/all_to_all | solution.py:32
  115.7 5.5 %stats.2 = (f32[2,256,1024]{2,1,0:T(8,128)}, f32[2,256,1024]{2,1,0:T(8,128)}) custom-call(s32[4]{0:T(128)} %copy-done.3, bf16[32,32,256]{2,1,0:T(8,128)(2,1)} %copy-done, bf16[32,32,256]{2,1,0:T(8,128)(2,1)} %copy-done.1, bf16[32,32,256]{2,1,0:T(8,128)(2,1)} %copy-done.8, bf16[16,32,256]{2,1,0:T(8,128)(2,1)} %copy-done.5, bf16[16,32,256]{2,1,0:T(8,128)(2,1)} %copy-done.4, ...), custom_call_target="tpu_custom_call" | custom-call | flops 6442450944 | bytes 6291456 | tf_op jit(solution)/shard_map/stats/pallas_call | solution.py:255
  121.3 2.0 %collective-permute-start.16 = (bf16[32,32,256]{2,1,0:T(8,128)(2,1)S(1)}, bf16[32,32,256]{2,1,0:T(8,128)(2,1)S(1)}, u32[]{:S(2)}, u32[]{:S(2)}) collective-permute-start(bf16[32,32,256]{2,1,0:T(8,128)(2,1)S(1)} %all-to-all-done.3.refs_2_), channel_id=1, source_target_pairs={{0,1},{1,2},{2,3},{3,0},{4,5},{5,6},{6,7},{7,4},{8,9},{9,10},{10,1... | collective-permute-start | bytes 1572872 | tf_op jit(solution)/shard_map/ppermute | solution.py:28
  123.3 7.0 %all-to-all-done.2 = bf16[32,48,256]{2,1,0:T(8,128)(2,1)S(1)} async-done(((bf16[32,48,256]{2,1,0:T(8,128)(2,1)}), bf16[32,48,256]{2,1,0:T(8,128)(2,1)S(1)}, u32[]{:S(2)}, u32[]{:S(2)}) %all-to-all-start.2) | async-done | bytes 786464 | tf_op jit(solution)/shard_map/all_to_all | solution.py:32
  133.3 5.6 %stats.3 = (f32[2,256,1024]{2,1,0:T(8,128)}, f32[2,256,1024]{2,1,0:T(8,128)}) custom-call(s32[4]{0:T(128)} %copy-done.2, bf16[32,32,1024]{2,1,0:T(8,128)(2,1)} %all-to-all-done.refs_3_.refs_1_, f32[2,256,1024]{2,1,0:T(8,128)} %refs_2_.1, f32[2,256,1024]{2,1,0:T(8,128)} %refs_3_.1, ...), custom_call_target="tpu_custom_call", output_to_operand_aliasing={{0}: (4, {}), {1}: (5, {})} | custom-call | flops 6442450944 | bytes 6291456 | tf_op jit(solution)/shard_map/stats/pallas_call | solution.py:255
  144.2 3.0 %collective-permute-done.9.refs_4_ = bf16[32,32,256]{2,1,0:T(8,128)(2,1)S(1)} collective-permute-done((bf16[32,32,256]{2,1,0:T(8,128)(2,1)S(1)}, bf16[32,32,256]{2,1,0:T(8,128)(2,1)S(1)}, u32[]{:S(2)}, u32[]{:S(2)}) %collective-permute-start.9) | collective-permute-done | bytes 524320 | tf_op jit(solution)/shard_map/ppermute | solution.py:28
  149.9 3.0 %collective-permute-done.19.refs_6_ = bf16[16,32,256]{2,1,0:T(8,128)(2,1)S(1)} collective-permute-done((bf16[16,32,256]{2,1,0:T(8,128)(2,1)}, bf16[16,32,256]{2,1,0:T(8,128)(2,1)S(1)}, u32[]{:S(2)}, u32[]{:S(2)}) %collective-permute-start.19) | collective-permute-done | bytes 262176 | tf_op jit(solution)/shard_map/ppermute | solution.py:28
  154.3 3.1 %scale.2.refs_7_ = bf16[32,2,32,1024]{3,2,1,0:T(8,128)(2,1)} custom-call(f32[64]{0:T(128)S(1)} %select_reduce_fusion.refs_0_, s32[1]{0:T(128)} %bitcast.2.refs_1_, bf16[32,32,256]{2,1,0:T(8,128)(2,1)S(1)} %all-to-all-done.3.refs_2_, bf16[32,32,256]{2,1,0:T(8,128)(2,1)S(1)} %collective-permute-done.16.refs_3_, ...), custom_call_target="tpu_custom_call" | custom-call | bytes 12582912 | tf_op jit(solution)/shard_map/scale/pallas_call | solution.py:304
  159.0 2.3 %scale.3 = bf16[32,2,32,1024]{3,2,1,0:T(8,128)(2,1)} custom-call(f32[64]{0:T(128)S(1)} %select_reduce_fusion.refs_0_, s32[1]{0:T(128)} %bitcast.2.refs_1_, bf16[32,32,256]{2,1,0:T(8,128)(2,1)S(1)} %slice.148.refs_2_, bf16[32,32,256]{2,1,0:T(8,128)(2,1)S(1)} %collective-permute-done.8.refs_3_, ...), custom_call_target="tpu_custom_call", output_to_operand_aliasing={{}: (7, {})} | custom-call | bytes 12582912 | tf_op jit(solution)/shard_map/scale/pallas_call | solution.py:304
  (98 shorter events, 35.9 us)
Async XLA Ops:
  21.7 27.2 %copy-start = (bf16[32,32,256]{2,1,0:T(8,128)(2,1)}, bf16[32,32,256]{2,1,0:T(8,128)(2,1)S(1)}, u32[]{:S(2)}) copy-start(bf16[32,32,256]{2,1,0:T(8,128)(2,1)S(1)} %all_to_all.20.refs_3_.refs_1_) | copy-start | bytes 1572868
  21.7 14.2 %collective-permute-start.1 = (bf16[32,32,256]{2,1,0:T(8,128)(2,1)S(1)}, bf16[32,32,256]{2,1,0:T(8,128)(2,1)S(1)}, u32[]{:S(2)}, u32[]{:S(2)}) collective-permute-start(bf16[32,32,256]{2,1,0:T(8,128)(2,1)S(1)} %all_to_all.20.refs_3_.refs_1_), channel_id=1, source_target_pairs={{0,3},{1,0},{2,1},{3,2},{4,7},{5,4},{6,5},{7,6},{8,11},{9,8},{10,9... | collective-permute-start | bytes 1572872 | tf_op jit(solution)/shard_map/ppermute | solution.py:28
  24.5 16.0 %collective-permute-start = (bf16[32,32,256]{2,1,0:T(8,128)(2,1)S(1)}, bf16[32,32,256]{2,1,0:T(8,128)(2,1)S(1)}, u32[]{:S(2)}, u32[]{:S(2)}) collective-permute-start(bf16[32,32,256]{2,1,0:T(8,128)(2,1)S(1)} %all_to_all.20.refs_3_.refs_1_), channel_id=1, source_target_pairs={{0,1},{1,2},{2,3},{3,0},{4,5},{5,6},{6,7},{7,4},{8,9},{9,10},{10,1... | collective-permute-start | bytes 1572872 | tf_op jit(solution)/shard_map/ppermute | solution.py:28
  26.9 34.7 %all-to-all-start = ((bf16[32,32,1024]{2,1,0:T(8,128)(2,1)}), bf16[32,32,1024]{2,1,0:T(8,128)(2,1)}, u32[]{:S(2)}, u32[]{:S(2)}) async-start(bf16[32,32,1024]{2,1,0:T(8,128)(2,1)} %pick.1), calls=%async_computation | async-start | bytes 4194304 | tf_op jit(solution)/shard_map/all_to_all | solution.py:32
  36.7 9.0 %collective-permute-start.3 = (bf16[16,32,256]{2,1,0:T(8,128)(2,1)S(1)}, bf16[16,32,256]{2,1,0:T(8,128)(2,1)S(1)}, u32[]{:S(2)}, u32[]{:S(2)}) collective-permute-start(bf16[16,32,256]{2,1,0:T(8,128)(2,1)S(1)} %slice.130), channel_id=1, source_target_pairs={{0,3},{1,0},{2,1},{3,2},{4,7},{5,4},{6,5},{7,6},{8,11},{9,8},{10,9... | collective-permute-start | bytes 786440 | tf_op jit(solution)/shard_map/ppermute | solution.py:28
  40.5 8.4 %collective-permute-start.2 = (bf16[16,32,256]{2,1,0:T(8,128)(2,1)S(1)}, bf16[16,32,256]{2,1,0:T(8,128)(2,1)S(1)}, u32[]{:S(2)}, u32[]{:S(2)}) collective-permute-start(bf16[16,32,256]{2,1,0:T(8,128)(2,1)S(1)} %slice.129), channel_id=1, source_target_pairs={{0,1},{1,2},{2,3},{3,0},{4,5},{5,6},{6,7},{7,4},{8,9},{9,10},{10,1... | collective-permute-start | bytes 786440 | tf_op jit(solution)/shard_map/ppermute | solution.py:28
  50.6 23.2 %collective-permute-start.12 = (bf16[32,32,256]{2,1,0:T(8,128)(2,1)}, bf16[32,32,256]{2,1,0:T(8,128)(2,1)}, u32[]{:S(2)}, u32[]{:S(2)}) collective-permute-start(bf16[32,32,256]{2,1,0:T(8,128)(2,1)} %get-tuple-element.25), channel_id=1, source_target_pairs={{0,3},{1,0},{2,1},{3,2},{4,7},{5,4},{6,5},{7,6},{8,11},{9,8},{10,9... | collective-permute-start | bytes 1572872 | tf_op jit(solution)/shard_map/ppermute | solution.py:28
  57.7 20.4 %collective-permute-start.13 = (bf16[32,32,256]{2,1,0:T(8,128)(2,1)}, bf16[32,32,256]{2,1,0:T(8,128)(2,1)}, u32[]{:S(2)}, u32[]{:S(2)}) collective-permute-start(bf16[32,32,256]{2,1,0:T(8,128)(2,1)} %get-tuple-element.27), channel_id=1, source_target_pairs={{0,1},{1,2},{2,3},{3,0},{4,5},{5,6},{6,7},{7,4},{8,9},{9,10},{10,1... | collective-permute-start | bytes 1572872 | tf_op jit(solution)/shard_map/ppermute | solution.py:28
  63.3 17.9 %collective-permute-start.4 = (bf16[33,32,256]{2,1,0:T(8,128)(2,1)}, bf16[33,32,256]{2,1,0:T(8,128)(2,1)}, u32[]{:S(2)}, u32[]{:S(2)}) collective-permute-start(bf16[33,32,256]{2,1,0:T(8,128)(2,1)} %get-tuple-element.20), channel_id=1, source_target_pairs={{0,3},{1,0},{2,1},{3,2},{4,7},{5,4},{6,5},{7,6},{8,11},{9,8},{10,9... | collective-permute-start | bytes 1622024 | tf_op jit(solution)/shard_map/ppermute | solution.py:28
  73.7 15.1 %collective-permute-start.5 = (bf16[33,32,256]{2,1,0:T(8,128)(2,1)S(1)}, bf16[33,32,256]{2,1,0:T(8,128)(2,1)}, u32[]{:S(2)}, u32[]{:S(2)}) collective-permute-start(bf16[33,32,256]{2,1,0:T(8,128)(2,1)S(1)} %get-tuple-element.22), channel_id=1, source_target_pairs={{0,1},{1,2},{2,3},{3,0},{4,5},{5,6},{6,7},{7,4},{8,9},{9,10},{10,1... | collective-permute-start | bytes 1622024 | tf_op jit(solution)/shard_map/ppermute | solution.py:28
  74.9 15.2 %collective-permute-start.15 = (bf16[16,32,256]{2,1,0:T(8,128)(2,1)S(1)}, bf16[16,32,256]{2,1,0:T(8,128)(2,1)S(1)}, u32[]{:S(2)}, u32[]{:S(2)}) collective-permute-start(bf16[16,32,256]{2,1,0:T(8,128)(2,1)S(1)} %slice_select_fusion), channel_id=1, source_target_pairs={{0,3},{1,0},{2,1},{3,2},{4,7},{5,4},{6,5},{7,6},{8,11},{9,8},{10,9... | collective-permute-start | bytes 786440 | tf_op jit(solution)/shard_map/ppermute | solution.py:28
  79.1 13.0 %collective-permute-start.14 = (bf16[16,32,256]{2,1,0:T(8,128)(2,1)S(1)}, bf16[16,32,256]{2,1,0:T(8,128)(2,1)S(1)}, u32[]{:S(2)}, u32[]{:S(2)}) collective-permute-start(bf16[16,32,256]{2,1,0:T(8,128)(2,1)S(1)} %slice_select_fusion.2), channel_id=1, source_target_pairs={{0,1},{1,2},{2,3},{3,0},{4,5},{5,6},{6,7},{7,4},{8,9},{9,10},{10,1... | collective-permute-start | bytes 786440 | tf_op jit(solution)/shard_map/ppermute | solution.py:28
  90.0 11.3 %collective-permute-start.6 = (bf16[17,32,256]{2,1,0:T(8,128)(2,1)S(1)}, bf16[17,32,256]{2,1,0:T(8,128)(2,1)S(1)}, u32[]{:S(2)}, u32[]{:S(2)}) collective-permute-start(bf16[17,32,256]{2,1,0:T(8,128)(2,1)S(1)} %get-tuple-element.44), channel_id=1, source_target_pairs={{0,1},{1,2},{2,3},{3,0},{4,5},{5,6},{6,7},{7,4},{8,9},{9,10},{10,1... | collective-permute-start | bytes 835592 | tf_op jit(solution)/shard_map/ppermute | solution.py:28
  93.3 8.0 %collective-permute-start.7 = (bf16[17,32,256]{2,1,0:T(8,128)(2,1)S(1)}, bf16[17,32,256]{2,1,0:T(8,128)(2,1)S(1)}, u32[]{:S(2)}, u32[]{:S(2)}) collective-permute-start(bf16[17,32,256]{2,1,0:T(8,128)(2,1)S(1)} %get-tuple-element.43), channel_id=1, source_target_pairs={{0,3},{1,0},{2,1},{3,2},{4,7},{5,4},{6,5},{7,6},{8,11},{9,8},{10,9... | collective-permute-start | bytes 835592 | tf_op jit(solution)/shard_map/ppermute | solution.py:28
  95.9 15.7 %all-to-all-start.3 = ((bf16[32,32,256]{2,1,0:T(8,128)(2,1)}), bf16[32,32,256]{2,1,0:T(8,128)(2,1)S(1)}, u32[]{:S(2)}, u32[]{:S(2)}) async-start(bf16[32,32,256]{2,1,0:T(8,128)(2,1)} %pad_maximum_fusion.1), calls=%async_computation.3 | async-start | bytes 1048576 | tf_op jit(solution)/shard_map/all_to_all | solution.py:32
  111.6 18.7 %all-to-all-start.2 = ((bf16[32,48,256]{2,1,0:T(8,128)(2,1)}), bf16[32,48,256]{2,1,0:T(8,128)(2,1)S(1)}, u32[]{:S(2)}, u32[]{:S(2)}) async-start(bf16[32,48,256]{2,1,0:T(8,128)(2,1)} %pad_maximum_fusion), calls=%async_computation.2 | async-start | bytes 1572864 | tf_op jit(solution)/shard_map/all_to_all | solution.py:32
  121.2 17.7 %collective-permute-start.17 = (bf16[32,32,256]{2,1,0:T(8,128)(2,1)S(1)}, bf16[32,32,256]{2,1,0:T(8,128)(2,1)S(1)}, u32[]{:S(2)}, u32[]{:S(2)}) collective-permute-start(bf16[32,32,256]{2,1,0:T(8,128)(2,1)S(1)} %all-to-all-done.3.refs_2_), channel_id=1, source_target_pairs={{0,3},{1,0},{2,1},{3,2},{4,7},{5,4},{6,5},{7,6},{8,11},{9,8},{10,9... | collective-permute-start | bytes 1572872 | tf_op jit(solution)/shard_map/ppermute | solution.py:28
  121.3 19.6 %collective-permute-start.16 = (bf16[32,32,256]{2,1,0:T(8,128)(2,1)S(1)}, bf16[32,32,256]{2,1,0:T(8,128)(2,1)S(1)}, u32[]{:S(2)}, u32[]{:S(2)}) collective-permute-start(bf16[32,32,256]{2,1,0:T(8,128)(2,1)S(1)} %all-to-all-done.3.refs_2_), channel_id=1, source_target_pairs={{0,1},{1,2},{2,3},{3,0},{4,5},{5,6},{6,7},{7,4},{8,9},{9,10},{10,1... | collective-permute-start | bytes 1572872 | tf_op jit(solution)/shard_map/ppermute | solution.py:28
  131.2 16.1 %collective-permute-start.9 = (bf16[32,32,256]{2,1,0:T(8,128)(2,1)S(1)}, bf16[32,32,256]{2,1,0:T(8,128)(2,1)S(1)}, u32[]{:S(2)}, u32[]{:S(2)}) collective-permute-start(bf16[32,32,256]{2,1,0:T(8,128)(2,1)S(1)} %slice.148.refs_2_), channel_id=1, source_target_pairs={{0,3},{1,0},{2,1},{3,2},{4,7},{5,4},{6,5},{7,6},{8,11},{9,8},{10,9... | collective-permute-start | bytes 1572872 | tf_op jit(solution)/shard_map/ppermute | solution.py:28
  131.3 17.3 %collective-permute-start.8 = (bf16[32,32,256]{2,1,0:T(8,128)(2,1)S(1)}, bf16[32,32,256]{2,1,0:T(8,128)(2,1)S(1)}, u32[]{:S(2)}, u32[]{:S(2)}) collective-permute-start(bf16[32,32,256]{2,1,0:T(8,128)(2,1)S(1)} %slice.148.refs_2_), channel_id=1, source_target_pairs={{0,1},{1,2},{2,3},{3,0},{4,5},{5,6},{6,7},{7,4},{8,9},{9,10},{10,1... | collective-permute-start | bytes 1572872 | tf_op jit(solution)/shard_map/ppermute | solution.py:28
  139.6 13.3 %collective-permute-start.19 = (bf16[16,32,256]{2,1,0:T(8,128)(2,1)}, bf16[16,32,256]{2,1,0:T(8,128)(2,1)S(1)}, u32[]{:S(2)}, u32[]{:S(2)}) collective-permute-start(bf16[16,32,256]{2,1,0:T(8,128)(2,1)} %slice.156), channel_id=1, source_target_pairs={{0,3},{1,0},{2,1},{3,2},{4,7},{5,4},{6,5},{7,6},{8,11},{9,8},{10,9... | collective-permute-start | bytes 786440 | tf_op jit(solution)/shard_map/ppermute | solution.py:28
  141.6 12.7 %collective-permute-start.18 = (bf16[16,32,256]{2,1,0:T(8,128)(2,1)}, bf16[16,32,256]{2,1,0:T(8,128)(2,1)}, u32[]{:S(2)}, u32[]{:S(2)}) collective-permute-start(bf16[16,32,256]{2,1,0:T(8,128)(2,1)} %slice.155), channel_id=1, source_target_pairs={{0,1},{1,2},{2,3},{3,0},{4,5},{5,6},{6,7},{7,4},{8,9},{9,10},{10,1... | collective-permute-start | bytes 786440 | tf_op jit(solution)/shard_map/ppermute | solution.py:28
  147.3 10.4 %collective-permute-start.11 = (bf16[16,32,256]{2,1,0:T(8,128)(2,1)S(1)}, bf16[16,32,256]{2,1,0:T(8,128)(2,1)S(1)}, u32[]{:S(2)}, u32[]{:S(2)}) collective-permute-start(bf16[16,32,256]{2,1,0:T(8,128)(2,1)S(1)} %slice.150), channel_id=1, source_target_pairs={{0,3},{1,0},{2,1},{3,2},{4,7},{5,4},{6,5},{7,6},{8,11},{9,8},{10,9... | collective-permute-start | bytes 786440 | tf_op jit(solution)/shard_map/ppermute | solution.py:28
  148.6 10.4 %collective-permute-start.10 = (bf16[16,32,256]{2,1,0:T(8,128)(2,1)S(1)}, bf16[16,32,256]{2,1,0:T(8,128)(2,1)S(1)}, u32[]{:S(2)}, u32[]{:S(2)}) collective-permute-start(bf16[16,32,256]{2,1,0:T(8,128)(2,1)S(1)} %slice.149), channel_id=1, source_target_pairs={{0,1},{1,2},{2,3},{3,0},{4,5},{5,6},{6,7},{7,4},{8,9},{9,10},{10,1... | collective-permute-start | bytes 786440 | tf_op jit(solution)/shard_map/ppermute | solution.py:28
  (13 other events, 99.5 us)

commit v4 on v3

--- a/solution.py
+++ b/solution.py
@@ -319,6 +319,10 @@
     )(*operands)
 
 
+def in_order(first, *later):
+    return lax.optimization_barrier((first, *later))
+
+
 def scatter_first(messages):
     return shift(messages[0], 1), shift(messages[1], -1)
 
@@ -393,10 +397,10 @@
     *sent, sums = apply_roots(infos[0], inv_left[0, 0], blocks[0], inv_right[0, 0])
     got = scatter_first(sent)
     sent_next = apply_roots(infos[1], inv_left[0, 0], blocks[1], inv_right[0, 0], sums)
+    sent_next, got = in_order(sent_next, got)
     got_more = scatter_second(choose_second(sent, got, away[0] == 0))
     got_next = scatter_first(sent_next)
     first = over_dp(merge(sent, got, got_more, away[0]))
-    stats = update_stats(0, infos[0], blocks[0], stat_left, stat_right, None)
 
     chunk = lax.broadcasted_iota(jnp.int32, sent_next[2].shape, 0)
     lane = lax.broadcasted_iota(jnp.int32, sent_next[2].shape, 2)
@@ -408,11 +412,14 @@
     sums = jnp.where(far_off == 3, got_next[0][2 * half], sums)
     sums = jnp.where(far_off == 0, sent_next[4][2 * half], sums)
     sums = jnp.broadcast_to(sums[None, :EXTRA], (dp_count, EXTRA, width))
-    stats = update_stats(1, infos[1], blocks[1], stat_left, stat_right, stats)
     quarter = merge(sent_next, got_next, got_next_more, away[1])
     second = over_dp(jnp.concatenate([quarter, sums], axis=1))
 
-    gathered = gather_second(gather_first(first))
+    pieces = gather_first(first)
+    pieces, stat_left, stat_right = in_order(pieces, stat_left, stat_right)
+    stats = update_stats(0, infos[0], blocks[0], stat_left, stat_right, None)
+    stats = update_stats(1, infos[1], blocks[1], stat_left, stat_right, stats)
+    gathered = gather_second(pieces)
     pieces_next = gather_first(second[:, :shard_rows])
     sums = second[:, shard_rows : shard_rows + 6, :].astype(F32)
     sums = sums.reshape(dp_count, 2, 3, local_total, width // local_total)[..., 0]

time: 163 us -> 155 us (0.951)
  waiting for transfers between devices: 47.1 us -> 33.8 us
  starting transfers between devices: 50.5 us -> 55.3 us
    ppermute x20, waiting for transfers between devices: 28.1 us -> 20.8 us  [shift(): lax.ppermute(x, 'replica', [(i, (i + step) % count) for i in range(count)])]
    all_to_all x3, waiting for transfers between devices: 19.1 us -> 13 us  [over_dp(): return lax.all_to_all(x, 'dp', split_axis=0, concat_axis=0, tiled=True)]
    all_to_all x3, starting transfers between devices: 12.8 us -> 17.8 us  [over_dp(): return lax.all_to_all(x, 'dp', split_axis=0, concat_axis=0, tiled=True)]
    unnamed x24 -> x22, local copies, waits for them, and re-layouts: 1.71 us -> 0.05 us
  transfers between devices with their start and end apart: 23 -> 23, of which waited for: 13 -> 10; matrix products, arithmetic and copies ran while one was open for 10% -> 11% of each run, Pallas kernels for 12% -> 13%
where the time goes in v4:
time: 155 us; the launch traced here: 154 us
  starting transfers between devices  55.3 us (36%)
  waiting for transfers between devices  33.8 us (22%)
  Pallas kernels  21.7 us (14%)
  blocking collectives  20 us (13%)
  local copies, waits for them, and re-layouts  10.3 us (7%)
  other arithmetic  10.2 us (7%)
  between operations  2.52 us (2%)
    ppermute x20, starting transfers between devices, shift(): lax.ppermute(x, 'replica', [(i, (i + step) % count) for i in range(count)])  37.5 us
    ppermute x20, waiting for transfers between devices, shift(): lax.ppermute(x, 'replica', [(i, (i + step) % count) for i in range(count)])  20.8 us
    all_to_all x1, blocking collectives, over_dp(): return lax.all_to_all(x, 'dp', split_axis=0, concat_axis=0, tiled=True)  20 us
    all_to_all x3, starting transfers between devices, over_dp(): return lax.all_to_all(x, 'dp', split_axis=0, concat_axis=0, tiled=True)  17.8 us
    all_to_all x3, waiting for transfers between devices, over_dp(): return lax.all_to_all(x, 'dp', split_axis=0, concat_axis=0, tiled=True)  13 us
    pallas_call x2, Pallas kernels, update_stats(): pl.pallas_call(lambda *refs: stats_kernel(len(pieces), *refs), out_shape=...  11 us
    pallas_call x2, Pallas kernels, scale_rows(): pl.pallas_call(lambda *refs: scale_kernel(which, slots, *refs), out_shape...  5.12 us
    pallas_call x2, Pallas kernels, apply_roots(): pl.pallas_call(lambda *refs: roots_kernel(len(pieces), before is not None...  3.28 us
  transfers between devices with their start and end apart: 23, of which 10 were waited for; matrix products, arithmetic and copies ran while one was open for 11% of the time, Pallas kernels for 13%

profile of v4, /device:TPU:0, one launch (start us, length us, event | category | flops | bytes accessed | tf_op | source)
XLA Modules:
  0.0 153.8 jit_solution(307196119694996298)
XLA Ops:
  1.7 20.0 %all_to_all.20.refs_3_.refs_1_ = bf16[32,32,256]{2,1,0:T(8,128)(2,1)S(1)} all-to-all(bf16[32,32,256]{2,1,0:T(8,128)(2,1)S(1)} %dynamic-slice_bitcast_fusion), channel_id=1, replica_groups=mesh['dp'=32,'replica'=4] {'dp'}, dimensions={0} | all-to-all | bytes 1048576 | tf_op jit(solution)/shard_map/all_to_all | solution.py:32
  25.0 2.4 %pick.1 = bf16[32,32,1024]{2,1,0:T(8,128)(2,1)} custom-call(bf16[32,2,32,1024]{3,2,1,0:T(8,128)(2,1)} %bitcast.21), custom_call_target="tpu_custom_call" | custom-call | bytes 8388608 | tf_op jit(solution)/shard_map/pick/pallas_call | solution.py:64
  27.4 4.8 %all-to-all-start = ((bf16[32,32,1024]{2,1,0:T(8,128)(2,1)}), bf16[32,32,1024]{2,1,0:T(8,128)(2,1)}, u32[]{:S(2)}, u32[]{:S(2)}) async-start(bf16[32,32,1024]{2,1,0:T(8,128)(2,1)} %pick.1), calls=%async_computation | async-start | bytes 4194304 | tf_op jit(solution)/shard_map/all_to_all | solution.py:32
  32.2 4.6 %collective-permute-done.refs_4_.refs_2_ = bf16[32,32,256]{2,1,0:T(8,128)(2,1)S(1)} collective-permute-done((bf16[32,32,256]{2,1,0:T(8,128)(2,1)S(1)}, bf16[32,32,256]{2,1,0:T(8,128)(2,1)S(1)}, u32[]{:S(2)}, u32[]{:S(2)}) %collective-permute-start) | collective-permute-done | bytes 524320 | tf_op jit(solution)/shard_map/ppermute | solution.py:28
  37.2 3.0 %collective-permute-start.3 = (bf16[16,32,256]{2,1,0:T(8,128)(2,1)S(1)}, bf16[16,32,256]{2,1,0:T(8,128)(2,1)S(1)}, u32[]{:S(2)}, u32[]{:S(2)}) collective-permute-start(bf16[16,32,256]{2,1,0:T(8,128)(2,1)S(1)} %slice.130), channel_id=1, source_target_pairs={{0,3},{1,0},{2,1},{3,2},{4,7},{5,4},{6,5},{7,6},{8,11},{9,8},{10,9... | collective-permute-start | bytes 786440 | tf_op jit(solution)/shard_map/ppermute | solution.py:28
  47.3 7.3 %collective-permute-start.4 = (bf16[32,32,256]{2,1,0:T(8,128)(2,1)}, bf16[32,32,256]{2,1,0:T(8,128)(2,1)}, u32[]{:S(2)}, u32[]{:S(2)}) collective-permute-start(bf16[32,32,256]{2,1,0:T(8,128)(2,1)} %get-tuple-element.36), channel_id=1, source_target_pairs={{0,1},{1,2},{2,3},{3,0},{4,5},{5,6},{6,7},{7,4},{8,9},{9,10},{10,1... | collective-permute-start | bytes 1572872 | tf_op jit(solution)/shard_map/ppermute | solution.py:28
  54.7 7.5 %all-to-all-done.refs_3_.refs_1_ = bf16[32,32,1024]{2,1,0:T(8,128)(2,1)} async-done(((bf16[32,32,1024]{2,1,0:T(8,128)(2,1)}), bf16[32,32,1024]{2,1,0:T(8,128)(2,1)}, u32[]{:S(2)}, u32[]{:S(2)}) %all-to-all-start) | async-done | bytes 2097184 | tf_op jit(solution)/shard_map/all_to_all | solution.py:32
  63.8 2.4 %collective-permute-done.5 = bf16[32,32,256]{2,1,0:T(8,128)(2,1)} collective-permute-done((bf16[32,32,256]{2,1,0:T(8,128)(2,1)}, bf16[32,32,256]{2,1,0:T(8,128)(2,1)}, u32[]{:S(2)}, u32[]{:S(2)}) %collective-permute-start.5) | collective-permute-done | bytes 524320 | tf_op jit(solution)/shard_map/ppermute | solution.py:28
  68.9 5.0 %collective-permute-start.14 = (bf16[16,32,256]{2,1,0:T(8,128)(2,1)S(1)}, bf16[16,32,256]{2,1,0:T(8,128)(2,1)S(1)}, u32[]{:S(2)}, u32[]{:S(2)}) collective-permute-start(bf16[16,32,256]{2,1,0:T(8,128)(2,1)S(1)} %slice_select_fusion.3), channel_id=1, source_target_pairs={{0,1},{1,2},{2,3},{3,0},{4,5},{5,6},{6,7},{7,4},{8,9},{9,10},{10,1... | collective-permute-start | bytes 786440 | tf_op jit(solution)/shard_map/ppermute | solution.py:28
  76.0 4.3 %collective-permute-done.15 = bf16[16,32,256]{2,1,0:T(8,128)(2,1)S(1)} collective-permute-done((bf16[16,32,256]{2,1,0:T(8,128)(2,1)}, bf16[16,32,256]{2,1,0:T(8,128)(2,1)S(1)}, u32[]{:S(2)}, u32[]{:S(2)}) %collective-permute-start.15) | collective-permute-done | bytes 262176 | tf_op jit(solution)/shard_map/ppermute | solution.py:28
  82.5 8.4 %all-to-all-start.3 = ((bf16[32,32,256]{2,1,0:T(8,128)(2,1)}), bf16[32,32,256]{2,1,0:T(8,128)(2,1)S(1)}, u32[]{:S(2)}, u32[]{:S(2)}) async-start(bf16[32,32,256]{2,1,0:T(8,128)(2,1)} %pad_maximum_fusion.1), calls=%async_computation.3 | async-start | bytes 1048576 | tf_op jit(solution)/shard_map/all_to_all | solution.py:32
  92.3 3.2 %collective-permute-start.9 = (bf16[17,32,256]{2,1,0:T(8,128)(2,1)S(1)}, bf16[17,32,256]{2,1,0:T(8,128)(2,1)}, u32[]{:S(2)}, u32[]{:S(2)}) collective-permute-start(bf16[17,32,256]{2,1,0:T(8,128)(2,1)S(1)} %get-tuple-element.67), channel_id=1, source_target_pairs={{0,3},{1,0},{2,1},{3,2},{4,7},{5,4},{6,5},{7,6},{8,11},{9,8},{10,9... | collective-permute-start | bytes 835592 | tf_op jit(solution)/shard_map/ppermute | solution.py:28
  97.2 5.5 %all-to-all-done.3.refs_2_ = bf16[32,32,256]{2,1,0:T(8,128)(2,1)S(1)} async-done(((bf16[32,32,256]{2,1,0:T(8,128)(2,1)}), bf16[32,32,256]{2,1,0:T(8,128)(2,1)S(1)}, u32[]{:S(2)}, u32[]{:S(2)}) %all-to-all-start.3) | async-done | bytes 524320 | tf_op jit(solution)/shard_map/all_to_all | solution.py:32
  102.7 3.2 %collective-permute-start.17 = (bf16[32,32,256]{2,1,0:T(8,128)(2,1)S(1)}, bf16[32,32,256]{2,1,0:T(8,128)(2,1)S(1)}, u32[]{:S(2)}, u32[]{:S(2)}) collective-permute-start(bf16[32,32,256]{2,1,0:T(8,128)(2,1)S(1)} %all-to-all-done.3.refs_2_), channel_id=1, source_target_pairs={{0,3},{1,0},{2,1},{3,2},{4,7},{5,4},{6,5},{7,6},{8,11},{9,8},{10,9... | collective-permute-start | bytes 1572872 | tf_op jit(solution)/shard_map/ppermute | solution.py:28
  108.2 4.6 %all-to-all-start.2 = ((bf16[32,48,256]{2,1,0:T(8,128)(2,1)}), bf16[32,48,256]{2,1,0:T(8,128)(2,1)}, u32[]{:S(2)}, u32[]{:S(2)}) async-start(bf16[32,48,256]{2,1,0:T(8,128)(2,1)} %pad_maximum_fusion), calls=%async_computation.2 | async-start | bytes 1572864 | tf_op jit(solution)/shard_map/all_to_all | solution.py:32
  112.8 5.0 %collective-permute-done.16.refs_3_ = bf16[32,32,256]{2,1,0:T(8,128)(2,1)S(1)} collective-permute-done((bf16[32,32,256]{2,1,0:T(8,128)(2,1)S(1)}, bf16[32,32,256]{2,1,0:T(8,128)(2,1)S(1)}, u32[]{:S(2)}, u32[]{:S(2)}) %collective-permute-start.16) | collective-permute-done | bytes 524320 | tf_op jit(solution)/shard_map/ppermute | solution.py:28
  119.3 3.2 %collective-permute-start.19 = (bf16[16,32,256]{2,1,0:T(8,128)(2,1)}, bf16[16,32,256]{2,1,0:T(8,128)(2,1)}, u32[]{:S(2)}, u32[]{:S(2)}) collective-permute-start(bf16[16,32,256]{2,1,0:T(8,128)(2,1)} %slice.127), channel_id=1, source_target_pairs={{0,3},{1,0},{2,1},{3,2},{4,7},{5,4},{6,5},{7,6},{8,11},{9,8},{10,9... | collective-permute-start | bytes 786440 | tf_op jit(solution)/shard_map/ppermute | solution.py:28
  122.5 5.4 %stats.2 = (f32[2,256,1024]{2,1,0:T(8,128)}, f32[2,256,1024]{2,1,0:T(8,128)}) custom-call(s32[4]{0:T(128)} %copy-done.3, bf16[32,32,256]{2,1,0:T(8,128)(2,1)} %copy-done, bf16[32,32,256]{2,1,0:T(8,128)(2,1)} %copy-done.1, bf16[32,32,256]{2,1,0:T(8,128)(2,1)} %copy-done.7, bf16[16,32,256]{2,1,0:T(8,128)(2,1)} %copy-done.4, bf16[16,32,256]{2,1,0:T(8,128)(2,1)} %copy-done.5, ...), custom_call_target="tpu_custom_call" | custom-call | flops 6442450944 | bytes 6291456 | tf_op jit(solution)/shard_map/stats/pallas_call | solution.py:255
  129.1 3.2 %collective-permute-start.11 = (bf16[32,32,256]{2,1,0:T(8,128)(2,1)S(1)}, bf16[32,32,256]{2,1,0:T(8,128)(2,1)S(1)}, u32[]{:S(2)}, u32[]{:S(2)}) collective-permute-start(bf16[32,32,256]{2,1,0:T(8,128)(2,1)S(1)} %slice.148.refs_2_), channel_id=1, source_target_pairs={{0,3},{1,0},{2,1},{3,2},{4,7},{5,4},{6,5},{7,6},{8,11},{9,8},{10,9... | collective-permute-start | bytes 1572872 | tf_op jit(solution)/shard_map/ppermute | solution.py:28
  132.4 5.5 %stats.3 = (f32[2,256,1024]{2,1,0:T(8,128)}, f32[2,256,1024]{2,1,0:T(8,128)}) custom-call(s32[4]{0:T(128)} %copy-done.2, bf16[32,32,1024]{2,1,0:T(8,128)(2,1)} %all-to-all-done.refs_3_.refs_1_, f32[2,256,1024]{2,1,0:T(8,128)} %refs_2_, f32[2,256,1024]{2,1,0:T(8,128)} %refs_3_, ...), custom_call_target="tpu_custom_call", output_to_operand_aliasing={{0}: (4, {}), {1}: (5, {})} | custom-call | flops 6442450944 | bytes 6291456 | tf_op jit(solution)/shard_map/stats/pallas_call | solution.py:255
  140.7 2.8 %collective-permute-done.10.refs_3_ = bf16[32,32,256]{2,1,0:T(8,128)(2,1)S(1)} collective-permute-done((bf16[32,32,256]{2,1,0:T(8,128)(2,1)S(1)}, bf16[32,32,256]{2,1,0:T(8,128)(2,1)S(1)}, u32[]{:S(2)}, u32[]{:S(2)}) %collective-permute-start.10) | collective-permute-done | bytes 524320 | tf_op jit(solution)/shard_map/ppermute | solution.py:28
  143.6 3.3 %collective-permute-start.13 = (bf16[16,32,256]{2,1,0:T(8,128)(2,1)S(1)}, bf16[16,32,256]{2,1,0:T(8,128)(2,1)S(1)}, u32[]{:S(2)}, u32[]{:S(2)}) collective-permute-start(bf16[16,32,256]{2,1,0:T(8,128)(2,1)S(1)} %slice.150), channel_id=1, source_target_pairs={{0,3},{1,0},{2,1},{3,2},{4,7},{5,4},{6,5},{7,6},{8,11},{9,8},{10,9... | collective-permute-start | bytes 786440 | tf_op jit(solution)/shard_map/ppermute | solution.py:28
  147.3 2.9 %scale.2.refs_7_ = bf16[32,2,32,1024]{3,2,1,0:T(8,128)(2,1)} custom-call(f32[64]{0:T(128)S(1)} %select_reduce_fusion.refs_0_, s32[1]{0:T(128)} %bitcast.2.refs_1_, bf16[32,32,256]{2,1,0:T(8,128)(2,1)S(1)} %all-to-all-done.3.refs_2_, bf16[32,32,256]{2,1,0:T(8,128)(2,1)S(1)} %collective-permute-done.16.refs_3_, ...), custom_call_target="tpu_custom_call" | custom-call | bytes 12582912 | tf_op jit(solution)/shard_map/scale/pallas_call | solution.py:304
  151.4 2.3 %scale.3 = bf16[32,2,32,1024]{3,2,1,0:T(8,128)(2,1)} custom-call(f32[64]{0:T(128)S(1)} %select_reduce_fusion.refs_0_, s32[1]{0:T(128)} %bitcast.2.refs_1_, bf16[32,32,256]{2,1,0:T(8,128)(2,1)S(1)} %slice.148.refs_2_, bf16[32,32,256]{2,1,0:T(8,128)(2,1)S(1)} %collective-permute-done.10.refs_3_, ...), custom_call_target="tpu_custom_call", output_to_operand_aliasing={{}: (7, {})} | custom-call | bytes 12582912 | tf_op jit(solution)/shard_map/scale/pallas_call | solution.py:304
  (95 shorter events, 31.4 us)
Async XLA Ops:
  21.7 23.9 %copy-start = (bf16[32,32,256]{2,1,0:T(8,128)(2,1)}, bf16[32,32,256]{2,1,0:T(8,128)(2,1)S(1)}, u32[]{:S(2)}) copy-start(bf16[32,32,256]{2,1,0:T(8,128)(2,1)S(1)} %all_to_all.20.refs_3_.refs_1_) | copy-start | bytes 1572868
  21.7 15.1 %collective-permute-start = (bf16[32,32,256]{2,1,0:T(8,128)(2,1)S(1)}, bf16[32,32,256]{2,1,0:T(8,128)(2,1)S(1)}, u32[]{:S(2)}, u32[]{:S(2)}) collective-permute-start(bf16[32,32,256]{2,1,0:T(8,128)(2,1)S(1)} %all_to_all.20.refs_3_.refs_1_), channel_id=1, source_target_pairs={{0,1},{1,2},{2,3},{3,0},{4,5},{5,6},{6,7},{7,4},{8,9},{9,10},{10,1... | collective-permute-start | bytes 1572872 | tf_op jit(solution)/shard_map/ppermute | solution.py:28
  23.2 14.0 %collective-permute-start.1 = (bf16[32,32,256]{2,1,0:T(8,128)(2,1)S(1)}, bf16[32,32,256]{2,1,0:T(8,128)(2,1)S(1)}, u32[]{:S(2)}, u32[]{:S(2)}) collective-permute-start(bf16[32,32,256]{2,1,0:T(8,128)(2,1)S(1)} %all_to_all.20.refs_3_.refs_1_), channel_id=1, source_target_pairs={{0,3},{1,0},{2,1},{3,2},{4,7},{5,4},{6,5},{7,6},{8,11},{9,8},{10,9... | collective-permute-start | bytes 1572872 | tf_op jit(solution)/shard_map/ppermute | solution.py:28
  27.4 34.7 %all-to-all-start = ((bf16[32,32,1024]{2,1,0:T(8,128)(2,1)}), bf16[32,32,1024]{2,1,0:T(8,128)(2,1)}, u32[]{:S(2)}, u32[]{:S(2)}) async-start(bf16[32,32,1024]{2,1,0:T(8,128)(2,1)} %pick.1), calls=%async_computation | async-start | bytes 4194304 | tf_op jit(solution)/shard_map/all_to_all | solution.py:32
  36.8 8.7 %collective-permute-start.2 = (bf16[16,32,256]{2,1,0:T(8,128)(2,1)S(1)}, bf16[16,32,256]{2,1,0:T(8,128)(2,1)S(1)}, u32[]{:S(2)}, u32[]{:S(2)}) collective-permute-start(bf16[16,32,256]{2,1,0:T(8,128)(2,1)S(1)} %slice.129), channel_id=1, source_target_pairs={{0,1},{1,2},{2,3},{3,0},{4,5},{5,6},{6,7},{7,4},{8,9},{9,10},{10,1... | collective-permute-start | bytes 786440 | tf_op jit(solution)/shard_map/ppermute | solution.py:28
  37.2 8.3 %collective-permute-start.3 = (bf16[16,32,256]{2,1,0:T(8,128)(2,1)S(1)}, bf16[16,32,256]{2,1,0:T(8,128)(2,1)S(1)}, u32[]{:S(2)}, u32[]{:S(2)}) collective-permute-start(bf16[16,32,256]{2,1,0:T(8,128)(2,1)S(1)} %slice.130), channel_id=1, source_target_pairs={{0,3},{1,0},{2,1},{3,2},{4,7},{5,4},{6,5},{7,6},{8,11},{9,8},{10,9... | collective-permute-start | bytes 786440 | tf_op jit(solution)/shard_map/ppermute | solution.py:28
  47.3 16.4 %collective-permute-start.4 = (bf16[32,32,256]{2,1,0:T(8,128)(2,1)}, bf16[32,32,256]{2,1,0:T(8,128)(2,1)}, u32[]{:S(2)}, u32[]{:S(2)}) collective-permute-start(bf16[32,32,256]{2,1,0:T(8,128)(2,1)} %get-tuple-element.36), channel_id=1, source_target_pairs={{0,1},{1,2},{2,3},{3,0},{4,5},{5,6},{6,7},{7,4},{8,9},{9,10},{10,1... | collective-permute-start | bytes 1572872 | tf_op jit(solution)/shard_map/ppermute | solution.py:28
  54.7 11.5 %collective-permute-start.5 = (bf16[32,32,256]{2,1,0:T(8,128)(2,1)}, bf16[32,32,256]{2,1,0:T(8,128)(2,1)}, u32[]{:S(2)}, u32[]{:S(2)}) collective-permute-start(bf16[32,32,256]{2,1,0:T(8,128)(2,1)} %get-tuple-element.37), channel_id=1, source_target_pairs={{0,3},{1,0},{2,1},{3,2},{4,7},{5,4},{6,5},{7,6},{8,11},{9,8},{10,9... | collective-permute-start | bytes 1572872 | tf_op jit(solution)/shard_map/ppermute | solution.py:28
  67.9 12.3 %collective-permute-start.15 = (bf16[16,32,256]{2,1,0:T(8,128)(2,1)}, bf16[16,32,256]{2,1,0:T(8,128)(2,1)S(1)}, u32[]{:S(2)}, u32[]{:S(2)}) collective-permute-start(bf16[16,32,256]{2,1,0:T(8,128)(2,1)} %slice_select_fusion.2), channel_id=1, source_target_pairs={{0,3},{1,0},{2,1},{3,2},{4,7},{5,4},{6,5},{7,6},{8,11},{9,8},{10,9... | collective-permute-start | bytes 786440 | tf_op jit(solution)/shard_map/ppermute | solution.py:28
  68.9 11.7 %collective-permute-start.14 = (bf16[16,32,256]{2,1,0:T(8,128)(2,1)S(1)}, bf16[16,32,256]{2,1,0:T(8,128)(2,1)S(1)}, u32[]{:S(2)}, u32[]{:S(2)}) collective-permute-start(bf16[16,32,256]{2,1,0:T(8,128)(2,1)S(1)} %slice_select_fusion.3), channel_id=1, source_target_pairs={{0,1},{1,2},{2,3},{3,0},{4,5},{5,6},{6,7},{7,4},{8,9},{9,10},{10,1... | collective-permute-start | bytes 786440 | tf_op jit(solution)/shard_map/ppermute | solution.py:28
  73.9 17.0 %collective-permute-start.6 = (bf16[33,32,256]{2,1,0:T(8,128)(2,1)}, bf16[33,32,256]{2,1,0:T(8,128)(2,1)}, u32[]{:S(2)}, u32[]{:S(2)}) collective-permute-start(bf16[33,32,256]{2,1,0:T(8,128)(2,1)} %get-tuple-element.39), channel_id=1, source_target_pairs={{0,3},{1,0},{2,1},{3,2},{4,7},{5,4},{6,5},{7,6},{8,11},{9,8},{10,9... | collective-permute-start | bytes 1622024 | tf_op jit(solution)/shard_map/ppermute | solution.py:28
  73.9 17.1 %collective-permute-start.7 = (bf16[33,32,256]{2,1,0:T(8,128)(2,1)S(1)}, bf16[33,32,256]{2,1,0:T(8,128)(2,1)}, u32[]{:S(2)}, u32[]{:S(2)}) collective-permute-start(bf16[33,32,256]{2,1,0:T(8,128)(2,1)S(1)} %get-tuple-element.41), channel_id=1, source_target_pairs={{0,1},{1,2},{2,3},{3,0},{4,5},{5,6},{6,7},{7,4},{8,9},{9,10},{10,1... | collective-permute-start | bytes 1622024 | tf_op jit(solution)/shard_map/ppermute | solution.py:28
  82.5 20.2 %all-to-all-start.3 = ((bf16[32,32,256]{2,1,0:T(8,128)(2,1)}), bf16[32,32,256]{2,1,0:T(8,128)(2,1)S(1)}, u32[]{:S(2)}, u32[]{:S(2)}) async-start(bf16[32,32,256]{2,1,0:T(8,128)(2,1)} %pad_maximum_fusion.1), calls=%async_computation.3 | async-start | bytes 1048576 | tf_op jit(solution)/shard_map/all_to_all | solution.py:32
  92.2 13.7 %collective-permute-start.8 = (bf16[17,32,256]{2,1,0:T(8,128)(2,1)S(1)}, bf16[17,32,256]{2,1,0:T(8,128)(2,1)S(1)}, u32[]{:S(2)}, u32[]{:S(2)}) collective-permute-start(bf16[17,32,256]{2,1,0:T(8,128)(2,1)S(1)} %get-tuple-element.68), channel_id=1, source_target_pairs={{0,1},{1,2},{2,3},{3,0},{4,5},{5,6},{6,7},{7,4},{8,9},{9,10},{10,1... | collective-permute-start | bytes 835592 | tf_op jit(solution)/shard_map/ppermute | solution.py:28
  92.3 13.6 %collective-permute-start.9 = (bf16[17,32,256]{2,1,0:T(8,128)(2,1)S(1)}, bf16[17,32,256]{2,1,0:T(8,128)(2,1)}, u32[]{:S(2)}, u32[]{:S(2)}) collective-permute-start(bf16[17,32,256]{2,1,0:T(8,128)(2,1)S(1)} %get-tuple-element.67), channel_id=1, source_target_pairs={{0,3},{1,0},{2,1},{3,2},{4,7},{5,4},{6,5},{7,6},{8,11},{9,8},{10,9... | collective-permute-start | bytes 835592 | tf_op jit(solution)/shard_map/ppermute | solution.py:28
  102.7 15.1 %collective-permute-start.16 = (bf16[32,32,256]{2,1,0:T(8,128)(2,1)S(1)}, bf16[32,32,256]{2,1,0:T(8,128)(2,1)S(1)}, u32[]{:S(2)}, u32[]{:S(2)}) collective-permute-start(bf16[32,32,256]{2,1,0:T(8,128)(2,1)S(1)} %all-to-all-done.3.refs_2_), channel_id=1, source_target_pairs={{0,1},{1,2},{2,3},{3,0},{4,5},{5,6},{6,7},{7,4},{8,9},{9,10},{10,1... | collective-permute-start | bytes 1572872 | tf_op jit(solution)/shard_map/ppermute | solution.py:28
  102.7 15.1 %collective-permute-start.17 = (bf16[32,32,256]{2,1,0:T(8,128)(2,1)S(1)}, bf16[32,32,256]{2,1,0:T(8,128)(2,1)S(1)}, u32[]{:S(2)}, u32[]{:S(2)}) collective-permute-start(bf16[32,32,256]{2,1,0:T(8,128)(2,1)S(1)} %all-to-all-done.3.refs_2_), channel_id=1, source_target_pairs={{0,3},{1,0},{2,1},{3,2},{4,7},{5,4},{6,5},{7,6},{8,11},{9,8},{10,9... | collective-permute-start | bytes 1572872 | tf_op jit(solution)/shard_map/ppermute | solution.py:28
  108.2 19.8 %all-to-all-start.2 = ((bf16[32,48,256]{2,1,0:T(8,128)(2,1)}), bf16[32,48,256]{2,1,0:T(8,128)(2,1)}, u32[]{:S(2)}, u32[]{:S(2)}) async-start(bf16[32,48,256]{2,1,0:T(8,128)(2,1)} %pad_maximum_fusion), calls=%async_computation.2 | async-start | bytes 1572864 | tf_op jit(solution)/shard_map/all_to_all | solution.py:32
  118.5 28.7 %collective-permute-start.18 = (bf16[16,32,256]{2,1,0:T(8,128)(2,1)}, bf16[16,32,256]{2,1,0:T(8,128)(2,1)S(1)}, u32[]{:S(2)}, u32[]{:S(2)}) collective-permute-start(bf16[16,32,256]{2,1,0:T(8,128)(2,1)} %slice.126), channel_id=1, source_target_pairs={{0,1},{1,2},{2,3},{3,0},{4,5},{5,6},{6,7},{7,4},{8,9},{9,10},{10,1... | collective-permute-start | bytes 786440 | tf_op jit(solution)/shard_map/ppermute | solution.py:28
  119.3 28.0 %collective-permute-start.19 = (bf16[16,32,256]{2,1,0:T(8,128)(2,1)}, bf16[16,32,256]{2,1,0:T(8,128)(2,1)}, u32[]{:S(2)}, u32[]{:S(2)}) collective-permute-start(bf16[16,32,256]{2,1,0:T(8,128)(2,1)} %slice.127), channel_id=1, source_target_pairs={{0,3},{1,0},{2,1},{3,2},{4,7},{5,4},{6,5},{7,6},{8,11},{9,8},{10,9... | collective-permute-start | bytes 786440 | tf_op jit(solution)/shard_map/ppermute | solution.py:28
  129.0 14.4 %collective-permute-start.10 = (bf16[32,32,256]{2,1,0:T(8,128)(2,1)S(1)}, bf16[32,32,256]{2,1,0:T(8,128)(2,1)S(1)}, u32[]{:S(2)}, u32[]{:S(2)}) collective-permute-start(bf16[32,32,256]{2,1,0:T(8,128)(2,1)S(1)} %slice.148.refs_2_), channel_id=1, source_target_pairs={{0,1},{1,2},{2,3},{3,0},{4,5},{5,6},{6,7},{7,4},{8,9},{9,10},{10,1... | collective-permute-start | bytes 1572872 | tf_op jit(solution)/shard_map/ppermute | solution.py:28
  129.1 14.5 %collective-permute-start.11 = (bf16[32,32,256]{2,1,0:T(8,128)(2,1)S(1)}, bf16[32,32,256]{2,1,0:T(8,128)(2,1)S(1)}, u32[]{:S(2)}, u32[]{:S(2)}) collective-permute-start(bf16[32,32,256]{2,1,0:T(8,128)(2,1)S(1)} %slice.148.refs_2_), channel_id=1, source_target_pairs={{0,3},{1,0},{2,1},{3,2},{4,7},{5,4},{6,5},{7,6},{8,11},{9,8},{10,9... | collective-permute-start | bytes 1572872 | tf_op jit(solution)/shard_map/ppermute | solution.py:28
  143.5 7.9 %collective-permute-start.12 = (bf16[16,32,256]{2,1,0:T(8,128)(2,1)S(1)}, bf16[16,32,256]{2,1,0:T(8,128)(2,1)S(1)}, u32[]{:S(2)}, u32[]{:S(2)}) collective-permute-start(bf16[16,32,256]{2,1,0:T(8,128)(2,1)S(1)} %slice.149), channel_id=1, source_target_pairs={{0,1},{1,2},{2,3},{3,0},{4,5},{5,6},{6,7},{7,4},{8,9},{9,10},{10,1... | collective-permute-start | bytes 786440 | tf_op jit(solution)/shard_map/ppermute | solution.py:28
  143.6 7.8 %collective-permute-start.13 = (bf16[16,32,256]{2,1,0:T(8,128)(2,1)S(1)}, bf16[16,32,256]{2,1,0:T(8,128)(2,1)S(1)}, u32[]{:S(2)}, u32[]{:S(2)}) collective-permute-start(bf16[16,32,256]{2,1,0:T(8,128)(2,1)S(1)} %slice.150), channel_id=1, source_target_pairs={{0,3},{1,0},{2,1},{3,2},{4,7},{5,4},{6,5},{7,6},{8,11},{9,8},{10,9... | collective-permute-start | bytes 786440 | tf_op jit(solution)/shard_map/ppermute | solution.py:28
  (11 other events, 68.2 us)

commit v5 on v4

--- a/solution.py
+++ b/solution.py
@@ -270,15 +270,18 @@
     )(*operands)
 
 
-def scale_kernel(which, slots, scales, place, *refs):
-    pieces = refs[:5]
+def scale_kernel(which, slots, parts, scales, place, *refs):
+    pieces = refs[:parts]
     out, held, ready, come, go = refs[-5:]
-    half = pieces[4].shape[0]
+    half = held.shape[1]
     reads = []
     for part in range(2):
         for at in range(4):
             i = 4 * part + at
-            source = pieces[3 + part] if at == 3 else pieces[at].at[pl.ds(part * half, half)]
+            if parts == 8:
+                source = pieces[i]
+            else:
+                source = pieces[3 + part] if at == 3 else pieces[at].at[pl.ds(part * half, half)]
             reads.append(pltpu.make_async_copy(source, held.at[i], come.at[i]))
     for read in reads:
         read.start()
@@ -300,9 +303,10 @@
 
 def scale_rows(which, slots, scales, place, pieces, earlier):
     count, rows, width = pieces[0].shape
+    count = 2 * count if len(pieces) == 8 else count
     operands = [scales, place, *pieces] + ([] if earlier is None else [earlier])
     return pl.pallas_call(
-        lambda *refs: scale_kernel(which, slots, *refs),
+        lambda *refs: scale_kernel(which, slots, len(pieces), *refs),
         out_shape=jax.ShapeDtypeStruct((count, slots, rows, 4 * width), BF16),
         in_specs=[SMEM, SMEM] + anywhere(len(operands) - 2),
         out_specs=anywhere(1)[0],
@@ -351,6 +355,16 @@
     return quarter, shift(quarter, 1), shift(quarter, -1)
 
 
+def gather_halves(low, high):
+    left_low = shift(low, 1)
+    right_high = shift(high, -1)
+    left_high = shift(high, 1)
+    right_low = shift(low, -1)
+    far_low = shift(left_low, 1)
+    far_high = shift(right_high, -1)
+    return [low, left_low, right_low, far_low, high, left_high, right_high, far_high]
+
+
 def gather_second(pieces):
     _, left, right = pieces
     half = left.shape[0] // 2
@@ -418,9 +432,10 @@
     pieces = gather_first(first)
     pieces, stat_left, stat_right = in_order(pieces, stat_left, stat_right)
     stats = update_stats(0, infos[0], blocks[0], stat_left, stat_right, None)
+    second, stats = in_order(second, stats)
     stats = update_stats(1, infos[1], blocks[1], stat_left, stat_right, stats)
     gathered = gather_second(pieces)
-    pieces_next = gather_first(second[:, :shard_rows])
+    pieces_next = gather_halves(second[:half, :shard_rows], second[half:, :shard_rows])
     sums = second[:, shard_rows : shard_rows + 6, :].astype(F32)
     sums = sums.reshape(dp_count, 2, 3, local_total, width // local_total)[..., 0]
     sums = jnp.sum(sums, axis=2) / SUM_SCALE
@@ -434,7 +449,7 @@
 
     place = me.reshape(1).astype(jnp.int32)
     update = scale_rows(0, local_total, scales, place, gathered, None)
-    update = scale_rows(1, local_total, scales, place, gather_second(pieces_next), update)
+    update = scale_rows(1, local_total, scales, place, pieces_next, update)
     return (update.reshape(block_total, shard_rows, order), *stats)
 
 

time: 155 us -> 154 us (level)
  waiting for transfers between devices: 33.8 us -> 43.5 us
  starting transfers between devices: 55.3 us -> 51.4 us
  local copies, waits for them, and re-layouts: 10.3 us -> 6.65 us
  other arithmetic: 10.2 us -> 8.54 us
    ppermute x20 -> x22, waiting for transfers between devices: 20.8 us -> 33.9 us  [shift(): lax.ppermute(x, 'replica', [(i, (i + step) % count) for i in range(count)])]
    all_to_all x3, starting transfers between devices: 17.8 us -> 13.4 us  [over_dp(): return lax.all_to_all(x, 'dp', split_axis=0, concat_axis=0, tiled=True)]
    all_to_all x3, waiting for transfers between devices: 13 us -> 9.6 us  [over_dp(): return lax.all_to_all(x, 'dp', split_axis=0, concat_axis=0, tiled=True)]
    slice x1, local copies, waits for them, and re-layouts: 1.57 us -> 0.01 us  [per_device(): sums = second[:, shard_rows:shard_rows + 6, :].astype(F32)]
    ppermute x20 -> x22, starting transfers between devices: 37.5 us -> 38 us  [shift(): lax.ppermute(x, 'replica', [(i, (i + step) % count) for i in range(count)])]
  transfers between devices with their start and end apart: 23 -> 25, of which waited for: 10 -> 14; matrix products, arithmetic and copies ran while one was open for 11% -> 9% of each run, Pallas kernels for 13% -> 12%
where the time goes in v5:
time: 154 us
  starting transfers between devices  51.4 us (33%)
  waiting for transfers between devices  43.5 us (28%)
  Pallas kernels  21.4 us (14%)
  blocking collectives  20 us (13%)
  other arithmetic  8.54 us (6%)
  local copies, waits for them, and re-layouts  6.65 us (4%)
  between operations  2.48 us (2%)
    ppermute x22, starting transfers between devices, shift(): lax.ppermute(x, 'replica', [(i, (i + step) % count) for i in range(count)])  38 us
    ppermute x22, waiting for transfers between devices, shift(): lax.ppermute(x, 'replica', [(i, (i + step) % count) for i in range(count)])  33.9 us
    all_to_all x1, blocking collectives, over_dp(): return lax.all_to_all(x, 'dp', split_axis=0, concat_axis=0, tiled=True)  20 us
    all_to_all x3, starting transfers between devices, over_dp(): return lax.all_to_all(x, 'dp', split_axis=0, concat_axis=0, tiled=True)  13.4 us
    pallas_call x2, Pallas kernels, update_stats(): pl.pallas_call(lambda *refs: stats_kernel(len(pieces), *refs), out_shape=...  11 us
    all_to_all x3, waiting for transfers between devices, over_dp(): return lax.all_to_all(x, 'dp', split_axis=0, concat_axis=0, tiled=True)  9.6 us
    pallas_call x2, Pallas kernels, scale_rows(): pl.pallas_call(lambda *refs: scale_kernel(which, slots, len(pieces), *ref...  4.54 us
    pallas_call x2, Pallas kernels, apply_roots(): pl.pallas_call(lambda *refs: roots_kernel(len(pieces), before is not None...  3.44 us
  transfers between devices with their start and end apart: 25, of which 14 were waited for; matrix products, arithmetic and copies ran while one was open for 9% of the time, Pallas kernels for 12%

profile of v5, /device:TPU:0, one launch (start us, length us, event | category | flops | bytes accessed | tf_op | source)
XLA Modules:
  0.0 153.9 jit_solution(12219025783071247952)
XLA Ops:
  1.7 20.0 %all_to_all.20.refs_3_.refs_1_ = bf16[32,32,256]{2,1,0:T(8,128)(2,1)S(1)} all-to-all(bf16[32,32,256]{2,1,0:T(8,128)(2,1)S(1)} %dynamic-slice_bitcast_fusion), channel_id=1, replica_groups=mesh['dp'=32,'replica'=4] {'dp'}, dimensions={0} | all-to-all | bytes 1048576 | tf_op jit(solution)/shard_map/all_to_all | solution.py:32
  21.7 2.8 %collective-permute-start.1 = (bf16[32,32,256]{2,1,0:T(8,128)(2,1)S(1)}, bf16[32,32,256]{2,1,0:T(8,128)(2,1)S(1)}, u32[]{:S(2)}, u32[]{:S(2)}) collective-permute-start(bf16[32,32,256]{2,1,0:T(8,128)(2,1)S(1)} %all_to_all.20.refs_3_.refs_1_), channel_id=1, source_target_pairs={{0,3},{1,0},{2,1},{3,2},{4,7},{5,4},{6,5},{7,6},{8,11},{9,8},{10,9... | collective-permute-start | bytes 1572872 | tf_op jit(solution)/shard_map/ppermute | solution.py:28
  24.5 2.4 %pick.1 = bf16[32,32,1024]{2,1,0:T(8,128)(2,1)} custom-call(bf16[32,2,32,1024]{3,2,1,0:T(8,128)(2,1)} %bitcast.21), custom_call_target="tpu_custom_call" | custom-call | bytes 8388608 | tf_op jit(solution)/shard_map/pick/pallas_call | solution.py:64
  26.9 4.8 %all-to-all-start = ((bf16[32,32,1024]{2,1,0:T(8,128)(2,1)}), bf16[32,32,1024]{2,1,0:T(8,128)(2,1)}, u32[]{:S(2)}, u32[]{:S(2)}) async-start(bf16[32,32,1024]{2,1,0:T(8,128)(2,1)} %pick.1), calls=%async_computation | async-start | bytes 4194304 | tf_op jit(solution)/shard_map/all_to_all | solution.py:32
  31.7 4.2 %collective-permute-done.1.refs_5_.refs_3_ = bf16[32,32,256]{2,1,0:T(8,128)(2,1)S(1)} collective-permute-done((bf16[32,32,256]{2,1,0:T(8,128)(2,1)S(1)}, bf16[32,32,256]{2,1,0:T(8,128)(2,1)S(1)}, u32[]{:S(2)}, u32[]{:S(2)}) %collective-permute-start.1) | collective-permute-done | bytes 524320 | tf_op jit(solution)/shard_map/ppermute | solution.py:28
  35.9 3.8 %collective-permute-start.3 = (bf16[16,32,256]{2,1,0:T(8,128)(2,1)S(1)}, bf16[16,32,256]{2,1,0:T(8,128)(2,1)S(1)}, u32[]{:S(2)}, u32[]{:S(2)}) collective-permute-start(bf16[16,32,256]{2,1,0:T(8,128)(2,1)S(1)} %slice.126), channel_id=1, source_target_pairs={{0,3},{1,0},{2,1},{3,2},{4,7},{5,4},{6,5},{7,6},{8,11},{9,8},{10,9... | collective-permute-start | bytes 786440 | tf_op jit(solution)/shard_map/ppermute | solution.py:28
  45.0 3.2 %collective-permute-done.2.refs_6_.refs_4_ = bf16[16,32,256]{2,1,0:T(8,128)(2,1)S(1)} collective-permute-done((bf16[16,32,256]{2,1,0:T(8,128)(2,1)S(1)}, bf16[16,32,256]{2,1,0:T(8,128)(2,1)S(1)}, u32[]{:S(2)}, u32[]{:S(2)}) %collective-permute-start.2) | collective-permute-done | bytes 262176 | tf_op jit(solution)/shard_map/ppermute | solution.py:28
  49.9 7.1 %collective-permute-start.5 = (bf16[32,32,256]{2,1,0:T(8,128)(2,1)}, bf16[32,32,256]{2,1,0:T(8,128)(2,1)S(1)}, u32[]{:S(2)}, u32[]{:S(2)}) collective-permute-start(bf16[32,32,256]{2,1,0:T(8,128)(2,1)} %get-tuple-element.40), channel_id=1, source_target_pairs={{0,3},{1,0},{2,1},{3,2},{4,7},{5,4},{6,5},{7,6},{8,11},{9,8},{10,9... | collective-permute-start | bytes 1572872 | tf_op jit(solution)/shard_map/ppermute | solution.py:28
  57.0 4.6 %all-to-all-done.refs_3_.refs_1_ = bf16[32,32,1024]{2,1,0:T(8,128)(2,1)} async-done(((bf16[32,32,1024]{2,1,0:T(8,128)(2,1)}), bf16[32,32,1024]{2,1,0:T(8,128)(2,1)}, u32[]{:S(2)}, u32[]{:S(2)}) %all-to-all-start) | async-done | bytes 2097184 | tf_op jit(solution)/shard_map/all_to_all | solution.py:32
  63.4 4.4 %collective-permute-done.4 = bf16[32,32,256]{2,1,0:T(8,128)(2,1)S(1)} collective-permute-done((bf16[32,32,256]{2,1,0:T(8,128)(2,1)}, bf16[32,32,256]{2,1,0:T(8,128)(2,1)S(1)}, u32[]{:S(2)}, u32[]{:S(2)}) %collective-permute-start.4) | collective-permute-done | bytes 524320 | tf_op jit(solution)/shard_map/ppermute | solution.py:28
  70.5 4.9 %collective-permute-start.11 = (bf16[16,32,256]{2,1,0:T(8,128)(2,1)}, bf16[16,32,256]{2,1,0:T(8,128)(2,1)}, u32[]{:S(2)}, u32[]{:S(2)}) collective-permute-start(bf16[16,32,256]{2,1,0:T(8,128)(2,1)} %slice_select_fusion.2), channel_id=1, source_target_pairs={{0,3},{1,0},{2,1},{3,2},{4,7},{5,4},{6,5},{7,6},{8,11},{9,8},{10,9... | collective-permute-start | bytes 786440 | tf_op jit(solution)/shard_map/ppermute | solution.py:28
  77.4 2.6 %collective-permute-done.10 = bf16[16,32,256]{2,1,0:T(8,128)(2,1)S(1)} collective-permute-done((bf16[16,32,256]{2,1,0:T(8,128)(2,1)}, bf16[16,32,256]{2,1,0:T(8,128)(2,1)S(1)}, u32[]{:S(2)}, u32[]{:S(2)}) %collective-permute-start.10) | collective-permute-done | bytes 262176 | tf_op jit(solution)/shard_map/ppermute | solution.py:28
  80.1 2.4 %collective-permute-done.11 = bf16[16,32,256]{2,1,0:T(8,128)(2,1)} collective-permute-done((bf16[16,32,256]{2,1,0:T(8,128)(2,1)}, bf16[16,32,256]{2,1,0:T(8,128)(2,1)}, u32[]{:S(2)}, u32[]{:S(2)}) %collective-permute-start.11) | collective-permute-done | bytes 262176 | tf_op jit(solution)/shard_map/ppermute | solution.py:28
  84.3 4.7 %all-to-all-start.3 = ((bf16[32,32,256]{2,1,0:T(8,128)(2,1)}), bf16[32,32,256]{2,1,0:T(8,128)(2,1)S(1)}, u32[]{:S(2)}, u32[]{:S(2)}) async-start(bf16[32,32,256]{2,1,0:T(8,128)(2,1)} %pad_maximum_fusion.1), calls=%async_computation.3 | async-start | bytes 1048576 | tf_op jit(solution)/shard_map/all_to_all | solution.py:32
  95.8 5.0 %all-to-all-done.3.refs_2_ = bf16[32,32,256]{2,1,0:T(8,128)(2,1)S(1)} async-done(((bf16[32,32,256]{2,1,0:T(8,128)(2,1)}), bf16[32,32,256]{2,1,0:T(8,128)(2,1)S(1)}, u32[]{:S(2)}, u32[]{:S(2)}) %all-to-all-start.3) | async-done | bytes 524320 | tf_op jit(solution)/shard_map/all_to_all | solution.py:32
  100.8 3.7 %collective-permute-start.13 = (bf16[32,32,256]{2,1,0:T(8,128)(2,1)S(1)}, bf16[32,32,256]{2,1,0:T(8,128)(2,1)S(1)}, u32[]{:S(2)}, u32[]{:S(2)}) collective-permute-start(bf16[32,32,256]{2,1,0:T(8,128)(2,1)S(1)} %all-to-all-done.3.refs_2_), channel_id=1, source_target_pairs={{0,3},{1,0},{2,1},{3,2},{4,7},{5,4},{6,5},{7,6},{8,11},{9,8},{10,9... | collective-permute-start | bytes 1572872 | tf_op jit(solution)/shard_map/ppermute | solution.py:28
  107.3 3.9 %all-to-all-start.2 = ((bf16[32,48,256]{2,1,0:T(8,128)(2,1)}), bf16[32,48,256]{2,1,0:T(8,128)(2,1)S(1)}, u32[]{:S(2)}, u32[]{:S(2)}) async-start(bf16[32,48,256]{2,1,0:T(8,128)(2,1)} %pad_maximum_fusion), calls=%async_computation.2 | async-start | bytes 1572864 | tf_op jit(solution)/shard_map/all_to_all | solution.py:32
  111.3 4.6 %collective-permute-done.13.refs_4_ = bf16[32,32,256]{2,1,0:T(8,128)(2,1)S(1)} collective-permute-done((bf16[32,32,256]{2,1,0:T(8,128)(2,1)S(1)}, bf16[32,32,256]{2,1,0:T(8,128)(2,1)S(1)}, u32[]{:S(2)}, u32[]{:S(2)}) %collective-permute-start.13) | collective-permute-done | bytes 524320 | tf_op jit(solution)/shard_map/ppermute | solution.py:28
  115.9 3.4 %collective-permute-done.12.refs_3_ = bf16[32,32,256]{2,1,0:T(8,128)(2,1)S(1)} collective-permute-done((bf16[32,32,256]{2,1,0:T(8,128)(2,1)S(1)}, bf16[32,32,256]{2,1,0:T(8,128)(2,1)S(1)}, u32[]{:S(2)}, u32[]{:S(2)}) %collective-permute-start.12) | collective-permute-done | bytes 524320 | tf_op jit(solution)/shard_map/ppermute | solution.py:28
  122.8 5.4 %stats.2 = (f32[2,256,1024]{2,1,0:T(8,128)}, f32[2,256,1024]{2,1,0:T(8,128)}) custom-call(s32[4]{0:T(128)} %copy-done.3, bf16[32,32,256]{2,1,0:T(8,128)(2,1)} %copy-done, bf16[32,32,256]{2,1,0:T(8,128)(2,1)} %copy-done.1, bf16[32,32,256]{2,1,0:T(8,128)(2,1)} %copy-done.8, bf16[16,32,256]{2,1,0:T(8,128)(2,1)} %copy-done.5, bf16[16,32,256]{2,1,0:T(8,128)(2,1)} %copy-done.4, ...), custom_call_target="tpu_custom_call" | custom-call | flops 6442450944 | bytes 6291456 | tf_op jit(solution)/shard_map/stats/pallas_call | solution.py:255
  131.2 5.6 %stats.3 = (f32[2,256,1024]{2,1,0:T(8,128)}, f32[2,256,1024]{2,1,0:T(8,128)}) custom-call(s32[4]{0:T(128)} %copy-done.2, bf16[32,32,1024]{2,1,0:T(8,128)(2,1)} %all-to-all-done.refs_3_.refs_1_, f32[2,256,1024]{2,1,0:T(8,128)} %refs_2_, f32[2,256,1024]{2,1,0:T(8,128)} %refs_3_, ...), custom_call_target="tpu_custom_call", output_to_operand_aliasing={{0}: (4, {}), {1}: (5, {})} | custom-call | flops 6442450944 | bytes 6291456 | tf_op jit(solution)/shard_map/stats/pallas_call | solution.py:255
  137.0 3.3 %collective-permute-start.15 = (bf16[16,32,256]{2,1,0:T(8,128)(2,1)S(1)}, bf16[16,32,256]{2,1,0:T(8,128)(2,1)S(1)}, u32[]{:S(2)}, u32[]{:S(2)}) collective-permute-start(bf16[16,32,256]{2,1,0:T(8,128)(2,1)S(1)} %get-tuple-element.68.refs_2_), channel_id=1, source_target_pairs={{0,3},{1,0},{2,1},{3,2},{4,7},{5,4},{6,5},{7,6},{8,11},{9,8},{10,9... | collective-permute-start | bytes 786440 | tf_op jit(solution)/shard_map/ppermute | solution.py:28
  144.3 2.3 %scale.2.refs_10_ = bf16[32,2,32,1024]{3,2,1,0:T(8,128)(2,1)} custom-call(f32[64]{0:T(128)S(1)} %select_reduce_fusion.refs_0_, s32[1]{0:T(128)} %bitcast.2.refs_1_, bf16[32,32,256]{2,1,0:T(8,128)(2,1)S(1)} %all-to-all-done.3.refs_2_, bf16[32,32,256]{2,1,0:T(8,128)(2,1)S(1)} %collective-permute-done.12.refs_3_, ...), custom_call_target="tpu_custom_call" | custom-call | bytes 12582912 | tf_op jit(solution)/shard_map/scale/pallas_call | solution.py:308
  147.0 2.8 %collective-permute-done.19.refs_9_ = bf16[16,32,256]{2,1,0:T(8,128)(2,1)S(1)} collective-permute-done((bf16[16,32,256]{2,1,0:T(8,128)(2,1)S(1)}, bf16[16,32,256]{2,1,0:T(8,128)(2,1)S(1)}, u32[]{:S(2)}, u32[]{:S(2)}) %collective-permute-start.19) | collective-permute-done | bytes 262176 | tf_op jit(solution)/shard_map/ppermute | solution.py:28
  (98 shorter events, 39.8 us)
Async XLA Ops:
  21.7 14.2 %collective-permute-start.1 = (bf16[32,32,256]{2,1,0:T(8,128)(2,1)S(1)}, bf16[32,32,256]{2,1,0:T(8,128)(2,1)S(1)}, u32[]{:S(2)}, u32[]{:S(2)}) collective-permute-start(bf16[32,32,256]{2,1,0:T(8,128)(2,1)S(1)} %all_to_all.20.refs_3_.refs_1_), channel_id=1, source_target_pairs={{0,3},{1,0},{2,1},{3,2},{4,7},{5,4},{6,5},{7,6},{8,11},{9,8},{10,9... | collective-permute-start | bytes 1572872 | tf_op jit(solution)/shard_map/ppermute | solution.py:28
  24.5 15.2 %collective-permute-start = (bf16[32,32,256]{2,1,0:T(8,128)(2,1)S(1)}, bf16[32,32,256]{2,1,0:T(8,128)(2,1)S(1)}, u32[]{:S(2)}, u32[]{:S(2)}) collective-permute-start(bf16[32,32,256]{2,1,0:T(8,128)(2,1)S(1)} %all_to_all.20.refs_3_.refs_1_), channel_id=1, source_target_pairs={{0,1},{1,2},{2,3},{3,0},{4,5},{5,6},{6,7},{7,4},{8,9},{9,10},{10,1... | collective-permute-start | bytes 1572872 | tf_op jit(solution)/shard_map/ppermute | solution.py:28
  26.9 34.7 %all-to-all-start = ((bf16[32,32,1024]{2,1,0:T(8,128)(2,1)}), bf16[32,32,1024]{2,1,0:T(8,128)(2,1)}, u32[]{:S(2)}, u32[]{:S(2)}) async-start(bf16[32,32,1024]{2,1,0:T(8,128)(2,1)} %pick.1), calls=%async_computation | async-start | bytes 4194304 | tf_op jit(solution)/shard_map/all_to_all | solution.py:32
  35.9 9.0 %collective-permute-start.3 = (bf16[16,32,256]{2,1,0:T(8,128)(2,1)S(1)}, bf16[16,32,256]{2,1,0:T(8,128)(2,1)S(1)}, u32[]{:S(2)}, u32[]{:S(2)}) collective-permute-start(bf16[16,32,256]{2,1,0:T(8,128)(2,1)S(1)} %slice.126), channel_id=1, source_target_pairs={{0,3},{1,0},{2,1},{3,2},{4,7},{5,4},{6,5},{7,6},{8,11},{9,8},{10,9... | collective-permute-start | bytes 786440 | tf_op jit(solution)/shard_map/ppermute | solution.py:28
  39.7 8.4 %collective-permute-start.2 = (bf16[16,32,256]{2,1,0:T(8,128)(2,1)S(1)}, bf16[16,32,256]{2,1,0:T(8,128)(2,1)S(1)}, u32[]{:S(2)}, u32[]{:S(2)}) collective-permute-start(bf16[16,32,256]{2,1,0:T(8,128)(2,1)S(1)} %slice.125), channel_id=1, source_target_pairs={{0,1},{1,2},{2,3},{3,0},{4,5},{5,6},{6,7},{7,4},{8,9},{9,10},{10,1... | collective-permute-start | bytes 786440 | tf_op jit(solution)/shard_map/ppermute | solution.py:28
  49.8 17.9 %collective-permute-start.4 = (bf16[32,32,256]{2,1,0:T(8,128)(2,1)}, bf16[32,32,256]{2,1,0:T(8,128)(2,1)S(1)}, u32[]{:S(2)}, u32[]{:S(2)}) collective-permute-start(bf16[32,32,256]{2,1,0:T(8,128)(2,1)} %get-tuple-element.39), channel_id=1, source_target_pairs={{0,1},{1,2},{2,3},{3,0},{4,5},{5,6},{6,7},{7,4},{8,9},{9,10},{10,1... | collective-permute-start | bytes 1572872 | tf_op jit(solution)/shard_map/ppermute | solution.py:28
  49.9 17.9 %collective-permute-start.5 = (bf16[32,32,256]{2,1,0:T(8,128)(2,1)}, bf16[32,32,256]{2,1,0:T(8,128)(2,1)S(1)}, u32[]{:S(2)}, u32[]{:S(2)}) collective-permute-start(bf16[32,32,256]{2,1,0:T(8,128)(2,1)} %get-tuple-element.40), channel_id=1, source_target_pairs={{0,3},{1,0},{2,1},{3,2},{4,7},{5,4},{6,5},{7,6},{8,11},{9,8},{10,9... | collective-permute-start | bytes 1572872 | tf_op jit(solution)/shard_map/ppermute | solution.py:28
  68.6 11.5 %collective-permute-start.10 = (bf16[16,32,256]{2,1,0:T(8,128)(2,1)}, bf16[16,32,256]{2,1,0:T(8,128)(2,1)S(1)}, u32[]{:S(2)}, u32[]{:S(2)}) collective-permute-start(bf16[16,32,256]{2,1,0:T(8,128)(2,1)} %slice_select_fusion.3), channel_id=1, source_target_pairs={{0,1},{1,2},{2,3},{3,0},{4,5},{5,6},{6,7},{7,4},{8,9},{9,10},{10,1... | collective-permute-start | bytes 786440 | tf_op jit(solution)/shard_map/ppermute | solution.py:28
  70.5 12.0 %collective-permute-start.11 = (bf16[16,32,256]{2,1,0:T(8,128)(2,1)}, bf16[16,32,256]{2,1,0:T(8,128)(2,1)}, u32[]{:S(2)}, u32[]{:S(2)}) collective-permute-start(bf16[16,32,256]{2,1,0:T(8,128)(2,1)} %slice_select_fusion.2), channel_id=1, source_target_pairs={{0,3},{1,0},{2,1},{3,2},{4,7},{5,4},{6,5},{7,6},{8,11},{9,8},{10,9... | collective-permute-start | bytes 786440 | tf_op jit(solution)/shard_map/ppermute | solution.py:28
  75.4 15.7 %collective-permute-start.6 = (bf16[33,32,256]{2,1,0:T(8,128)(2,1)}, bf16[33,32,256]{2,1,0:T(8,128)(2,1)S(1)}, u32[]{:S(2)}, u32[]{:S(2)}) collective-permute-start(bf16[33,32,256]{2,1,0:T(8,128)(2,1)} %get-tuple-element.42), channel_id=1, source_target_pairs={{0,3},{1,0},{2,1},{3,2},{4,7},{5,4},{6,5},{7,6},{8,11},{9,8},{10,9... | collective-permute-start | bytes 1622024 | tf_op jit(solution)/shard_map/ppermute | solution.py:28
  77.4 13.7 %collective-permute-start.7 = (bf16[33,32,256]{2,1,0:T(8,128)(2,1)}, bf16[33,32,256]{2,1,0:T(8,128)(2,1)S(1)}, u32[]{:S(2)}, u32[]{:S(2)}) collective-permute-start(bf16[33,32,256]{2,1,0:T(8,128)(2,1)} %get-tuple-element.44), channel_id=1, source_target_pairs={{0,1},{1,2},{2,3},{3,0},{4,5},{5,6},{6,7},{7,4},{8,9},{9,10},{10,1... | collective-permute-start | bytes 1622024 | tf_op jit(solution)/shard_map/ppermute | solution.py:28
  84.3 16.5 %all-to-all-start.3 = ((bf16[32,32,256]{2,1,0:T(8,128)(2,1)}), bf16[32,32,256]{2,1,0:T(8,128)(2,1)S(1)}, u32[]{:S(2)}, u32[]{:S(2)}) async-start(bf16[32,32,256]{2,1,0:T(8,128)(2,1)} %pad_maximum_fusion.1), calls=%async_computation.3 | async-start | bytes 1048576 | tf_op jit(solution)/shard_map/all_to_all | solution.py:32
  92.1 12.4 %collective-permute-start.8 = (bf16[17,32,256]{2,1,0:T(8,128)(2,1)}, bf16[17,32,256]{2,1,0:T(8,128)(2,1)}, u32[]{:S(2)}, u32[]{:S(2)}) collective-permute-start(bf16[17,32,256]{2,1,0:T(8,128)(2,1)} %get-tuple-element.76), channel_id=1, source_target_pairs={{0,1},{1,2},{2,3},{3,0},{4,5},{5,6},{6,7},{7,4},{8,9},{9,10},{10,1... | collective-permute-start | bytes 835592 | tf_op jit(solution)/shard_map/ppermute | solution.py:28
  93.8 11.4 %collective-permute-start.9 = (bf16[17,32,256]{2,1,0:T(8,128)(2,1)S(1)}, bf16[17,32,256]{2,1,0:T(8,128)(2,1)}, u32[]{:S(2)}, u32[]{:S(2)}) collective-permute-start(bf16[17,32,256]{2,1,0:T(8,128)(2,1)S(1)} %get-tuple-element.75), channel_id=1, source_target_pairs={{0,3},{1,0},{2,1},{3,2},{4,7},{5,4},{6,5},{7,6},{8,11},{9,8},{10,9... | collective-permute-start | bytes 835592 | tf_op jit(solution)/shard_map/ppermute | solution.py:28
  100.8 15.1 %collective-permute-start.13 = (bf16[32,32,256]{2,1,0:T(8,128)(2,1)S(1)}, bf16[32,32,256]{2,1,0:T(8,128)(2,1)S(1)}, u32[]{:S(2)}, u32[]{:S(2)}) collective-permute-start(bf16[32,32,256]{2,1,0:T(8,128)(2,1)S(1)} %all-to-all-done.3.refs_2_), channel_id=1, source_target_pairs={{0,3},{1,0},{2,1},{3,2},{4,7},{5,4},{6,5},{7,6},{8,11},{9,8},{10,9... | collective-permute-start | bytes 1572872 | tf_op jit(solution)/shard_map/ppermute | solution.py:28
  104.5 14.8 %collective-permute-start.12 = (bf16[32,32,256]{2,1,0:T(8,128)(2,1)S(1)}, bf16[32,32,256]{2,1,0:T(8,128)(2,1)S(1)}, u32[]{:S(2)}, u32[]{:S(2)}) collective-permute-start(bf16[32,32,256]{2,1,0:T(8,128)(2,1)S(1)} %all-to-all-done.3.refs_2_), channel_id=1, source_target_pairs={{0,1},{1,2},{2,3},{3,0},{4,5},{5,6},{6,7},{7,4},{8,9},{9,10},{10,1... | collective-permute-start | bytes 1572872 | tf_op jit(solution)/shard_map/ppermute | solution.py:28
  107.3 20.9 %all-to-all-start.2 = ((bf16[32,48,256]{2,1,0:T(8,128)(2,1)}), bf16[32,48,256]{2,1,0:T(8,128)(2,1)S(1)}, u32[]{:S(2)}, u32[]{:S(2)}) async-start(bf16[32,48,256]{2,1,0:T(8,128)(2,1)} %pad_maximum_fusion), calls=%async_computation.2 | async-start | bytes 1572864 | tf_op jit(solution)/shard_map/all_to_all | solution.py:32
  120.8 16.2 %collective-permute-start.21 = (bf16[16,32,256]{2,1,0:T(8,128)(2,1)}, bf16[16,32,256]{2,1,0:T(8,128)(2,1)S(1)}, u32[]{:S(2)}, u32[]{:S(2)}) collective-permute-start(bf16[16,32,256]{2,1,0:T(8,128)(2,1)} %slice.123), channel_id=1, source_target_pairs={{0,3},{1,0},{2,1},{3,2},{4,7},{5,4},{6,5},{7,6},{8,11},{9,8},{10,9... | collective-permute-start | bytes 786440 | tf_op jit(solution)/shard_map/ppermute | solution.py:28
  121.1 23.2 %collective-permute-start.20 = (bf16[16,32,256]{2,1,0:T(8,128)(2,1)}, bf16[16,32,256]{2,1,0:T(8,128)(2,1)S(1)}, u32[]{:S(2)}, u32[]{:S(2)}) collective-permute-start(bf16[16,32,256]{2,1,0:T(8,128)(2,1)} %slice.122), channel_id=1, source_target_pairs={{0,1},{1,2},{2,3},{3,0},{4,5},{5,6},{6,7},{7,4},{8,9},{9,10},{10,1... | collective-permute-start | bytes 786440 | tf_op jit(solution)/shard_map/ppermute | solution.py:28
  128.3 12.0 %collective-permute-start.18 = (bf16[16,32,256]{2,1,0:T(8,128)(2,1)S(1)}, bf16[16,32,256]{2,1,0:T(8,128)(2,1)S(1)}, u32[]{:S(2)}, u32[]{:S(2)}) collective-permute-start(bf16[16,32,256]{2,1,0:T(8,128)(2,1)S(1)} %get-tuple-element.67.refs_6_), channel_id=1, source_target_pairs={{0,3},{1,0},{2,1},{3,2},{4,7},{5,4},{6,5},{7,6},{8,11},{9,8},{10,9... | collective-permute-start | bytes 786440 | tf_op jit(solution)/shard_map/ppermute | solution.py:28
  129.9 16.6 %collective-permute-start.17 = (bf16[16,32,256]{2,1,0:T(8,128)(2,1)S(1)}, bf16[16,32,256]{2,1,0:T(8,128)(2,1)S(1)}, u32[]{:S(2)}, u32[]{:S(2)}) collective-permute-start(bf16[16,32,256]{2,1,0:T(8,128)(2,1)S(1)} %get-tuple-element.67.refs_6_), channel_id=1, source_target_pairs={{0,1},{1,2},{2,3},{3,0},{4,5},{5,6},{6,7},{7,4},{8,9},{9,10},{10,1... | collective-permute-start | bytes 786440 | tf_op jit(solution)/shard_map/ppermute | solution.py:28
  131.1 12.7 %collective-permute-start.14 = (bf16[16,32,256]{2,1,0:T(8,128)(2,1)S(1)}, bf16[16,32,256]{2,1,0:T(8,128)(2,1)S(1)}, u32[]{:S(2)}, u32[]{:S(2)}) collective-permute-start(bf16[16,32,256]{2,1,0:T(8,128)(2,1)S(1)} %get-tuple-element.68.refs_2_), channel_id=1, source_target_pairs={{0,1},{1,2},{2,3},{3,0},{4,5},{5,6},{6,7},{7,4},{8,9},{9,10},{10,1... | collective-permute-start | bytes 786440 | tf_op jit(solution)/shard_map/ppermute | solution.py:28
  137.0 10.0 %collective-permute-start.15 = (bf16[16,32,256]{2,1,0:T(8,128)(2,1)S(1)}, bf16[16,32,256]{2,1,0:T(8,128)(2,1)S(1)}, u32[]{:S(2)}, u32[]{:S(2)}) collective-permute-start(bf16[16,32,256]{2,1,0:T(8,128)(2,1)S(1)} %get-tuple-element.68.refs_2_), channel_id=1, source_target_pairs={{0,3},{1,0},{2,1},{3,2},{4,7},{5,4},{6,5},{7,6},{8,11},{9,8},{10,9... | collective-permute-start | bytes 786440 | tf_op jit(solution)/shard_map/ppermute | solution.py:28
  140.3 9.5 %collective-permute-start.19 = (bf16[16,32,256]{2,1,0:T(8,128)(2,1)S(1)}, bf16[16,32,256]{2,1,0:T(8,128)(2,1)S(1)}, u32[]{:S(2)}, u32[]{:S(2)}) collective-permute-start(bf16[16,32,256]{2,1,0:T(8,128)(2,1)S(1)} %collective-permute-done.18.refs_8_), channel_id=1, source_target_pairs={{0,3},{1,0},{2,1},{3,2},{4,7},{5,4},{6,5},{7,6},{8,11},{9,8},{10,9... | collective-permute-start | bytes 786440 | tf_op jit(solution)/shard_map/ppermute | solution.py:28
  (13 other events, 113.0 us)

commit v6 on v5

--- a/solution.py
+++ b/solution.py
@@ -125,25 +125,31 @@
     @pl.when(owned)
     def _():
         first = block_copies(me, pieces, block, sems)
-        first.append(pltpu.make_async_copy(left.at[slot], left_held, sems.at[8]))
+        tops = [pl.ds(i * wide, wide) for i in range(2)]
+        halves = [
+            pltpu.make_async_copy(left.at[slot, span], left_held.at[span], sems.at[7 + i])
+            for i, span in enumerate(tops)
+        ]
         second = []
         for place, offset in enumerate((2, 1, 3, 0)):
             column = pl.multiple_of(lax.rem(me + offset, 4) * width, width)
             source = right.at[slot, :, pl.ds(column, width)]
             target = right_held.at[:, pl.ds(place * width, width)]
             second.append(pltpu.make_async_copy(source, target, sems.at[9 + place]))
-        for copy in first + second:
+        for copy in first + halves:
             copy.start()
         for copy in first:
             copy.wait()
-
-        @pl.loop(0, 2)
-        def _(i):
-            columns = pl.ds(pl.multiple_of(i * wide, wide), wide)
-            values = block[:, :, columns].reshape(order, wide)
-            product = jnp.dot(left_held[...], values, preferred_element_type=F32)
-            middle[:, columns] = product.astype(BF16)
-            grad_sum[...] += sum_squares(values)
+        for i, span in enumerate(tops):
+            halves[i].wait()
+            if i == 0:
+                for copy in second:
+                    copy.start()
+            values = block[...].reshape(order, order)
+            product = jnp.dot(left_held[span, :], values, preferred_element_type=F32)
+            middle[span, :] = product.astype(BF16)
+            squares = sum_squares(values[i * wide : (i + 1) * wide])
+            grad_sum[...] += squares[:, :wide] + squares[:, wide:]
 
         for copy in second:
             copy.wait()

time: 154 us -> 154 us (level)
  starting transfers between devices: 51.4 us -> 53.8 us
  waiting for transfers between devices: 43.5 us -> 41.6 us
    ppermute x22, waiting for transfers between devices: 33.9 us -> 30.8 us  [shift(): lax.ppermute(x, 'replica', [(i, (i + step) % count) for i in range(count)])]
  transfers between devices with their start and end apart: 25 -> 25, of which waited for: 14 -> 15; matrix products, arithmetic and copies ran while one was open for 9% -> 9% of each run, Pallas kernels for 12% -> 12%
where the time goes in v6:
time: 154 us
  starting transfers between devices  53.8 us (35%)
  waiting for transfers between devices  41.6 us (27%)
  Pallas kernels  21.4 us (14%)
  blocking collectives  20 us (13%)
  other arithmetic  8.52 us (6%)
  local copies, waits for them, and re-layouts  6.65 us (4%)
  between operations  2.48 us (2%)
    ppermute x22, starting transfers between devices, shift(): lax.ppermute(x, 'replica', [(i, (i + step) % count) for i in range(count)])  39.5 us
    ppermute x22, waiting for transfers between devices, shift(): lax.ppermute(x, 'replica', [(i, (i + step) % count) for i in range(count)])  30.8 us
    all_to_all x1, blocking collectives, over_dp(): return lax.all_to_all(x, 'dp', split_axis=0, concat_axis=0, tiled=True)  20 us
    all_to_all x3, starting transfers between devices, over_dp(): return lax.all_to_all(x, 'dp', split_axis=0, concat_axis=0, tiled=True)  14.2 us
    pallas_call x2, Pallas kernels, update_stats(): pl.pallas_call(lambda *refs: stats_kernel(len(pieces), *refs), out_shape=...  11 us
    all_to_all x3, waiting for transfers between devices, over_dp(): return lax.all_to_all(x, 'dp', split_axis=0, concat_axis=0, tiled=True)  10.8 us
    pallas_call x2, Pallas kernels, scale_rows(): pl.pallas_call(lambda *refs: scale_kernel(which, slots, len(pieces), *ref...  4.54 us
    pallas_call x2, Pallas kernels, apply_roots(): pl.pallas_call(lambda *refs: roots_kernel(len(pieces), before is not None...  3.45 us
  transfers between devices with their start and end apart: 25, of which 15 were waited for; matrix products, arithmetic and copies ran while one was open for 9% of the time, Pallas kernels for 12%

profile of v6, /device:TPU:0, one launch (start us, length us, event | category | flops | bytes accessed | tf_op | source)
XLA Modules:
  0.0 154.3 jit_solution(3702026379189373053)
XLA Ops:
  1.7 20.0 %all_to_all.20.refs_3_.refs_1_ = bf16[32,32,256]{2,1,0:T(8,128)(2,1)S(1)} all-to-all(bf16[32,32,256]{2,1,0:T(8,128)(2,1)S(1)} %dynamic-slice_bitcast_fusion), channel_id=1, replica_groups=mesh['dp'=32,'replica'=4] {'dp'}, dimensions={0} | all-to-all | bytes 1048576 | tf_op jit(solution)/shard_map/all_to_all | solution.py:32
  21.7 2.8 %collective-permute-start.1 = (bf16[32,32,256]{2,1,0:T(8,128)(2,1)S(1)}, bf16[32,32,256]{2,1,0:T(8,128)(2,1)S(1)}, u32[]{:S(2)}, u32[]{:S(2)}) collective-permute-start(bf16[32,32,256]{2,1,0:T(8,128)(2,1)S(1)} %all_to_all.20.refs_3_.refs_1_), channel_id=1, source_target_pairs={{0,3},{1,0},{2,1},{3,2},{4,7},{5,4},{6,5},{7,6},{8,11},{9,8},{10,9... | collective-permute-start | bytes 1572872 | tf_op jit(solution)/shard_map/ppermute | solution.py:28
  24.5 2.4 %pick.1 = bf16[32,32,1024]{2,1,0:T(8,128)(2,1)} custom-call(bf16[32,2,32,1024]{3,2,1,0:T(8,128)(2,1)} %bitcast.21), custom_call_target="tpu_custom_call" | custom-call | bytes 8388608 | tf_op jit(solution)/shard_map/pick/pallas_call | solution.py:64
  26.9 4.8 %all-to-all-start = ((bf16[32,32,1024]{2,1,0:T(8,128)(2,1)}), bf16[32,32,1024]{2,1,0:T(8,128)(2,1)}, u32[]{:S(2)}, u32[]{:S(2)}) async-start(bf16[32,32,1024]{2,1,0:T(8,128)(2,1)} %pick.1), calls=%async_computation | async-start | bytes 4194304 | tf_op jit(solution)/shard_map/all_to_all | solution.py:32
  31.7 4.2 %collective-permute-done.1.refs_5_.refs_3_ = bf16[32,32,256]{2,1,0:T(8,128)(2,1)S(1)} collective-permute-done((bf16[32,32,256]{2,1,0:T(8,128)(2,1)S(1)}, bf16[32,32,256]{2,1,0:T(8,128)(2,1)S(1)}, u32[]{:S(2)}, u32[]{:S(2)}) %collective-permute-start.1) | collective-permute-done | bytes 524320 | tf_op jit(solution)/shard_map/ppermute | solution.py:28
  35.9 3.8 %collective-permute-start.3 = (bf16[16,32,256]{2,1,0:T(8,128)(2,1)S(1)}, bf16[16,32,256]{2,1,0:T(8,128)(2,1)S(1)}, u32[]{:S(2)}, u32[]{:S(2)}) collective-permute-start(bf16[16,32,256]{2,1,0:T(8,128)(2,1)S(1)} %slice.126), channel_id=1, source_target_pairs={{0,3},{1,0},{2,1},{3,2},{4,7},{5,4},{6,5},{7,6},{8,11},{9,8},{10,9... | collective-permute-start | bytes 786440 | tf_op jit(solution)/shard_map/ppermute | solution.py:28
  45.0 3.2 %collective-permute-done.2.refs_6_.refs_4_ = bf16[16,32,256]{2,1,0:T(8,128)(2,1)S(1)} collective-permute-done((bf16[16,32,256]{2,1,0:T(8,128)(2,1)S(1)}, bf16[16,32,256]{2,1,0:T(8,128)(2,1)S(1)}, u32[]{:S(2)}, u32[]{:S(2)}) %collective-permute-start.2) | collective-permute-done | bytes 262176 | tf_op jit(solution)/shard_map/ppermute | solution.py:28
  49.9 6.7 %collective-permute-start.5 = (bf16[32,32,256]{2,1,0:T(8,128)(2,1)}, bf16[32,32,256]{2,1,0:T(8,128)(2,1)S(1)}, u32[]{:S(2)}, u32[]{:S(2)}) collective-permute-start(bf16[32,32,256]{2,1,0:T(8,128)(2,1)} %get-tuple-element.40), channel_id=1, source_target_pairs={{0,3},{1,0},{2,1},{3,2},{4,7},{5,4},{6,5},{7,6},{8,11},{9,8},{10,9... | collective-permute-start | bytes 1572872 | tf_op jit(solution)/shard_map/ppermute | solution.py:28
  56.7 5.0 %all-to-all-done.refs_3_.refs_1_ = bf16[32,32,1024]{2,1,0:T(8,128)(2,1)} async-done(((bf16[32,32,1024]{2,1,0:T(8,128)(2,1)}), bf16[32,32,1024]{2,1,0:T(8,128)(2,1)}, u32[]{:S(2)}, u32[]{:S(2)}) %all-to-all-start) | async-done | bytes 2097184 | tf_op jit(solution)/shard_map/all_to_all | solution.py:32
  66.3 2.5 %collective-permute-start.10 = (bf16[16,32,256]{2,1,0:T(8,128)(2,1)}, bf16[16,32,256]{2,1,0:T(8,128)(2,1)S(1)}, u32[]{:S(2)}, u32[]{:S(2)}) collective-permute-start(bf16[16,32,256]{2,1,0:T(8,128)(2,1)} %slice_select_fusion.3), channel_id=1, source_target_pairs={{0,1},{1,2},{2,3},{3,0},{4,5},{5,6},{6,7},{7,4},{8,9},{9,10},{10,1... | collective-permute-start | bytes 786440 | tf_op jit(solution)/shard_map/ppermute | solution.py:28
  69.5 5.5 %collective-permute-start.11 = (bf16[16,32,256]{2,1,0:T(8,128)(2,1)}, bf16[16,32,256]{2,1,0:T(8,128)(2,1)}, u32[]{:S(2)}, u32[]{:S(2)}) collective-permute-start(bf16[16,32,256]{2,1,0:T(8,128)(2,1)} %slice_select_fusion.2), channel_id=1, source_target_pairs={{0,3},{1,0},{2,1},{3,2},{4,7},{5,4},{6,5},{7,6},{8,11},{9,8},{10,9... | collective-permute-start | bytes 786440 | tf_op jit(solution)/shard_map/ppermute | solution.py:28
  77.1 2.6 %collective-permute-done.10 = bf16[16,32,256]{2,1,0:T(8,128)(2,1)S(1)} collective-permute-done((bf16[16,32,256]{2,1,0:T(8,128)(2,1)}, bf16[16,32,256]{2,1,0:T(8,128)(2,1)S(1)}, u32[]{:S(2)}, u32[]{:S(2)}) %collective-permute-start.10) | collective-permute-done | bytes 262176 | tf_op jit(solution)/shard_map/ppermute | solution.py:28
  79.7 2.4 %collective-permute-done.11 = bf16[16,32,256]{2,1,0:T(8,128)(2,1)} collective-permute-done((bf16[16,32,256]{2,1,0:T(8,128)(2,1)}, bf16[16,32,256]{2,1,0:T(8,128)(2,1)}, u32[]{:S(2)}, u32[]{:S(2)}) %collective-permute-start.11) | collective-permute-done | bytes 262176 | tf_op jit(solution)/shard_map/ppermute | solution.py:28
  83.9 5.5 %all-to-all-start.3 = ((bf16[32,32,256]{2,1,0:T(8,128)(2,1)}), bf16[32,32,256]{2,1,0:T(8,128)(2,1)S(1)}, u32[]{:S(2)}, u32[]{:S(2)}) async-start(bf16[32,32,256]{2,1,0:T(8,128)(2,1)} %pad_maximum_fusion.1), calls=%async_computation.3 | async-start | bytes 1048576 | tf_op jit(solution)/shard_map/all_to_all | solution.py:32
  95.4 5.8 %all-to-all-done.3.refs_2_ = bf16[32,32,256]{2,1,0:T(8,128)(2,1)S(1)} async-done(((bf16[32,32,256]{2,1,0:T(8,128)(2,1)}), bf16[32,32,256]{2,1,0:T(8,128)(2,1)S(1)}, u32[]{:S(2)}, u32[]{:S(2)}) %all-to-all-start.3) | async-done | bytes 524320 | tf_op jit(solution)/shard_map/all_to_all | solution.py:32
  101.2 3.7 %collective-permute-start.13 = (bf16[32,32,256]{2,1,0:T(8,128)(2,1)S(1)}, bf16[32,32,256]{2,1,0:T(8,128)(2,1)S(1)}, u32[]{:S(2)}, u32[]{:S(2)}) collective-permute-start(bf16[32,32,256]{2,1,0:T(8,128)(2,1)S(1)} %all-to-all-done.3.refs_2_), channel_id=1, source_target_pairs={{0,3},{1,0},{2,1},{3,2},{4,7},{5,4},{6,5},{7,6},{8,11},{9,8},{10,9... | collective-permute-start | bytes 1572872 | tf_op jit(solution)/shard_map/ppermute | solution.py:28
  107.8 3.9 %all-to-all-start.2 = ((bf16[32,48,256]{2,1,0:T(8,128)(2,1)}), bf16[32,48,256]{2,1,0:T(8,128)(2,1)S(1)}, u32[]{:S(2)}, u32[]{:S(2)}) async-start(bf16[32,48,256]{2,1,0:T(8,128)(2,1)} %pad_maximum_fusion), calls=%async_computation.2 | async-start | bytes 1572864 | tf_op jit(solution)/shard_map/all_to_all | solution.py:32
  111.7 4.6 %collective-permute-done.13.refs_4_ = bf16[32,32,256]{2,1,0:T(8,128)(2,1)S(1)} collective-permute-done((bf16[32,32,256]{2,1,0:T(8,128)(2,1)S(1)}, bf16[32,32,256]{2,1,0:T(8,128)(2,1)S(1)}, u32[]{:S(2)}, u32[]{:S(2)}) %collective-permute-start.13) | collective-permute-done | bytes 524320 | tf_op jit(solution)/shard_map/ppermute | solution.py:28
  116.4 3.4 %collective-permute-done.12.refs_3_ = bf16[32,32,256]{2,1,0:T(8,128)(2,1)S(1)} collective-permute-done((bf16[32,32,256]{2,1,0:T(8,128)(2,1)S(1)}, bf16[32,32,256]{2,1,0:T(8,128)(2,1)S(1)}, u32[]{:S(2)}, u32[]{:S(2)}) %collective-permute-start.12) | collective-permute-done | bytes 524320 | tf_op jit(solution)/shard_map/ppermute | solution.py:28
  123.3 5.4 %stats.2 = (f32[2,256,1024]{2,1,0:T(8,128)}, f32[2,256,1024]{2,1,0:T(8,128)}) custom-call(s32[4]{0:T(128)} %copy-done.3, bf16[32,32,256]{2,1,0:T(8,128)(2,1)} %copy-done, bf16[32,32,256]{2,1,0:T(8,128)(2,1)} %copy-done.1, bf16[32,32,256]{2,1,0:T(8,128)(2,1)} %copy-done.8, bf16[16,32,256]{2,1,0:T(8,128)(2,1)} %copy-done.5, bf16[16,32,256]{2,1,0:T(8,128)(2,1)} %copy-done.4, ...), custom_call_target="tpu_custom_call" | custom-call | flops 6442450944 | bytes 6291456 | tf_op jit(solution)/shard_map/stats/pallas_call | solution.py:261
  131.6 5.6 %stats.3 = (f32[2,256,1024]{2,1,0:T(8,128)}, f32[2,256,1024]{2,1,0:T(8,128)}) custom-call(s32[4]{0:T(128)} %copy-done.2, bf16[32,32,1024]{2,1,0:T(8,128)(2,1)} %all-to-all-done.refs_3_.refs_1_, f32[2,256,1024]{2,1,0:T(8,128)} %refs_2_, f32[2,256,1024]{2,1,0:T(8,128)} %refs_3_, ...), custom_call_target="tpu_custom_call", output_to_operand_aliasing={{0}: (4, {}), {1}: (5, {})} | custom-call | flops 6442450944 | bytes 6291456 | tf_op jit(solution)/shard_map/stats/pallas_call | solution.py:261
  137.5 3.3 %collective-permute-start.15 = (bf16[16,32,256]{2,1,0:T(8,128)(2,1)S(1)}, bf16[16,32,256]{2,1,0:T(8,128)(2,1)S(1)}, u32[]{:S(2)}, u32[]{:S(2)}) collective-permute-start(bf16[16,32,256]{2,1,0:T(8,128)(2,1)S(1)} %get-tuple-element.68.refs_2_), channel_id=1, source_target_pairs={{0,3},{1,0},{2,1},{3,2},{4,7},{5,4},{6,5},{7,6},{8,11},{9,8},{10,9... | collective-permute-start | bytes 786440 | tf_op jit(solution)/shard_map/ppermute | solution.py:28
  144.7 2.3 %scale.2.refs_10_ = bf16[32,2,32,1024]{3,2,1,0:T(8,128)(2,1)} custom-call(f32[64]{0:T(128)S(1)} %select_reduce_fusion.refs_0_, s32[1]{0:T(128)} %bitcast.2.refs_1_, bf16[32,32,256]{2,1,0:T(8,128)(2,1)S(1)} %all-to-all-done.3.refs_2_, bf16[32,32,256]{2,1,0:T(8,128)(2,1)S(1)} %collective-permute-done.12.refs_3_, ...), custom_call_target="tpu_custom_call" | custom-call | bytes 12582912 | tf_op jit(solution)/shard_map/scale/pallas_call | solution.py:314
  147.4 2.8 %collective-permute-done.19.refs_9_ = bf16[16,32,256]{2,1,0:T(8,128)(2,1)S(1)} collective-permute-done((bf16[16,32,256]{2,1,0:T(8,128)(2,1)S(1)}, bf16[16,32,256]{2,1,0:T(8,128)(2,1)S(1)}, u32[]{:S(2)}, u32[]{:S(2)}) %collective-permute-start.19) | collective-permute-done | bytes 262176 | tf_op jit(solution)/shard_map/ppermute | solution.py:28
  (98 shorter events, 39.9 us)
Async XLA Ops:
  21.7 14.2 %collective-permute-start.1 = (bf16[32,32,256]{2,1,0:T(8,128)(2,1)S(1)}, bf16[32,32,256]{2,1,0:T(8,128)(2,1)S(1)}, u32[]{:S(2)}, u32[]{:S(2)}) collective-permute-start(bf16[32,32,256]{2,1,0:T(8,128)(2,1)S(1)} %all_to_all.20.refs_3_.refs_1_), channel_id=1, source_target_pairs={{0,3},{1,0},{2,1},{3,2},{4,7},{5,4},{6,5},{7,6},{8,11},{9,8},{10,9... | collective-permute-start | bytes 1572872 | tf_op jit(solution)/shard_map/ppermute | solution.py:28
  24.5 15.2 %collective-permute-start = (bf16[32,32,256]{2,1,0:T(8,128)(2,1)S(1)}, bf16[32,32,256]{2,1,0:T(8,128)(2,1)S(1)}, u32[]{:S(2)}, u32[]{:S(2)}) collective-permute-start(bf16[32,32,256]{2,1,0:T(8,128)(2,1)S(1)} %all_to_all.20.refs_3_.refs_1_), channel_id=1, source_target_pairs={{0,1},{1,2},{2,3},{3,0},{4,5},{5,6},{6,7},{7,4},{8,9},{9,10},{10,1... | collective-permute-start | bytes 1572872 | tf_op jit(solution)/shard_map/ppermute | solution.py:28
  26.9 34.7 %all-to-all-start = ((bf16[32,32,1024]{2,1,0:T(8,128)(2,1)}), bf16[32,32,1024]{2,1,0:T(8,128)(2,1)}, u32[]{:S(2)}, u32[]{:S(2)}) async-start(bf16[32,32,1024]{2,1,0:T(8,128)(2,1)} %pick.1), calls=%async_computation | async-start | bytes 4194304 | tf_op jit(solution)/shard_map/all_to_all | solution.py:32
  35.9 9.0 %collective-permute-start.3 = (bf16[16,32,256]{2,1,0:T(8,128)(2,1)S(1)}, bf16[16,32,256]{2,1,0:T(8,128)(2,1)S(1)}, u32[]{:S(2)}, u32[]{:S(2)}) collective-permute-start(bf16[16,32,256]{2,1,0:T(8,128)(2,1)S(1)} %slice.126), channel_id=1, source_target_pairs={{0,3},{1,0},{2,1},{3,2},{4,7},{5,4},{6,5},{7,6},{8,11},{9,8},{10,9... | collective-permute-start | bytes 786440 | tf_op jit(solution)/shard_map/ppermute | solution.py:28
  39.7 8.4 %collective-permute-start.2 = (bf16[16,32,256]{2,1,0:T(8,128)(2,1)S(1)}, bf16[16,32,256]{2,1,0:T(8,128)(2,1)S(1)}, u32[]{:S(2)}, u32[]{:S(2)}) collective-permute-start(bf16[16,32,256]{2,1,0:T(8,128)(2,1)S(1)} %slice.125), channel_id=1, source_target_pairs={{0,1},{1,2},{2,3},{3,0},{4,5},{5,6},{6,7},{7,4},{8,9},{9,10},{10,1... | collective-permute-start | bytes 786440 | tf_op jit(solution)/shard_map/ppermute | solution.py:28
  49.9 14.1 %collective-permute-start.4 = (bf16[32,32,256]{2,1,0:T(8,128)(2,1)}, bf16[32,32,256]{2,1,0:T(8,128)(2,1)S(1)}, u32[]{:S(2)}, u32[]{:S(2)}) collective-permute-start(bf16[32,32,256]{2,1,0:T(8,128)(2,1)} %get-tuple-element.39), channel_id=1, source_target_pairs={{0,1},{1,2},{2,3},{3,0},{4,5},{5,6},{6,7},{7,4},{8,9},{9,10},{10,1... | collective-permute-start | bytes 1572872 | tf_op jit(solution)/shard_map/ppermute | solution.py:28
  49.9 15.6 %collective-permute-start.5 = (bf16[32,32,256]{2,1,0:T(8,128)(2,1)}, bf16[32,32,256]{2,1,0:T(8,128)(2,1)S(1)}, u32[]{:S(2)}, u32[]{:S(2)}) collective-permute-start(bf16[32,32,256]{2,1,0:T(8,128)(2,1)} %get-tuple-element.40), channel_id=1, source_target_pairs={{0,3},{1,0},{2,1},{3,2},{4,7},{5,4},{6,5},{7,6},{8,11},{9,8},{10,9... | collective-permute-start | bytes 1572872 | tf_op jit(solution)/shard_map/ppermute | solution.py:28
  66.3 13.4 %collective-permute-start.10 = (bf16[16,32,256]{2,1,0:T(8,128)(2,1)}, bf16[16,32,256]{2,1,0:T(8,128)(2,1)S(1)}, u32[]{:S(2)}, u32[]{:S(2)}) collective-permute-start(bf16[16,32,256]{2,1,0:T(8,128)(2,1)} %slice_select_fusion.3), channel_id=1, source_target_pairs={{0,1},{1,2},{2,3},{3,0},{4,5},{5,6},{6,7},{7,4},{8,9},{9,10},{10,1... | collective-permute-start | bytes 786440 | tf_op jit(solution)/shard_map/ppermute | solution.py:28
  69.5 12.6 %collective-permute-start.11 = (bf16[16,32,256]{2,1,0:T(8,128)(2,1)}, bf16[16,32,256]{2,1,0:T(8,128)(2,1)}, u32[]{:S(2)}, u32[]{:S(2)}) collective-permute-start(bf16[16,32,256]{2,1,0:T(8,128)(2,1)} %slice_select_fusion.2), channel_id=1, source_target_pairs={{0,3},{1,0},{2,1},{3,2},{4,7},{5,4},{6,5},{7,6},{8,11},{9,8},{10,9... | collective-permute-start | bytes 786440 | tf_op jit(solution)/shard_map/ppermute | solution.py:28
  75.0 15.7 %collective-permute-start.6 = (bf16[33,32,256]{2,1,0:T(8,128)(2,1)}, bf16[33,32,256]{2,1,0:T(8,128)(2,1)S(1)}, u32[]{:S(2)}, u32[]{:S(2)}) collective-permute-start(bf16[33,32,256]{2,1,0:T(8,128)(2,1)} %get-tuple-element.42), channel_id=1, source_target_pairs={{0,3},{1,0},{2,1},{3,2},{4,7},{5,4},{6,5},{7,6},{8,11},{9,8},{10,9... | collective-permute-start | bytes 1622024 | tf_op jit(solution)/shard_map/ppermute | solution.py:28
  77.0 13.7 %collective-permute-start.7 = (bf16[33,32,256]{2,1,0:T(8,128)(2,1)}, bf16[33,32,256]{2,1,0:T(8,128)(2,1)S(1)}, u32[]{:S(2)}, u32[]{:S(2)}) collective-permute-start(bf16[33,32,256]{2,1,0:T(8,128)(2,1)} %get-tuple-element.44), channel_id=1, source_target_pairs={{0,1},{1,2},{2,3},{3,0},{4,5},{5,6},{6,7},{7,4},{8,9},{9,10},{10,1... | collective-permute-start | bytes 1622024 | tf_op jit(solution)/shard_map/ppermute | solution.py:28
  83.9 17.3 %all-to-all-start.3 = ((bf16[32,32,256]{2,1,0:T(8,128)(2,1)}), bf16[32,32,256]{2,1,0:T(8,128)(2,1)S(1)}, u32[]{:S(2)}, u32[]{:S(2)}) async-start(bf16[32,32,256]{2,1,0:T(8,128)(2,1)} %pad_maximum_fusion.1), calls=%async_computation.3 | async-start | bytes 1048576 | tf_op jit(solution)/shard_map/all_to_all | solution.py:32
  91.7 13.3 %collective-permute-start.8 = (bf16[17,32,256]{2,1,0:T(8,128)(2,1)}, bf16[17,32,256]{2,1,0:T(8,128)(2,1)}, u32[]{:S(2)}, u32[]{:S(2)}) collective-permute-start(bf16[17,32,256]{2,1,0:T(8,128)(2,1)} %get-tuple-element.76), channel_id=1, source_target_pairs={{0,1},{1,2},{2,3},{3,0},{4,5},{5,6},{6,7},{7,4},{8,9},{9,10},{10,1... | collective-permute-start | bytes 835592 | tf_op jit(solution)/shard_map/ppermute | solution.py:28
  93.4 12.2 %collective-permute-start.9 = (bf16[17,32,256]{2,1,0:T(8,128)(2,1)S(1)}, bf16[17,32,256]{2,1,0:T(8,128)(2,1)}, u32[]{:S(2)}, u32[]{:S(2)}) collective-permute-start(bf16[17,32,256]{2,1,0:T(8,128)(2,1)S(1)} %get-tuple-element.75), channel_id=1, source_target_pairs={{0,3},{1,0},{2,1},{3,2},{4,7},{5,4},{6,5},{7,6},{8,11},{9,8},{10,9... | collective-permute-start | bytes 835592 | tf_op jit(solution)/shard_map/ppermute | solution.py:28
  101.2 15.1 %collective-permute-start.13 = (bf16[32,32,256]{2,1,0:T(8,128)(2,1)S(1)}, bf16[32,32,256]{2,1,0:T(8,128)(2,1)S(1)}, u32[]{:S(2)}, u32[]{:S(2)}) collective-permute-start(bf16[32,32,256]{2,1,0:T(8,128)(2,1)S(1)} %all-to-all-done.3.refs_2_), channel_id=1, source_target_pairs={{0,3},{1,0},{2,1},{3,2},{4,7},{5,4},{6,5},{7,6},{8,11},{9,8},{10,9... | collective-permute-start | bytes 1572872 | tf_op jit(solution)/shard_map/ppermute | solution.py:28
  104.9 14.8 %collective-permute-start.12 = (bf16[32,32,256]{2,1,0:T(8,128)(2,1)S(1)}, bf16[32,32,256]{2,1,0:T(8,128)(2,1)S(1)}, u32[]{:S(2)}, u32[]{:S(2)}) collective-permute-start(bf16[32,32,256]{2,1,0:T(8,128)(2,1)S(1)} %all-to-all-done.3.refs_2_), channel_id=1, source_target_pairs={{0,1},{1,2},{2,3},{3,0},{4,5},{5,6},{6,7},{7,4},{8,9},{9,10},{10,1... | collective-permute-start | bytes 1572872 | tf_op jit(solution)/shard_map/ppermute | solution.py:28
  107.8 20.9 %all-to-all-start.2 = ((bf16[32,48,256]{2,1,0:T(8,128)(2,1)}), bf16[32,48,256]{2,1,0:T(8,128)(2,1)S(1)}, u32[]{:S(2)}, u32[]{:S(2)}) async-start(bf16[32,48,256]{2,1,0:T(8,128)(2,1)} %pad_maximum_fusion), calls=%async_computation.2 | async-start | bytes 1572864 | tf_op jit(solution)/shard_map/all_to_all | solution.py:32
  121.2 16.2 %collective-permute-start.21 = (bf16[16,32,256]{2,1,0:T(8,128)(2,1)}, bf16[16,32,256]{2,1,0:T(8,128)(2,1)S(1)}, u32[]{:S(2)}, u32[]{:S(2)}) collective-permute-start(bf16[16,32,256]{2,1,0:T(8,128)(2,1)} %slice.123), channel_id=1, source_target_pairs={{0,3},{1,0},{2,1},{3,2},{4,7},{5,4},{6,5},{7,6},{8,11},{9,8},{10,9... | collective-permute-start | bytes 786440 | tf_op jit(solution)/shard_map/ppermute | solution.py:28
  121.5 23.2 %collective-permute-start.20 = (bf16[16,32,256]{2,1,0:T(8,128)(2,1)}, bf16[16,32,256]{2,1,0:T(8,128)(2,1)S(1)}, u32[]{:S(2)}, u32[]{:S(2)}) collective-permute-start(bf16[16,32,256]{2,1,0:T(8,128)(2,1)} %slice.122), channel_id=1, source_target_pairs={{0,1},{1,2},{2,3},{3,0},{4,5},{5,6},{6,7},{7,4},{8,9},{9,10},{10,1... | collective-permute-start | bytes 786440 | tf_op jit(solution)/shard_map/ppermute | solution.py:28
  128.8 12.0 %collective-permute-start.18 = (bf16[16,32,256]{2,1,0:T(8,128)(2,1)S(1)}, bf16[16,32,256]{2,1,0:T(8,128)(2,1)S(1)}, u32[]{:S(2)}, u32[]{:S(2)}) collective-permute-start(bf16[16,32,256]{2,1,0:T(8,128)(2,1)S(1)} %get-tuple-element.67.refs_6_), channel_id=1, source_target_pairs={{0,3},{1,0},{2,1},{3,2},{4,7},{5,4},{6,5},{7,6},{8,11},{9,8},{10,9... | collective-permute-start | bytes 786440 | tf_op jit(solution)/shard_map/ppermute | solution.py:28
  130.4 16.6 %collective-permute-start.17 = (bf16[16,32,256]{2,1,0:T(8,128)(2,1)S(1)}, bf16[16,32,256]{2,1,0:T(8,128)(2,1)S(1)}, u32[]{:S(2)}, u32[]{:S(2)}) collective-permute-start(bf16[16,32,256]{2,1,0:T(8,128)(2,1)S(1)} %get-tuple-element.67.refs_6_), channel_id=1, source_target_pairs={{0,1},{1,2},{2,3},{3,0},{4,5},{5,6},{6,7},{7,4},{8,9},{9,10},{10,1... | collective-permute-start | bytes 786440 | tf_op jit(solution)/shard_map/ppermute | solution.py:28
  131.6 12.7 %collective-permute-start.14 = (bf16[16,32,256]{2,1,0:T(8,128)(2,1)S(1)}, bf16[16,32,256]{2,1,0:T(8,128)(2,1)S(1)}, u32[]{:S(2)}, u32[]{:S(2)}) collective-permute-start(bf16[16,32,256]{2,1,0:T(8,128)(2,1)S(1)} %get-tuple-element.68.refs_2_), channel_id=1, source_target_pairs={{0,1},{1,2},{2,3},{3,0},{4,5},{5,6},{6,7},{7,4},{8,9},{9,10},{10,1... | collective-permute-start | bytes 786440 | tf_op jit(solution)/shard_map/ppermute | solution.py:28
  137.5 10.0 %collective-permute-start.15 = (bf16[16,32,256]{2,1,0:T(8,128)(2,1)S(1)}, bf16[16,32,256]{2,1,0:T(8,128)(2,1)S(1)}, u32[]{:S(2)}, u32[]{:S(2)}) collective-permute-start(bf16[16,32,256]{2,1,0:T(8,128)(2,1)S(1)} %get-tuple-element.68.refs_2_), channel_id=1, source_target_pairs={{0,3},{1,0},{2,1},{3,2},{4,7},{5,4},{6,5},{7,6},{8,11},{9,8},{10,9... | collective-permute-start | bytes 786440 | tf_op jit(solution)/shard_map/ppermute | solution.py:28
  140.7 9.5 %collective-permute-start.19 = (bf16[16,32,256]{2,1,0:T(8,128)(2,1)S(1)}, bf16[16,32,256]{2,1,0:T(8,128)(2,1)S(1)}, u32[]{:S(2)}, u32[]{:S(2)}) collective-permute-start(bf16[16,32,256]{2,1,0:T(8,128)(2,1)S(1)} %collective-permute-done.18.refs_8_), channel_id=1, source_target_pairs={{0,3},{1,0},{2,1},{3,2},{4,7},{5,4},{6,5},{7,6},{8,11},{9,8},{10,9... | collective-permute-start | bytes 786440 | tf_op jit(solution)/shard_map/ppermute | solution.py:28
  (13 other events, 114.9 us)

commit v7 on v6

--- a/solution.py
+++ b/solution.py
@@ -71,7 +71,7 @@
             pltpu.SemaphoreType.DMA((parts,)),
             pltpu.SemaphoreType.DMA((parts,)),
         ],
-        compiler_params=params(0),
+        compiler_params=params(0, 50),
         cost_estimate=cost(0, 8 * count * rows * order),
         name="pick",
     )(by_owner)
@@ -438,10 +438,11 @@
     pieces = gather_first(first)
     pieces, stat_left, stat_right = in_order(pieces, stat_left, stat_right)
     stats = update_stats(0, infos[0], blocks[0], stat_left, stat_right, None)
-    second, stats = in_order(second, stats)
-    stats = update_stats(1, infos[1], blocks[1], stat_left, stat_right, stats)
     gathered = gather_second(pieces)
     pieces_next = gather_halves(second[:half, :shard_rows], second[half:, :shard_rows])
+    passed_on, stats = in_order((pieces_next[1], pieces_next[6]), stats)
+    pieces_next[1], pieces_next[6] = passed_on
+    stats = update_stats(1, infos[1], blocks[1], stat_left, stat_right, stats)
     sums = second[:, shard_rows : shard_rows + 6, :].astype(F32)
     sums = sums.reshape(dp_count, 2, 3, local_total, width // local_total)[..., 0]
     sums = jnp.sum(sums, axis=2) / SUM_SCALE

time: 154 us -> 154 us (level)
  waiting for transfers between devices: 41.6 us -> 39 us
  local copies, waits for them, and re-layouts: 6.65 us -> 8.39 us
  starting transfers between devices: 53.8 us -> 52.2 us
    ppermute x22, waiting for transfers between devices: 30.8 us -> 21.7 us  [shift(): lax.ppermute(x, 'replica', [(i, (i + step) % count) for i in range(count)])]
    all_to_all x3, waiting for transfers between devices: 10.8 us -> 17.2 us  [over_dp(): return lax.all_to_all(x, 'dp', split_axis=0, concat_axis=0, tiled=True)]
    ppermute x22, starting transfers between devices: 39.5 us -> 37.8 us  [shift(): lax.ppermute(x, 'replica', [(i, (i + step) % count) for i in range(count)])]
  transfers between devices with their start and end apart: 25 -> 25, of which waited for: 15 -> 8; matrix products, arithmetic and copies ran while one was open for 9% -> 10% of each run, Pallas kernels for 12% -> 12%
where the time goes in v7:
time: 154 us; the launch traced here: 153 us
  starting transfers between devices  52.2 us (34%)
  waiting for transfers between devices  39 us (25%)
  Pallas kernels  21.3 us (14%)
  blocking collectives  20 us (13%)
  other arithmetic  9.52 us (6%)
  local copies, waits for them, and re-layouts  8.39 us (5%)
  between operations  2.53 us (2%)
    ppermute x22, starting transfers between devices, shift(): lax.ppermute(x, 'replica', [(i, (i + step) % count) for i in range(count)])  37.8 us
    ppermute x22, waiting for transfers between devices, shift(): lax.ppermute(x, 'replica', [(i, (i + step) % count) for i in range(count)])  21.7 us
    all_to_all x1, blocking collectives, over_dp(): return lax.all_to_all(x, 'dp', split_axis=0, concat_axis=0, tiled=True)  20 us
    all_to_all x3, waiting for transfers between devices, over_dp(): return lax.all_to_all(x, 'dp', split_axis=0, concat_axis=0, tiled=True)  17.2 us
    all_to_all x3, starting transfers between devices, over_dp(): return lax.all_to_all(x, 'dp', split_axis=0, concat_axis=0, tiled=True)  14.4 us
    pallas_call x2, Pallas kernels, update_stats(): pl.pallas_call(lambda *refs: stats_kernel(len(pieces), *refs), out_shape=...  11 us
    pallas_call x2, Pallas kernels, scale_rows(): pl.pallas_call(lambda *refs: scale_kernel(which, slots, len(pieces), *ref...  4.55 us
    pallas_call x2, Pallas kernels, apply_roots(): pl.pallas_call(lambda *refs: roots_kernel(len(pieces), before is not None...  3.45 us
  transfers between devices with their start and end apart: 25, of which 8 were waited for; matrix products, arithmetic and copies ran while one was open for 10% of the time, Pallas kernels for 12%

profile of v7, /device:TPU:0, one launch (start us, length us, event | category | flops | bytes accessed | tf_op | source)
XLA Modules:
  0.0 153.0 jit_solution(16119921734260276256)
XLA Ops:
  1.7 20.0 %all_to_all.20.refs_3_.refs_1_ = bf16[32,32,256]{2,1,0:T(8,128)(2,1)S(1)} all-to-all(bf16[32,32,256]{2,1,0:T(8,128)(2,1)S(1)} %dynamic-slice_bitcast_fusion), channel_id=1, replica_groups=mesh['dp'=32,'replica'=4] {'dp'}, dimensions={0} | all-to-all | bytes 1048576 | tf_op jit(solution)/shard_map/all_to_all | solution.py:32
  25.0 2.4 %pick.1 = bf16[32,32,1024]{2,1,0:T(8,128)(2,1)} custom-call(bf16[32,2,32,1024]{3,2,1,0:T(8,128)(2,1)} %bitcast.21), custom_call_target="tpu_custom_call" | custom-call | bytes 8388608 | tf_op jit(solution)/shard_map/pick/pallas_call | solution.py:64
  27.4 4.8 %all-to-all-start = ((bf16[32,32,1024]{2,1,0:T(8,128)(2,1)}), bf16[32,32,1024]{2,1,0:T(8,128)(2,1)}, u32[]{:S(2)}, u32[]{:S(2)}) async-start(bf16[32,32,1024]{2,1,0:T(8,128)(2,1)} %pick.1), calls=%async_computation | async-start | bytes 4194304 | tf_op jit(solution)/shard_map/all_to_all | solution.py:32
  32.2 4.6 %collective-permute-done.refs_4_.refs_2_ = bf16[32,32,256]{2,1,0:T(8,128)(2,1)S(1)} collective-permute-done((bf16[32,32,256]{2,1,0:T(8,128)(2,1)S(1)}, bf16[32,32,256]{2,1,0:T(8,128)(2,1)S(1)}, u32[]{:S(2)}, u32[]{:S(2)}) %collective-permute-start) | collective-permute-done | bytes 524320 | tf_op jit(solution)/shard_map/ppermute | solution.py:28
  37.2 3.0 %collective-permute-start.3 = (bf16[16,32,256]{2,1,0:T(8,128)(2,1)S(1)}, bf16[16,32,256]{2,1,0:T(8,128)(2,1)S(1)}, u32[]{:S(2)}, u32[]{:S(2)}) collective-permute-start(bf16[16,32,256]{2,1,0:T(8,128)(2,1)S(1)} %slice.126), channel_id=1, source_target_pairs={{0,3},{1,0},{2,1},{3,2},{4,7},{5,4},{6,5},{7,6},{8,11},{9,8},{10,9... | collective-permute-start | bytes 786440 | tf_op jit(solution)/shard_map/ppermute | solution.py:28
  47.8 2.8 %collective-permute-start.5 = (bf16[32,32,256]{2,1,0:T(8,128)(2,1)}, bf16[32,32,256]{2,1,0:T(8,128)(2,1)S(1)}, u32[]{:S(2)}, u32[]{:S(2)}) collective-permute-start(bf16[32,32,256]{2,1,0:T(8,128)(2,1)} %get-tuple-element.41), channel_id=1, source_target_pairs={{0,3},{1,0},{2,1},{3,2},{4,7},{5,4},{6,5},{7,6},{8,11},{9,8},{10,9... | collective-permute-start | bytes 1572872 | tf_op jit(solution)/shard_map/ppermute | solution.py:28
  50.6 11.5 %all-to-all-done.refs_3_.refs_1_ = bf16[32,32,1024]{2,1,0:T(8,128)(2,1)} async-done(((bf16[32,32,1024]{2,1,0:T(8,128)(2,1)}), bf16[32,32,1024]{2,1,0:T(8,128)(2,1)}, u32[]{:S(2)}, u32[]{:S(2)}) %all-to-all-start) | async-done | bytes 2097184 | tf_op jit(solution)/shard_map/all_to_all | solution.py:32
  64.7 5.1 %collective-permute-start.13 = (bf16[16,32,256]{2,1,0:T(8,128)(2,1)}, bf16[16,32,256]{2,1,0:T(8,128)(2,1)S(1)}, u32[]{:S(2)}, u32[]{:S(2)}) collective-permute-start(bf16[16,32,256]{2,1,0:T(8,128)(2,1)} %slice_select_fusion.2), channel_id=1, source_target_pairs={{0,3},{1,0},{2,1},{3,2},{4,7},{5,4},{6,5},{7,6},{8,11},{9,8},{10,9... | collective-permute-start | bytes 786440 | tf_op jit(solution)/shard_map/ppermute | solution.py:28
  70.5 4.1 %collective-permute-start.6 = (bf16[33,32,256]{2,1,0:T(8,128)(2,1)}, bf16[33,32,256]{2,1,0:T(8,128)(2,1)S(1)}, u32[]{:S(2)}, u32[]{:S(2)}) collective-permute-start(bf16[33,32,256]{2,1,0:T(8,128)(2,1)} %get-tuple-element.43), channel_id=1, source_target_pairs={{0,3},{1,0},{2,1},{3,2},{4,7},{5,4},{6,5},{7,6},{8,11},{9,8},{10,9... | collective-permute-start | bytes 1622024 | tf_op jit(solution)/shard_map/ppermute | solution.py:28
  76.8 5.3 %collective-permute-done.12 = bf16[16,32,256]{2,1,0:T(8,128)(2,1)} collective-permute-done((bf16[16,32,256]{2,1,0:T(8,128)(2,1)}, bf16[16,32,256]{2,1,0:T(8,128)(2,1)}, u32[]{:S(2)}, u32[]{:S(2)}) %collective-permute-start.12) | collective-permute-done | bytes 262176 | tf_op jit(solution)/shard_map/ppermute | solution.py:28
  84.1 5.8 %all-to-all-start.3 = ((bf16[32,32,256]{2,1,0:T(8,128)(2,1)}), bf16[32,32,256]{2,1,0:T(8,128)(2,1)S(1)}, u32[]{:S(2)}, u32[]{:S(2)}) async-start(bf16[32,32,256]{2,1,0:T(8,128)(2,1)} %pad_maximum_fusion.1), calls=%async_computation.3 | async-start | bytes 1048576 | tf_op jit(solution)/shard_map/all_to_all | solution.py:32
  92.5 3.2 %collective-permute-start.9 = (bf16[17,32,256]{2,1,0:T(8,128)(2,1)S(1)}, bf16[17,32,256]{2,1,0:T(8,128)(2,1)}, u32[]{:S(2)}, u32[]{:S(2)}) collective-permute-start(bf16[17,32,256]{2,1,0:T(8,128)(2,1)S(1)} %get-tuple-element.77), channel_id=1, source_target_pairs={{0,3},{1,0},{2,1},{3,2},{4,7},{5,4},{6,5},{7,6},{8,11},{9,8},{10,9... | collective-permute-start | bytes 835592 | tf_op jit(solution)/shard_map/ppermute | solution.py:28
  95.9 5.7 %all-to-all-done.3.refs_2_ = bf16[32,32,256]{2,1,0:T(8,128)(2,1)S(1)} async-done(((bf16[32,32,256]{2,1,0:T(8,128)(2,1)}), bf16[32,32,256]{2,1,0:T(8,128)(2,1)S(1)}, u32[]{:S(2)}, u32[]{:S(2)}) %all-to-all-start.3) | async-done | bytes 524320 | tf_op jit(solution)/shard_map/all_to_all | solution.py:32
  101.6 3.2 %collective-permute-start.15 = (bf16[32,32,256]{2,1,0:T(8,128)(2,1)S(1)}, bf16[32,32,256]{2,1,0:T(8,128)(2,1)S(1)}, u32[]{:S(2)}, u32[]{:S(2)}) collective-permute-start(bf16[32,32,256]{2,1,0:T(8,128)(2,1)S(1)} %all-to-all-done.3.refs_2_), channel_id=1, source_target_pairs={{0,3},{1,0},{2,1},{3,2},{4,7},{5,4},{6,5},{7,6},{8,11},{9,8},{10,9... | collective-permute-start | bytes 1572872 | tf_op jit(solution)/shard_map/ppermute | solution.py:28
  107.7 3.9 %all-to-all-start.2 = ((bf16[32,48,256]{2,1,0:T(8,128)(2,1)}), bf16[32,48,256]{2,1,0:T(8,128)(2,1)S(1)}, u32[]{:S(2)}, u32[]{:S(2)}) async-start(bf16[32,48,256]{2,1,0:T(8,128)(2,1)} %pad_maximum_fusion), calls=%async_computation.2 | async-start | bytes 1572864 | tf_op jit(solution)/shard_map/all_to_all | solution.py:32
  111.6 5.1 %collective-permute-done.14.refs_3_ = bf16[32,32,256]{2,1,0:T(8,128)(2,1)S(1)} collective-permute-done((bf16[32,32,256]{2,1,0:T(8,128)(2,1)S(1)}, bf16[32,32,256]{2,1,0:T(8,128)(2,1)S(1)}, u32[]{:S(2)}, u32[]{:S(2)}) %collective-permute-start.14) | collective-permute-done | bytes 524320 | tf_op jit(solution)/shard_map/ppermute | solution.py:28
  118.2 3.2 %collective-permute-start.21 = (bf16[16,32,256]{2,1,0:T(8,128)(2,1)}, bf16[16,32,256]{2,1,0:T(8,128)(2,1)S(1)}, u32[]{:S(2)}, u32[]{:S(2)}) collective-permute-start(bf16[16,32,256]{2,1,0:T(8,128)(2,1)} %slice.123), channel_id=1, source_target_pairs={{0,3},{1,0},{2,1},{3,2},{4,7},{5,4},{6,5},{7,6},{8,11},{9,8},{10,9... | collective-permute-start | bytes 786440 | tf_op jit(solution)/shard_map/ppermute | solution.py:28
  121.4 5.4 %stats.2 = (f32[2,256,1024]{2,1,0:T(8,128)}, f32[2,256,1024]{2,1,0:T(8,128)}) custom-call(s32[4]{0:T(128)} %copy-done.3, bf16[32,32,256]{2,1,0:T(8,128)(2,1)} %copy-done, bf16[32,32,256]{2,1,0:T(8,128)(2,1)} %copy-done.1, bf16[32,32,256]{2,1,0:T(8,128)(2,1)} %copy-done.8, bf16[16,32,256]{2,1,0:T(8,128)(2,1)} %copy-done.4, bf16[16,32,256]{2,1,0:T(8,128)(2,1)} %copy-done.5, ...), custom_call_target="tpu_custom_call" | custom-call | flops 6442450944 | bytes 6291456 | tf_op jit(solution)/shard_map/stats/pallas_call | solution.py:261
  127.7 3.2 %collective-permute-start.16 = (bf16[16,32,256]{2,1,0:T(8,128)(2,1)S(1)}, bf16[16,32,256]{2,1,0:T(8,128)(2,1)S(1)}, u32[]{:S(2)}, u32[]{:S(2)}) collective-permute-start(bf16[16,32,256]{2,1,0:T(8,128)(2,1)S(1)} %get-tuple-element.70.refs_2_), channel_id=1, source_target_pairs={{0,3},{1,0},{2,1},{3,2},{4,7},{5,4},{6,5},{7,6},{8,11},{9,8},{10,9... | collective-permute-start | bytes 786440 | tf_op jit(solution)/shard_map/ppermute | solution.py:28
  136.3 2.3 %scale.2.refs_10_ = bf16[32,2,32,1024]{3,2,1,0:T(8,128)(2,1)} custom-call(f32[64]{0:T(128)S(1)} %select_reduce_fusion.refs_0_, s32[1]{0:T(128)} %bitcast.2.refs_1_, bf16[32,32,256]{2,1,0:T(8,128)(2,1)S(1)} %all-to-all-done.3.refs_2_, bf16[32,32,256]{2,1,0:T(8,128)(2,1)S(1)} %collective-permute-done.14.refs_3_, ...), custom_call_target="tpu_custom_call" | custom-call | bytes 12582912 | tf_op jit(solution)/shard_map/scale/pallas_call | solution.py:314
  138.6 2.7 %collective-permute-done.11.refs_8_ = bf16[16,32,256]{2,1,0:T(8,128)(2,1)S(1)} collective-permute-done((bf16[16,32,256]{2,1,0:T(8,128)(2,1)S(1)}, bf16[16,32,256]{2,1,0:T(8,128)(2,1)S(1)}, u32[]{:S(2)}, u32[]{:S(2)}) %collective-permute-start.11) | collective-permute-done | bytes 262176 | tf_op jit(solution)/shard_map/ppermute | solution.py:28
  141.9 3.1 %collective-permute-start.19 = (bf16[16,32,256]{2,1,0:T(8,128)(2,1)S(1)}, bf16[16,32,256]{2,1,0:T(8,128)(2,1)S(1)}, u32[]{:S(2)}, u32[]{:S(2)}) collective-permute-start(bf16[16,32,256]{2,1,0:T(8,128)(2,1)S(1)} %collective-permute-done.11.refs_8_), channel_id=1, source_target_pairs={{0,3},{1,0},{2,1},{3,2},{4,7},{5,4},{6,5},{7,6},{8,11},{9,8},{10,9... | collective-permute-start | bytes 786440 | tf_op jit(solution)/shard_map/ppermute | solution.py:28
  145.0 5.5 %stats.3 = (f32[2,256,1024]{2,1,0:T(8,128)}, f32[2,256,1024]{2,1,0:T(8,128)}) custom-call(s32[4]{0:T(128)} %copy-done.2, bf16[32,32,1024]{2,1,0:T(8,128)(2,1)} %all-to-all-done.refs_3_.refs_1_, f32[2,256,1024]{2,1,0:T(8,128)} %refs_2_, f32[2,256,1024]{2,1,0:T(8,128)} %refs_3_, ...), custom_call_target="tpu_custom_call", output_to_operand_aliasing={{0}: (4, {}), {1}: (5, {})} | custom-call | flops 6442450944 | bytes 6291456 | tf_op jit(solution)/shard_map/stats/pallas_call | solution.py:261
  150.5 2.3 %scale.3 = bf16[32,2,32,1024]{3,2,1,0:T(8,128)(2,1)} custom-call(f32[64]{0:T(128)S(1)} %select_reduce_fusion.refs_0_, s32[1]{0:T(128)} %bitcast.2.refs_1_, bf16[16,32,256]{2,1,0:T(8,128)(2,1)S(1)} %get-tuple-element.70.refs_2_, bf16[16,32,256]{2,1,0:T(8,128)(2,1)S(1)} %collective-permute-done.10.refs_3_, ...), custom_call_target="tpu_custom_call", output_to_operand_aliasing={{}: (10, {})} | custom-call | bytes 12582912 | tf_op jit(solution)/shard_map/scale/pallas_call | solution.py:314
  (98 shorter events, 32.2 us)
Async XLA Ops:
  21.7 15.1 %collective-permute-start = (bf16[32,32,256]{2,1,0:T(8,128)(2,1)S(1)}, bf16[32,32,256]{2,1,0:T(8,128)(2,1)S(1)}, u32[]{:S(2)}, u32[]{:S(2)}) collective-permute-start(bf16[32,32,256]{2,1,0:T(8,128)(2,1)S(1)} %all_to_all.20.refs_3_.refs_1_), channel_id=1, source_target_pairs={{0,1},{1,2},{2,3},{3,0},{4,5},{5,6},{6,7},{7,4},{8,9},{9,10},{10,1... | collective-permute-start | bytes 1572872 | tf_op jit(solution)/shard_map/ppermute | solution.py:28
  23.2 14.0 %collective-permute-start.1 = (bf16[32,32,256]{2,1,0:T(8,128)(2,1)S(1)}, bf16[32,32,256]{2,1,0:T(8,128)(2,1)S(1)}, u32[]{:S(2)}, u32[]{:S(2)}) collective-permute-start(bf16[32,32,256]{2,1,0:T(8,128)(2,1)S(1)} %all_to_all.20.refs_3_.refs_1_), channel_id=1, source_target_pairs={{0,3},{1,0},{2,1},{3,2},{4,7},{5,4},{6,5},{7,6},{8,11},{9,8},{10,9... | collective-permute-start | bytes 1572872 | tf_op jit(solution)/shard_map/ppermute | solution.py:28
  27.4 34.7 %all-to-all-start = ((bf16[32,32,1024]{2,1,0:T(8,128)(2,1)}), bf16[32,32,1024]{2,1,0:T(8,128)(2,1)}, u32[]{:S(2)}, u32[]{:S(2)}) async-start(bf16[32,32,1024]{2,1,0:T(8,128)(2,1)} %pick.1), calls=%async_computation | async-start | bytes 4194304 | tf_op jit(solution)/shard_map/all_to_all | solution.py:32
  36.8 8.7 %collective-permute-start.2 = (bf16[16,32,256]{2,1,0:T(8,128)(2,1)S(1)}, bf16[16,32,256]{2,1,0:T(8,128)(2,1)S(1)}, u32[]{:S(2)}, u32[]{:S(2)}) collective-permute-start(bf16[16,32,256]{2,1,0:T(8,128)(2,1)S(1)} %slice.125), channel_id=1, source_target_pairs={{0,1},{1,2},{2,3},{3,0},{4,5},{5,6},{6,7},{7,4},{8,9},{9,10},{10,1... | collective-permute-start | bytes 786440 | tf_op jit(solution)/shard_map/ppermute | solution.py:28
  47.3 16.6 %collective-permute-start.4 = (bf16[32,32,256]{2,1,0:T(8,128)(2,1)}, bf16[32,32,256]{2,1,0:T(8,128)(2,1)S(1)}, u32[]{:S(2)}, u32[]{:S(2)}) collective-permute-start(bf16[32,32,256]{2,1,0:T(8,128)(2,1)} %get-tuple-element.40), channel_id=1, source_target_pairs={{0,1},{1,2},{2,3},{3,0},{4,5},{5,6},{6,7},{7,4},{8,9},{9,10},{10,1... | collective-permute-start | bytes 1572872 | tf_op jit(solution)/shard_map/ppermute | solution.py:28
  47.8 16.1 %collective-permute-start.5 = (bf16[32,32,256]{2,1,0:T(8,128)(2,1)}, bf16[32,32,256]{2,1,0:T(8,128)(2,1)S(1)}, u32[]{:S(2)}, u32[]{:S(2)}) collective-permute-start(bf16[32,32,256]{2,1,0:T(8,128)(2,1)} %get-tuple-element.41), channel_id=1, source_target_pairs={{0,3},{1,0},{2,1},{3,2},{4,7},{5,4},{6,5},{7,6},{8,11},{9,8},{10,9... | collective-permute-start | bytes 1572872 | tf_op jit(solution)/shard_map/ppermute | solution.py:28
  64.7 12.1 %collective-permute-start.13 = (bf16[16,32,256]{2,1,0:T(8,128)(2,1)}, bf16[16,32,256]{2,1,0:T(8,128)(2,1)S(1)}, u32[]{:S(2)}, u32[]{:S(2)}) collective-permute-start(bf16[16,32,256]{2,1,0:T(8,128)(2,1)} %slice_select_fusion.2), channel_id=1, source_target_pairs={{0,3},{1,0},{2,1},{3,2},{4,7},{5,4},{6,5},{7,6},{8,11},{9,8},{10,9... | collective-permute-start | bytes 786440 | tf_op jit(solution)/shard_map/ppermute | solution.py:28
  70.5 11.6 %collective-permute-start.12 = (bf16[16,32,256]{2,1,0:T(8,128)(2,1)}, bf16[16,32,256]{2,1,0:T(8,128)(2,1)}, u32[]{:S(2)}, u32[]{:S(2)}) collective-permute-start(bf16[16,32,256]{2,1,0:T(8,128)(2,1)} %slice_select_fusion.3), channel_id=1, source_target_pairs={{0,1},{1,2},{2,3},{3,0},{4,5},{5,6},{6,7},{7,4},{8,9},{9,10},{10,1... | collective-permute-start | bytes 786440 | tf_op jit(solution)/shard_map/ppermute | solution.py:28
  70.5 19.3 %collective-permute-start.6 = (bf16[33,32,256]{2,1,0:T(8,128)(2,1)}, bf16[33,32,256]{2,1,0:T(8,128)(2,1)S(1)}, u32[]{:S(2)}, u32[]{:S(2)}) collective-permute-start(bf16[33,32,256]{2,1,0:T(8,128)(2,1)} %get-tuple-element.43), channel_id=1, source_target_pairs={{0,3},{1,0},{2,1},{3,2},{4,7},{5,4},{6,5},{7,6},{8,11},{9,8},{10,9... | collective-permute-start | bytes 1622024 | tf_op jit(solution)/shard_map/ppermute | solution.py:28
  74.6 17.0 %collective-permute-start.7 = (bf16[33,32,256]{2,1,0:T(8,128)(2,1)}, bf16[33,32,256]{2,1,0:T(8,128)(2,1)S(1)}, u32[]{:S(2)}, u32[]{:S(2)}) collective-permute-start(bf16[33,32,256]{2,1,0:T(8,128)(2,1)} %get-tuple-element.45), channel_id=1, source_target_pairs={{0,1},{1,2},{2,3},{3,0},{4,5},{5,6},{6,7},{7,4},{8,9},{9,10},{10,1... | collective-permute-start | bytes 1622024 | tf_op jit(solution)/shard_map/ppermute | solution.py:28
  84.1 17.5 %all-to-all-start.3 = ((bf16[32,32,256]{2,1,0:T(8,128)(2,1)}), bf16[32,32,256]{2,1,0:T(8,128)(2,1)S(1)}, u32[]{:S(2)}, u32[]{:S(2)}) async-start(bf16[32,32,256]{2,1,0:T(8,128)(2,1)} %pad_maximum_fusion.1), calls=%async_computation.3 | async-start | bytes 1048576 | tf_op jit(solution)/shard_map/all_to_all | solution.py:32
  92.5 12.4 %collective-permute-start.8 = (bf16[17,32,256]{2,1,0:T(8,128)(2,1)}, bf16[17,32,256]{2,1,0:T(8,128)(2,1)}, u32[]{:S(2)}, u32[]{:S(2)}) collective-permute-start(bf16[17,32,256]{2,1,0:T(8,128)(2,1)} %get-tuple-element.78), channel_id=1, source_target_pairs={{0,1},{1,2},{2,3},{3,0},{4,5},{5,6},{6,7},{7,4},{8,9},{9,10},{10,1... | collective-permute-start | bytes 835592 | tf_op jit(solution)/shard_map/ppermute | solution.py:28
  92.5 13.1 %collective-permute-start.9 = (bf16[17,32,256]{2,1,0:T(8,128)(2,1)S(1)}, bf16[17,32,256]{2,1,0:T(8,128)(2,1)}, u32[]{:S(2)}, u32[]{:S(2)}) collective-permute-start(bf16[17,32,256]{2,1,0:T(8,128)(2,1)S(1)} %get-tuple-element.77), channel_id=1, source_target_pairs={{0,3},{1,0},{2,1},{3,2},{4,7},{5,4},{6,5},{7,6},{8,11},{9,8},{10,9... | collective-permute-start | bytes 835592 | tf_op jit(solution)/shard_map/ppermute | solution.py:28
  101.6 15.1 %collective-permute-start.14 = (bf16[32,32,256]{2,1,0:T(8,128)(2,1)S(1)}, bf16[32,32,256]{2,1,0:T(8,128)(2,1)S(1)}, u32[]{:S(2)}, u32[]{:S(2)}) collective-permute-start(bf16[32,32,256]{2,1,0:T(8,128)(2,1)S(1)} %all-to-all-done.3.refs_2_), channel_id=1, source_target_pairs={{0,1},{1,2},{2,3},{3,0},{4,5},{5,6},{6,7},{7,4},{8,9},{9,10},{10,1... | collective-permute-start | bytes 1572872 | tf_op jit(solution)/shard_map/ppermute | solution.py:28
  101.6 15.1 %collective-permute-start.15 = (bf16[32,32,256]{2,1,0:T(8,128)(2,1)S(1)}, bf16[32,32,256]{2,1,0:T(8,128)(2,1)S(1)}, u32[]{:S(2)}, u32[]{:S(2)}) collective-permute-start(bf16[32,32,256]{2,1,0:T(8,128)(2,1)S(1)} %all-to-all-done.3.refs_2_), channel_id=1, source_target_pairs={{0,3},{1,0},{2,1},{3,2},{4,7},{5,4},{6,5},{7,6},{8,11},{9,8},{10,9... | collective-permute-start | bytes 1572872 | tf_op jit(solution)/shard_map/ppermute | solution.py:28
  107.7 19.2 %all-to-all-start.2 = ((bf16[32,48,256]{2,1,0:T(8,128)(2,1)}), bf16[32,48,256]{2,1,0:T(8,128)(2,1)S(1)}, u32[]{:S(2)}, u32[]{:S(2)}) async-start(bf16[32,48,256]{2,1,0:T(8,128)(2,1)} %pad_maximum_fusion), calls=%async_computation.2 | async-start | bytes 1572864 | tf_op jit(solution)/shard_map/all_to_all | solution.py:32
  117.4 17.2 %collective-permute-start.20 = (bf16[16,32,256]{2,1,0:T(8,128)(2,1)}, bf16[16,32,256]{2,1,0:T(8,128)(2,1)S(1)}, u32[]{:S(2)}, u32[]{:S(2)}) collective-permute-start(bf16[16,32,256]{2,1,0:T(8,128)(2,1)} %slice.122), channel_id=1, source_target_pairs={{0,1},{1,2},{2,3},{3,0},{4,5},{5,6},{6,7},{7,4},{8,9},{9,10},{10,1... | collective-permute-start | bytes 786440 | tf_op jit(solution)/shard_map/ppermute | solution.py:28
  118.2 18.1 %collective-permute-start.21 = (bf16[16,32,256]{2,1,0:T(8,128)(2,1)}, bf16[16,32,256]{2,1,0:T(8,128)(2,1)S(1)}, u32[]{:S(2)}, u32[]{:S(2)}) collective-permute-start(bf16[16,32,256]{2,1,0:T(8,128)(2,1)} %slice.123), channel_id=1, source_target_pairs={{0,3},{1,0},{2,1},{3,2},{4,7},{5,4},{6,5},{7,6},{8,11},{9,8},{10,9... | collective-permute-start | bytes 786440 | tf_op jit(solution)/shard_map/ppermute | solution.py:28
  127.7 10.8 %collective-permute-start.10 = (bf16[16,32,256]{2,1,0:T(8,128)(2,1)S(1)}, bf16[16,32,256]{2,1,0:T(8,128)(2,1)S(1)}, u32[]{:S(2)}, u32[]{:S(2)}) collective-permute-start(bf16[16,32,256]{2,1,0:T(8,128)(2,1)S(1)} %get-tuple-element.70.refs_2_), channel_id=1, source_target_pairs={{0,1},{1,2},{2,3},{3,0},{4,5},{5,6},{6,7},{7,4},{8,9},{9,10},{10,1... | collective-permute-start | bytes 786440 | tf_op jit(solution)/shard_map/ppermute | solution.py:28
  127.7 22.8 %collective-permute-start.16 = (bf16[16,32,256]{2,1,0:T(8,128)(2,1)S(1)}, bf16[16,32,256]{2,1,0:T(8,128)(2,1)S(1)}, u32[]{:S(2)}, u32[]{:S(2)}) collective-permute-start(bf16[16,32,256]{2,1,0:T(8,128)(2,1)S(1)} %get-tuple-element.70.refs_2_), channel_id=1, source_target_pairs={{0,3},{1,0},{2,1},{3,2},{4,7},{5,4},{6,5},{7,6},{8,11},{9,8},{10,9... | collective-permute-start | bytes 786440 | tf_op jit(solution)/shard_map/ppermute | solution.py:28
  131.0 10.3 %collective-permute-start.11 = (bf16[16,32,256]{2,1,0:T(8,128)(2,1)S(1)}, bf16[16,32,256]{2,1,0:T(8,128)(2,1)S(1)}, u32[]{:S(2)}, u32[]{:S(2)}) collective-permute-start(bf16[16,32,256]{2,1,0:T(8,128)(2,1)S(1)} %get-tuple-element.69.refs_6_), channel_id=1, source_target_pairs={{0,3},{1,0},{2,1},{3,2},{4,7},{5,4},{6,5},{7,6},{8,11},{9,8},{10,9... | collective-permute-start | bytes 786440 | tf_op jit(solution)/shard_map/ppermute | solution.py:28
  134.7 15.8 %collective-permute-start.18 = (bf16[16,32,256]{2,1,0:T(8,128)(2,1)S(1)}, bf16[16,32,256]{2,1,0:T(8,128)(2,1)S(1)}, u32[]{:S(2)}, u32[]{:S(2)}) collective-permute-start(bf16[16,32,256]{2,1,0:T(8,128)(2,1)S(1)} %get-tuple-element.69.refs_6_), channel_id=1, source_target_pairs={{0,1},{1,2},{2,3},{3,0},{4,5},{5,6},{6,7},{7,4},{8,9},{9,10},{10,1... | collective-permute-start | bytes 786440 | tf_op jit(solution)/shard_map/ppermute | solution.py:28
  141.3 9.2 %collective-permute-start.17 = (bf16[16,32,256]{2,1,0:T(8,128)(2,1)S(1)}, bf16[16,32,256]{2,1,0:T(8,128)(2,1)S(1)}, u32[]{:S(2)}, u32[]{:S(2)}) collective-permute-start(bf16[16,32,256]{2,1,0:T(8,128)(2,1)S(1)} %collective-permute-done.10.refs_3_), channel_id=1, source_target_pairs={{0,1},{1,2},{2,3},{3,0},{4,5},{5,6},{6,7},{7,4},{8,9},{9,10},{10,1... | collective-permute-start | bytes 786440 | tf_op jit(solution)/shard_map/ppermute | solution.py:28
  141.9 8.7 %collective-permute-start.19 = (bf16[16,32,256]{2,1,0:T(8,128)(2,1)S(1)}, bf16[16,32,256]{2,1,0:T(8,128)(2,1)S(1)}, u32[]{:S(2)}, u32[]{:S(2)}) collective-permute-start(bf16[16,32,256]{2,1,0:T(8,128)(2,1)S(1)} %collective-permute-done.11.refs_8_), channel_id=1, source_target_pairs={{0,3},{1,0},{2,1},{3,2},{4,7},{5,4},{6,5},{7,6},{8,11},{9,8},{10,9... | collective-permute-start | bytes 786440 | tf_op jit(solution)/shard_map/ppermute | solution.py:28
  (13 other events, 95.6 us)
